TPU v7x, 32 devices: a whole 2x2x4 slice. The times are simulated.
32 devices in a mesh: depth: 4 (over x, core), tile: 8 (over z, y).
Axes of the slice: x: 2, y: 2, z: 4, core: 2. Of those that a mesh axis runs over, the one named last changes fastest.
Arguments:
- transmission: float32 [8, 2, 2048, 512], P('depth', None, 'tile'), may hold values from -5 to 5
- probe_field: float32 [2, 256, 256], replicated, may hold values from -5 to 5
- scan_positions: int32 [32, 2], P('tile'), may hold values from 0 to 1792, as said below
- amplitudes: float32 [32, 256, 256], P('tile'), may hold values from 0 to 3
Outputs:
- object_grad: float32 [8, 2, 2048, 512], P('depth', None, 'tile')
- probe_grad: float32 [2, 256, 256], P(None, 'depth')
Inputs may be any that keep to these rules, and one draw needn't show every extreme that they name: `scan_positions`: column 0 holds a window's first row and column 1 its first column. The first row of window b lies in strip b // 4, that is between (b // 4) * 256 and (b // 4 + 1) * 256 - 1; windows of the last strip end inside the object, and a window's first column is at most 256.
All inputs are finite; a program needn't handle non-finite values.
Results may differ from a plain program's by a relative error of at most 0.0003.
Values sent between devices are 32-bit elements; how exact they have to be, the bound alone decides.
No kernel may reach another device: no remote copies, remote signals or barrier semaphores. Data moves between devices by JAX's collectives and lax.ppermute only.
A program may use at most 128 MiB of HBM per device.

v0:
```python
import functools

import jax
import jax.numpy as jnp
import ml_dtypes
import numpy as np
from jax import lax
from jax.experimental import pallas as pl
from jax.experimental.pallas import tpu as pltpu
from jax.sharding import PartitionSpec as P

LANES = 128
VMEM_BYTES = 48 * 1024 * 1024
F32 = jnp.float32
BF16 = jnp.bfloat16


def split_table(table):
    high = table.astype(np.float32).astype(ml_dtypes.bfloat16)
    low = (table - high.astype(np.float64)).astype(np.float32).astype(ml_dtypes.bfloat16)
    return high, low


def left_form(matrix):
    return np.block([[matrix.real, -matrix.imag], [matrix.imag, matrix.real]])


def folded(matrix):
    half = matrix.shape[0] // 2
    near = matrix[:half, :half]
    mirrored = matrix[:half, half:][:, ::-1]
    return (near + mirrored) / 2, (near - mirrored) / 2


def optics_tables(length):
    index = np.arange(length)
    fourier = np.exp(-2j * np.pi * (index[:, None] * index[None, :] % length) / length)
    frequency = np.where(index < length // 2, index, index - length).astype(np.float64)
    phase = np.exp(-1j * np.pi * frequency**2 / (4 * length))
    fresnel = (np.conj(fourier) * phase[None, :]) @ fourier / length
    odd = 2 * index + 1
    turn = odd[:, None] * odd[None, :] % (4 * length)
    shifted = np.exp(-2j * np.pi * turn / (4 * length)) / np.sqrt(length)
    left, right = [], []
    for matrix in (fresnel, shifted):
        for block in folded(matrix):
            high, low = split_table(left_form(block))
            left.append(np.concatenate([high, high, low], axis=1))
            high, low = split_table(left_form(np.conj(block)))
            left.append(np.concatenate([high, high, low], axis=1))
            high, low = split_table(left_form(np.conj(block)))
            right.append(np.concatenate([high, high, low], axis=0))
            high, low = split_table(left_form(block))
            right.append(np.concatenate([high, high, low], axis=0))
    order = np.concatenate([index[: length // 2], index[length // 2 :][::-1]])
    ramp = np.exp(1j * np.pi * order / length)
    tilt = ramp[:, None] * ramp[None, :]
    return np.stack(left), np.stack(right), np.stack([tilt.real, tilt.imag]).astype(np.float32)


def reversal(size):
    row = lax.broadcasted_iota(jnp.int32, (size, size), 0)
    col = lax.broadcasted_iota(jnp.int32, (size, size), 1)
    return jnp.where(row + col == size - 1, 1.0, 0.0).astype(F32)


def exact_dot(a, b):
    return jnp.dot(a, b, precision=lax.Precision.HIGHEST, preferred_element_type=F32)


def mirror_halves(x, flip):
    half = x.shape[0] // 2
    x = jnp.concatenate([x[:, :half], exact_dot(x[:, half:], flip)], axis=1)
    return jnp.concatenate([x[:half], exact_dot(flip, x[half:])], axis=0)


def prep_kernel(ids, probe, amplitudes, probe_out, amp_out):
    flip = reversal(probe.shape[-1] // 2)
    for part in range(2):
        probe_out[part] = mirror_halves(probe[part], flip)
    amp_out[...] = mirror_halves(amplitudes[ids[0]], flip)


def crop_kernel(peers, ids, positions, own, rim, *rest):
    outs, ext = rest[:peers], rest[peers]
    planes, rows, cols = own.shape
    blocks = cols // LANES
    size = outs[0].shape[-1]
    flip = reversal(size // 2)
    lane = lax.broadcasted_iota(jnp.int32, (size, LANES), 1)
    ext[blocks] = jnp.zeros((2 * rows, LANES), F32)
    for plane in range(planes):
        for block in range(blocks):
            ext[block, 0:rows, :] = own[plane, :, block * LANES : (block + 1) * LANES]
            ext[block, rows : 2 * rows, :] = rim[plane, :, block * LANES : (block + 1) * LANES]
        for offset in range(peers):
            window = ids[0] ^ offset
            row_first = positions[window, 0] - ids[1] * rows
            col_first = positions[window, 1]
            block_first = col_first >> 7
            within = col_first & (LANES - 1)
            moved = [
                pltpu.roll(ext[block_first + i, pl.ds(row_first, size), :], (LANES - within) & (LANES - 1), 1)
                for i in range(size // LANES + 1)
            ]
            keep = lane < LANES - within
            picked = [jnp.where(keep, moved[i], moved[i + 1]) for i in range(size // LANES)]
            outs[offset][plane] = mirror_halves(jnp.concatenate(picked, axis=1), flip)


def place_kernel(peers, ids, positions, *rest):
    pieces, own, rim, ext = rest[:peers], rest[peers], rest[peers + 1], rest[peers + 2]
    planes, rows, cols = own.shape
    blocks = cols // LANES
    size = pieces[0].shape[-1]
    flip = reversal(size // 2)
    lane = lax.broadcasted_iota(jnp.int32, (size, LANES), 1)
    for plane in range(planes):
        ext[...] = jnp.zeros(ext.shape, F32)
        for offset in range(peers):
            window = ids[0] ^ offset
            row_first = positions[window, 0] - ids[1] * rows
            col_first = positions[window, 1]
            block_first = col_first >> 7
            within = col_first & (LANES - 1)
            plain = mirror_halves(pieces[offset][plane], flip)
            moved = [
                pltpu.roll(plain[:, i * LANES : (i + 1) * LANES], within, 1) for i in range(size // LANES)
            ]
            keep = lane >= within
            zero = jnp.zeros((size, LANES), F32)
            moved = [zero] + moved + [zero]
            for i in range(size // LANES + 1):
                place = (block_first + i, pl.ds(row_first, size))
                ext[place] = ext[place] + jnp.where(keep, moved[i + 1], moved[i])
        for block in range(blocks):
            own[plane, :, block * LANES : (block + 1) * LANES] = ext[block, 0:rows, :]
            rim[plane, :, block * LANES : (block + 1) * LANES] = ext[block, rows : 2 * rows, :]


def split_value(x):
    high = x.astype(BF16)
    low = (x - high.astype(F32)).astype(BF16)
    return high, low


def sandwich(re, im, left, right, base, conj):
    half = re.shape[0] // 2

    def fold(x):
        upper, lower = x[:half], x[half:]
        even, odd = upper + lower, upper - lower
        parts = []
        for y in (even, odd):
            near, far = y[:, :half], y[:, half:]
            parts.append((near + far, near - far))
        return parts

    re_parts, im_parts = fold(re), fold(im)
    middle = []
    for b in range(2):
        field = jnp.concatenate(
            [jnp.concatenate([re_parts[a][b], im_parts[a][b]], axis=1) for a in range(2)], axis=0
        )
        high, low = split_value(field)
        middle.append(
            jnp.dot(
                jnp.concatenate([high, low, high], axis=1),
                right[base + 2 * b + conj],
                preferred_element_type=F32,
            )
        )
    done = []
    for a in range(2):
        rows = slice(a * half, (a + 1) * half)
        field = jnp.concatenate(
            [
                jnp.concatenate([middle[b][rows, :half] for b in range(2)], axis=1),
                jnp.concatenate([middle[b][rows, half:] for b in range(2)], axis=1),
            ],
            axis=0,
        )
        high, low = split_value(field)
        done.append(
            jnp.dot(
                left[base + 2 * a + conj],
                jnp.concatenate([high, low, high], axis=0),
                preferred_element_type=F32,
            )
        )

    def unfold(even, odd):
        rows = jnp.concatenate([even + odd, even - odd], axis=0)
        near, far = rows[:, :half], rows[:, half:]
        return jnp.concatenate([near + far, near - far], axis=1)

    return (
        unfold(done[0][:half], done[1][:half]),
        unfold(done[0][half:], done[1][half:]),
    )


def optics_kernel(peers, per_device, ids, probe, amplitude, left, right, tilt, *rest):
    chunks = 2 * per_device
    crops = rest[: chunks * peers]
    pieces = rest[chunks * peers : 2 * chunks * peers]
    shares = rest[2 * chunks * peers : 2 * chunks * peers + peers]
    trans, history, terms, grad, copied = rest[2 * chunks * peers + peers :]
    layers = peers * per_device
    me = ids[0]
    arrivals = []
    for j in range(per_device):
        for part in range(2):
            for offset in range(peers):
                at = (me ^ offset) * per_device + j
                arrivals.append(
                    pltpu.make_async_copy(
                        crops[(j * 2 + part) * peers + offset].at[0],
                        trans.at[at, part],
                        copied.at[(j * 2 + part) * peers + offset],
                    )
                )
    for copy in arrivals:
        copy.start()
    history[0] = probe[...]
    for copy in arrivals:
        copy.wait()

    def mixed(layer):
        t_re, t_im = trans[layer, 0], trans[layer, 1]
        w_re, w_im = history[layer, 0], history[layer, 1]
        return t_re * w_re - t_im * w_im, t_re * w_im + t_im * w_re

    def forward(layer, carry):
        re, im = mixed(layer)
        re, im = sandwich(re, im, left, right, 0, 0)
        history[layer + 1, 0] = re
        history[layer + 1, 1] = im
        return carry

    lax.fori_loop(0, layers - 1, forward, 0)
    re, im = mixed(layers - 1)
    d_re, d_im = tilt[0], tilt[1]
    re, im = re * d_re - im * d_im, re * d_im + im * d_re
    re, im = sandwich(re, im, left, right, 4, 0)
    factor = 1.0 - amplitude[...] / jnp.sqrt(re * re + im * im + 1.0)
    re, im = sandwich(re * factor, im * factor, left, right, 4, 1)
    back_re, back_im = re * d_re + im * d_im, im * d_re - re * d_im

    def collect(layer, back_re, back_im):
        w_re, w_im = history[layer, 0], history[layer, 1]
        terms[layer, 0] = w_re * back_re + w_im * back_im
        terms[layer, 1] = w_re * back_im - w_im * back_re
        t_re, t_im = trans[layer, 0], trans[layer, 1]
        grad[0] = t_re * back_re + t_im * back_im
        grad[1] = t_re * back_im - t_im * back_re

    collect(layers - 1, back_re, back_im)

    def backward(step, carry):
        back_re, back_im = sandwich(grad[0], grad[1], left, right, 0, 1)
        collect(layers - 2 - step, back_re, back_im)
        return carry

    lax.fori_loop(0, layers - 1, backward, 0)
    departures = []
    for j in range(per_device):
        for part in range(2):
            for offset in range(peers):
                at = (me ^ offset) * per_device + j
                departures.append(
                    pltpu.make_async_copy(
                        terms.at[at, part],
                        pieces[(j * 2 + part) * peers + offset].at[0],
                        copied.at[(j * 2 + part) * peers + offset],
                    )
                )
    for copy in departures:
        copy.start()
    flip = reversal(grad.shape[-1] // 2)
    share_rows = shares[0].shape[1]
    for part in range(2):
        grad[part] = mirror_halves(grad[part], flip)
    for offset in range(peers):
        first = pl.multiple_of((me ^ offset) * share_rows, share_rows)
        shares[offset][...] = grad[:, pl.ds(first, share_rows), :]
    for copy in departures:
        copy.wait()


SMEM_SPEC = pl.BlockSpec(memory_space=pltpu.SMEM)
VMEM_SPEC = pl.BlockSpec(memory_space=pltpu.VMEM)
ANY_SPEC = pl.BlockSpec(memory_space=pl.ANY)


def run_kernel(kernel, name, out_shapes, in_specs, out_specs, scratch, micros):
    return pl.pallas_call(
        kernel,
        name=name,
        out_shape=out_shapes,
        in_specs=in_specs,
        out_specs=out_specs,
        scratch_shapes=scratch,
        compiler_params=pltpu.CompilerParams(vmem_limit_bytes=VMEM_BYTES),
        cost_estimate=pl.CostEstimate(
            flops=int(micros * 1e9), bytes_accessed=int(micros * 1e6), transcendentals=0
        ),
    )


def shape(*dims):
    return jax.ShapeDtypeStruct(dims, F32)


def swap(x, axis, offset):
    peers = lax.axis_size(axis)
    return lax.ppermute(x, axis, [(i, i ^ offset) for i in range(peers)])


def shift(x, axis, by):
    peers = lax.axis_size(axis)
    return lax.ppermute(x, axis, [(i, i + by) for i in range(peers) if 0 <= i + by < peers])


def body(transmission, probe_field, scan_positions, amplitudes):
    size = probe_field.shape[-1]
    per_device, _, rows, cols = transmission.shape
    peers = lax.axis_size("depth")
    tiles = lax.axis_size("tile")
    ids = jnp.stack([lax.axis_index("depth"), lax.axis_index("tile")]).astype(jnp.int32)
    left, right, tilt = (jnp.asarray(x) for x in optics_tables(size))

    probe, amplitude = run_kernel(
        prep_kernel,
        "prep",
        (shape(2, size, size), shape(size, size)),
        [SMEM_SPEC, VMEM_SPEC, VMEM_SPEC],
        [VMEM_SPEC, VMEM_SPEC],
        [],
        2,
    )(ids, probe_field, amplitudes)

    chunks = [(j, part) for j in range(per_device) for part in range(2)]
    strips = {c: transmission[c[0], c[1]][None] for c in chunks}
    rims = {c: shift(strips[c], "tile", -1) for c in chunks}
    crops = {}
    for c in chunks:
        mine = run_kernel(
            functools.partial(crop_kernel, peers),
            "crop",
            (shape(1, size, size),) * peers,
            [SMEM_SPEC, SMEM_SPEC, VMEM_SPEC, VMEM_SPEC],
            [VMEM_SPEC] * peers,
            [pltpu.VMEM((cols // LANES + 1, 2 * rows, LANES), F32)],
            2,
        )(ids, scan_positions, strips[c], rims[c])
        crops[c] = [mine[0]] + [swap(mine[m], "depth", m) for m in range(1, peers)]

    layers = per_device * peers
    result = run_kernel(
        functools.partial(optics_kernel, peers, per_device),
        "optics",
        (shape(1, size, size),) * (len(chunks) * peers) + (shape(2, size // peers, size),) * peers,
        [SMEM_SPEC, VMEM_SPEC, VMEM_SPEC, VMEM_SPEC, VMEM_SPEC, VMEM_SPEC] + [ANY_SPEC] * (len(chunks) * peers),
        [ANY_SPEC] * (len(chunks) * peers) + [VMEM_SPEC] * peers,
        [
            pltpu.VMEM((layers, 2, size, size), F32),
            pltpu.VMEM((layers, 2, size, size), F32),
            pltpu.VMEM((layers, 2, size, size), F32),
            pltpu.VMEM((2, size, size), F32),
            pltpu.SemaphoreType.DMA((len(chunks) * peers,)),
        ],
        20,
    )(ids, probe, amplitude, left, right, tilt, *[x for c in chunks for x in crops[c]])

    own, rim_back = {}, {}
    for c in reversed(chunks):
        at = chunks.index(c) * peers
        mine = result[at : at + peers]
        returned = [mine[0]] + [swap(mine[m], "depth", m) for m in range(1, peers)]
        own[c], outside = run_kernel(
            functools.partial(place_kernel, peers),
            "place",
            (shape(1, rows, cols), shape(1, rows, cols)),
            [SMEM_SPEC, SMEM_SPEC] + [VMEM_SPEC] * peers,
            [VMEM_SPEC, VMEM_SPEC],
            [pltpu.VMEM((cols // LANES + 1, 2 * rows, LANES), F32)],
            2,
        )(ids, scan_positions, *returned)
        rim_back[c] = shift(outside, "tile", 1)

    shares = result[len(chunks) * peers :]
    probe_grad = shares[0]
    for m in range(1, peers):
        probe_grad = probe_grad + swap(shares[m], "depth", m)
    step = 1
    while step < tiles:
        probe_grad = probe_grad + swap(probe_grad, "tile", step)
        step *= 2
    object_grad = jnp.stack(
        [
            jnp.stack([own[(j, part)][0] + rim_back[(j, part)][0] for part in range(2)])
            for j in range(per_device)
        ]
    )
    return (object_grad, probe_grad)


def solution(mesh):
    placed = (P("depth", None, "tile", None), P(), P("tile", None), P("tile", None, None))
    return jax.shard_map(
        body,
        mesh=mesh,
        in_specs=placed,
        out_specs=(P("depth", None, "tile", None), P(None, "depth", None)),
        check_vma=False,
    )
```

profile of v0, /device:TPU:4, one launch (start us, length us, event | category | flops | bytes accessed | tf_op | source)
XLA Modules:
  0.0 213.1 jit_solution(2522065714995373856)
XLA Ops:
  10.2 9.8 %collective-permute-done.12.rim = f32[1,256,512]{2,1,0:T(8,128)} collective-permute-done((f32[1,256,512]{2,1,0:T(8,128)S(1)}, f32[1,256,512]{2,1,0:T(8,128)}, u32[]{:S(2)}, u32[]{:S(2)}) %collective-permute-start.12) | collective-permute-done | bytes 524320 | tf_op jit(solution)/shard_map/ppermute | solution.py:322
  20.0 2.5 %crop.7 = (f32[1,256,256]{2,1,0:T(8,128)S(1)}, f32[1,256,256]{2,1,0:T(8,128)S(1)}, f32[1,256,256]{2,1,0:T(8,128)S(1)}, f32[1,256,256]{2,1,0:T(8,128)S(1)}) custom-call(s32[2]{0:T(128)S(1)} %pad_add_fusion.ids, s32[4,2]{1,0:T(4,128)S(1)} %copy.13.positions, f32[1,256,512]{2,1,0:T(8,128)S(1)} %get-tuple-element.94.own, f32[1,256,512]{2,1,0:T(8,128)} %collective-permute-done.12.rim), custom_call_target="tpu_custom_call" | custom-call | flops 2000000000 | bytes 2000000 | tf_op jit(solution)/shard_map/crop/pallas_call | solution.py:348
  24.8 6.5 %collective-permute-done.4.rim = f32[1,256,512]{2,1,0:T(8,128)} collective-permute-done((f32[1,256,512]{2,1,0:T(8,128)S(1)}, f32[1,256,512]{2,1,0:T(8,128)}, u32[]{:S(2)}, u32[]{:S(2)}) %collective-permute-start.4) | collective-permute-done | bytes 524320 | tf_op jit(solution)/shard_map/ppermute | solution.py:322
  31.3 2.5 %crop.5 = (f32[1,256,256]{2,1,0:T(8,128)S(1)}, f32[1,256,256]{2,1,0:T(8,128)S(1)}, f32[1,256,256]{2,1,0:T(8,128)S(1)}, f32[1,256,256]{2,1,0:T(8,128)S(1)}) custom-call(s32[2]{0:T(128)S(1)} %pad_add_fusion.ids, s32[4,2]{1,0:T(4,128)S(1)} %copy.13.positions, f32[1,256,512]{2,1,0:T(8,128)S(1)} %get-tuple-element.95.own, f32[1,256,512]{2,1,0:T(8,128)} %collective-permute-done.4.rim), custom_call_target="tpu_custom_call" | custom-call | flops 2000000000 | bytes 2000000 | tf_op jit(solution)/shard_map/crop/pallas_call | solution.py:348
  34.5 7.9 %collective-permute-done.rim = f32[1,256,512]{2,1,0:T(8,128)S(1)} collective-permute-done((f32[1,256,512]{2,1,0:T(8,128)S(1)}, f32[1,256,512]{2,1,0:T(8,128)S(1)}, u32[]{:S(2)}, u32[]{:S(2)}) %collective-permute-start) | collective-permute-done | bytes 524320 | tf_op jit(solution)/shard_map/ppermute | solution.py:322
  42.4 2.1 crop.4
  44.5 8.0 %collective-permute-done.8.rim = f32[1,256,512]{2,1,0:T(8,128)S(1)} collective-permute-done((f32[1,256,512]{2,1,0:T(8,128)S(1)}, f32[1,256,512]{2,1,0:T(8,128)S(1)}, u32[]{:S(2)}, u32[]{:S(2)}) %collective-permute-start.8) | collective-permute-done | bytes 524320 | tf_op jit(solution)/shard_map/ppermute | solution.py:322
  54.7 2.1 crop.6
  59.1 2.7 %collective-permute-done.6.rest_6_ = f32[1,256,256]{2,1,0:T(8,128)S(1)} collective-permute-done((f32[1,256,256]{2,1,0:T(8,128)S(1)}, f32[1,256,256]{2,1,0:T(8,128)S(1)}, u32[]{:S(2)}, u32[]{:S(2)}) %collective-permute-start.6) | collective-permute-done | bytes 262176 | tf_op jit(solution)/shard_map/ppermute | solution.py:317
  61.7 4.6 %collective-permute-done.7.rest_7_ = f32[1,256,256]{2,1,0:T(8,128)S(1)} collective-permute-done((f32[1,256,256]{2,1,0:T(8,128)S(1)}, f32[1,256,256]{2,1,0:T(8,128)S(1)}, u32[]{:S(2)}, u32[]{:S(2)}) %collective-permute-start.7) | collective-permute-done | bytes 262176 | tf_op jit(solution)/shard_map/ppermute | solution.py:317
  71.0 2.0 collective-permute-done.2.rest_2_
  73.0 4.6 %collective-permute-done.3.rest_3_ = f32[1,256,256]{2,1,0:T(8,128)S(1)} collective-permute-done((f32[1,256,256]{2,1,0:T(8,128)S(1)}, f32[1,256,256]{2,1,0:T(8,128)S(1)}, u32[]{:S(2)}, u32[]{:S(2)}) %collective-permute-start.3) | collective-permute-done | bytes 262176 | tf_op jit(solution)/shard_map/ppermute | solution.py:317
  77.6 6.6 %collective-permute-done.10.rest_10_ = f32[1,256,256]{2,1,0:T(8,128)S(1)} collective-permute-done((f32[1,256,256]{2,1,0:T(8,128)S(1)}, f32[1,256,256]{2,1,0:T(8,128)S(1)}, u32[]{:S(2)}, u32[]{:S(2)}) %collective-permute-start.10) | collective-permute-done | bytes 262176 | tf_op jit(solution)/shard_map/ppermute | solution.py:317
  84.2 2.6 %collective-permute-done.11.rest_11_ = f32[1,256,256]{2,1,0:T(8,128)S(1)} collective-permute-done((f32[1,256,256]{2,1,0:T(8,128)S(1)}, f32[1,256,256]{2,1,0:T(8,128)S(1)}, u32[]{:S(2)}, u32[]{:S(2)}) %collective-permute-start.11) | collective-permute-done | bytes 262176 | tf_op jit(solution)/shard_map/ppermute | solution.py:317
  87.5 19.8 %optics.1 = (f32[1,256,256]{2,1,0:T(8,128)S(1)}, f32[1,256,256]{2,1,0:T(8,128)S(1)}, f32[1,256,256]{2,1,0:T(8,128)S(1)}, f32[1,256,256]{2,1,0:T(8,128)S(1)}, f32...) custom-call(s32[2]{0:T(128)S(1)} %pad_add_fusion.ids, ...), custom_call_target="tpu_custom_call" | custom-call | flops 20000000000 | bytes 20000000 | tf_op jit(solution)/shard_map/optics/pallas_call | solution.py:360
  111.9 8.2 %collective-permute-done.33 = f32[2,64,256]{2,1,0:T(8,128)S(1)} collective-permute-done((f32[2,64,256]{2,1,0:T(8,128)S(1)}, f32[2,64,256]{2,1,0:T(8,128)S(1)}, u32[]{:S(2)}, u32[]{:S(2)}) %collective-permute-start.33) | collective-permute-done | bytes 131104 | tf_op jit(solution)/shard_map/ppermute | solution.py:317
  124.6 3.0 %collective-permute-done.22.rest_3_ = f32[1,256,256]{2,1,0:T(8,128)S(1)} collective-permute-done((f32[1,256,256]{2,1,0:T(8,128)S(1)}, f32[1,256,256]{2,1,0:T(8,128)S(1)}, u32[]{:S(2)}, u32[]{:S(2)}) %collective-permute-start.22) | collective-permute-done | bytes 262176 | tf_op jit(solution)/shard_map/ppermute | solution.py:317
  129.7 2.2 %place.5 = (f32[1,256,512]{2,1,0:T(8,128)S(1)}, f32[1,256,512]{2,1,0:T(8,128)S(1)}) custom-call(s32[2]{0:T(128)S(1)} %pad_add_fusion.ids, s32[4,2]{1,0:T(4,128)S(1)} %copy.13.positions, f32[1,256,256]{2,1,0:T(8,128)S(1)} %get-tuple-element.72.rest_0_, f32[1,256,256]{2,1,0:T(8,128)S(1)} %collective-permute-done.20.rest_1_, ...), custom_call_target="tpu_custom_call" | custom-call | flops 2000000000 | bytes 2000000 | tf_op jit(solution)/shard_map/place/pallas_call | solution.py:381
  132.0 2.1 %collective-permute-done.29.rest_2_ = f32[1,256,256]{2,1,0:T(8,128)S(1)} collective-permute-done((f32[1,256,256]{2,1,0:T(8,128)S(1)}, f32[1,256,256]{2,1,0:T(8,128)S(1)}, u32[]{:S(2)}, u32[]{:S(2)}) %collective-permute-start.29) | collective-permute-done | bytes 262176 | tf_op jit(solution)/shard_map/ppermute | solution.py:317
  135.6 3.1 %collective-permute-done.30.rest_3_ = f32[1,256,256]{2,1,0:T(8,128)S(1)} collective-permute-done((f32[1,256,256]{2,1,0:T(8,128)S(1)}, f32[1,256,256]{2,1,0:T(8,128)S(1)}, u32[]{:S(2)}, u32[]{:S(2)}) %collective-permute-start.30) | collective-permute-done | bytes 262176 | tf_op jit(solution)/shard_map/ppermute | solution.py:317
  140.7 2.2 %place.7 = (f32[1,256,512]{2,1,0:T(8,128)S(1)}, f32[1,256,512]{2,1,0:T(8,128)S(1)}) custom-call(s32[2]{0:T(128)S(1)} %pad_add_fusion.ids, s32[4,2]{1,0:T(4,128)S(1)} %copy.13.positions, f32[1,256,256]{2,1,0:T(8,128)S(1)} %get-tuple-element.84.rest_0_, f32[1,256,256]{2,1,0:T(8,128)S(1)} %collective-permute-done.28.rest_1_, ...), custom_call_target="tpu_custom_call" | custom-call | flops 2000000000 | bytes 2000000 | tf_op jit(solution)/shard_map/place/pallas_call | solution.py:381
  142.9 2.5 %collective-permute-done.25.rest_2_ = f32[1,256,256]{2,1,0:T(8,128)S(1)} collective-permute-done((f32[1,256,256]{2,1,0:T(8,128)S(1)}, f32[1,256,256]{2,1,0:T(8,128)S(1)}, u32[]{:S(2)}, u32[]{:S(2)}) %collective-permute-start.25) | collective-permute-done | bytes 262176 | tf_op jit(solution)/shard_map/ppermute | solution.py:317
  145.4 4.6 %collective-permute-done.26.rest_3_ = f32[1,256,256]{2,1,0:T(8,128)S(1)} collective-permute-done((f32[1,256,256]{2,1,0:T(8,128)S(1)}, f32[1,256,256]{2,1,0:T(8,128)S(1)}, u32[]{:S(2)}, u32[]{:S(2)}) %collective-permute-start.26) | collective-permute-done | bytes 262176 | tf_op jit(solution)/shard_map/ppermute | solution.py:317
  150.0 2.5 %collective-permute-start.31 = (f32[1,256,512]{2,1,0:T(8,128)S(1)}, f32[1,256,512]{2,1,0:T(8,128)S(1)}, u32[]{:S(2)}, u32[]{:S(2)}) collective-permute-start(f32[1,256,512]{2,1,0:T(8,128)S(1)} %get-tuple-element.89), channel_id=1, source_target_pairs={{0,1},{1,2},{2,3},{3,4},{4,5},{5,6},{6,7},{8,9},{9,10},{10,11},{11... | collective-permute-start | bytes 1572872 | tf_op jit(solution)/shard_map/ppermute | solution.py:322
  152.5 2.2 %place.6 = (f32[1,256,512]{2,1,0:T(8,128)S(1)}, f32[1,256,512]{2,1,0:T(8,128)S(1)}) custom-call(s32[2]{0:T(128)S(1)} %pad_add_fusion.ids, s32[4,2]{1,0:T(4,128)S(1)} %copy.13.positions, f32[1,256,256]{2,1,0:T(8,128)S(1)} %get-tuple-element.78.rest_0_, f32[1,256,256]{2,1,0:T(8,128)S(1)} %collective-permute-done.24.rest_1_, ...), custom_call_target="tpu_custom_call" | custom-call | flops 2000000000 | bytes 2000000 | tf_op jit(solution)/shard_map/place/pallas_call | solution.py:381
  154.8 4.3 %collective-permute-start.27 = (f32[1,256,512]{2,1,0:T(8,128)S(1)}, f32[1,256,512]{2,1,0:T(8,128)S(1)}, u32[]{:S(2)}, u32[]{:S(2)}) collective-permute-start(f32[1,256,512]{2,1,0:T(8,128)S(1)} %get-tuple-element.83), channel_id=1, source_target_pairs={{0,1},{1,2},{2,3},{3,4},{4,5},{5,6},{6,7},{8,9},{9,10},{10,11},{11... | collective-permute-start | bytes 1572872 | tf_op jit(solution)/shard_map/ppermute | solution.py:322
  159.1 2.5 %collective-permute-start.23 = (f32[1,256,512]{2,1,0:T(8,128)S(1)}, f32[1,256,512]{2,1,0:T(8,128)S(1)}, u32[]{:S(2)}, u32[]{:S(2)}) collective-permute-start(f32[1,256,512]{2,1,0:T(8,128)S(1)} %get-tuple-element.77), channel_id=1, source_target_pairs={{0,1},{1,2},{2,3},{3,4},{4,5},{5,6},{6,7},{8,9},{9,10},{10,11},{11... | collective-permute-start | bytes 1572872 | tf_op jit(solution)/shard_map/ppermute | solution.py:322
  161.6 2.2 %place.4 = (f32[1,256,512]{2,1,0:T(8,128)S(1)}, f32[1,256,512]{2,1,0:T(8,128)S(1)}) custom-call(s32[2]{0:T(128)S(1)} %pad_add_fusion.ids, s32[4,2]{1,0:T(4,128)S(1)} %copy.13.positions, f32[1,256,256]{2,1,0:T(8,128)S(1)} %get-tuple-element.66.rest_0_, f32[1,256,256]{2,1,0:T(8,128)S(1)} %collective-permute-done.16.rest_1_, ...), custom_call_target="tpu_custom_call" | custom-call | flops 2000000000 | bytes 2000000 | tf_op jit(solution)/shard_map/place/pallas_call | solution.py:381
  163.8 4.3 %collective-permute-start.19 = (f32[1,256,512]{2,1,0:T(8,128)S(1)}, f32[1,256,512]{2,1,0:T(8,128)S(1)}, u32[]{:S(2)}, u32[]{:S(2)}) collective-permute-start(f32[1,256,512]{2,1,0:T(8,128)S(1)} %get-tuple-element.71), channel_id=1, source_target_pairs={{0,1},{1,2},{2,3},{3,4},{4,5},{5,6},{6,7},{8,9},{9,10},{10,11},{11... | collective-permute-start | bytes 1572872 | tf_op jit(solution)/shard_map/ppermute | solution.py:322
  168.3 32.9 %collective-permute-done.36 = f32[2,64,256]{2,1,0:T(8,128)S(1)} collective-permute-done((f32[2,64,256]{2,1,0:T(8,128)S(1)}, f32[2,64,256]{2,1,0:T(8,128)S(1)}, u32[]{:S(2)}, u32[]{:S(2)}) %collective-permute-start.36) | collective-permute-done | bytes 131104 | tf_op jit(solution)/shard_map/ppermute | solution.py:317
  201.3 2.6 %collective-permute-start.37 = (f32[2,64,256]{2,1,0:T(8,128)S(1)}, f32[2,64,256]{2,1,0:T(8,128)S(1)}, u32[]{:S(2)}, u32[]{:S(2)}) collective-permute-start(f32[2,64,256]{2,1,0:T(8,128)S(1)} %add.42), channel_id=1, source_target_pairs={{0,4},{1,5},{2,6},{3,7},{4,0},{5,1},{6,2},{7,3},{8,12},{9,13},{10,... | collective-permute-start | bytes 393224 | tf_op jit(solution)/shard_map/ppermute | solution.py:317
  203.9 6.6 %collective-permute-done.37 = f32[2,64,256]{2,1,0:T(8,128)S(1)} collective-permute-done((f32[2,64,256]{2,1,0:T(8,128)S(1)}, f32[2,64,256]{2,1,0:T(8,128)S(1)}, u32[]{:S(2)}, u32[]{:S(2)}) %collective-permute-start.37) | collective-permute-done | bytes 131104 | tf_op jit(solution)/shard_map/ppermute | solution.py:317
  (100 shorter events, 39.6 us)
Async XLA Ops:
  2.3 17.7 %collective-permute-start.12 = (f32[1,256,512]{2,1,0:T(8,128)S(1)}, f32[1,256,512]{2,1,0:T(8,128)}, u32[]{:S(2)}, u32[]{:S(2)}) collective-permute-start(f32[1,256,512]{2,1,0:T(8,128)S(1)} %get-tuple-element.94.own), channel_id=1, source_target_pairs={{1,0},{2,1},{3,2},{4,3},{5,4},{6,5},{7,6},{9,8},{10,9},{11,10},{12... | collective-permute-start | bytes 1572872 | tf_op jit(solution)/shard_map/ppermute | solution.py:322
  4.3 27.0 %collective-permute-start.4 = (f32[1,256,512]{2,1,0:T(8,128)S(1)}, f32[1,256,512]{2,1,0:T(8,128)}, u32[]{:S(2)}, u32[]{:S(2)}) collective-permute-start(f32[1,256,512]{2,1,0:T(8,128)S(1)} %get-tuple-element.95.own), channel_id=1, source_target_pairs={{1,0},{2,1},{3,2},{4,3},{5,4},{6,5},{7,6},{9,8},{10,9},{11,10},{12... | collective-permute-start | bytes 1572872 | tf_op jit(solution)/shard_map/ppermute | solution.py:322
  6.2 36.2 %collective-permute-start = (f32[1,256,512]{2,1,0:T(8,128)S(1)}, f32[1,256,512]{2,1,0:T(8,128)S(1)}, u32[]{:S(2)}, u32[]{:S(2)}) collective-permute-start(f32[1,256,512]{2,1,0:T(8,128)S(1)} %get-tuple-element.96.own), channel_id=1, source_target_pairs={{1,0},{2,1},{3,2},{4,3},{5,4},{6,5},{7,6},{9,8},{10,9},{11,10},{12... | collective-permute-start | bytes 1572872 | tf_op jit(solution)/shard_map/ppermute | solution.py:322
  8.1 44.4 %collective-permute-start.8 = (f32[1,256,512]{2,1,0:T(8,128)S(1)}, f32[1,256,512]{2,1,0:T(8,128)S(1)}, u32[]{:S(2)}, u32[]{:S(2)}) collective-permute-start(f32[1,256,512]{2,1,0:T(8,128)S(1)} %get-tuple-element.97.own), channel_id=1, source_target_pairs={{1,0},{2,1},{3,2},{4,3},{5,4},{6,5},{7,6},{9,8},{10,9},{11,10},{12... | collective-permute-start | bytes 1572872 | tf_op jit(solution)/shard_map/ppermute | solution.py:322
  23.3 30.7 %collective-permute-start.13 = (f32[1,256,256]{2,1,0:T(8,128)S(1)}, f32[1,256,256]{2,1,0:T(8,128)S(1)}, u32[]{:S(2)}, u32[]{:S(2)}) collective-permute-start(f32[1,256,256]{2,1,0:T(8,128)S(1)} %get-tuple-element.63), channel_id=1, source_target_pairs={{0,8},{8,0},{16,24},{24,16},{1,9},{9,1},{17,25},{25,17},{2,10},{10... | collective-permute-start | bytes 786440 | tf_op jit(solution)/shard_map/ppermute | solution.py:317
  23.3 30.7 %collective-permute-start.14 = (f32[1,256,256]{2,1,0:T(8,128)S(1)}, f32[1,256,256]{2,1,0:T(8,128)S(1)}, u32[]{:S(2)}, u32[]{:S(2)}) collective-permute-start(f32[1,256,256]{2,1,0:T(8,128)S(1)} %get-tuple-element.64), channel_id=1, source_target_pairs={{0,16},{8,24},{16,0},{24,8},{1,17},{9,25},{17,1},{25,9},{2,18},{10... | collective-permute-start | bytes 786440 | tf_op jit(solution)/shard_map/ppermute | solution.py:317
  31.3 26.3 %collective-permute-start.15 = (f32[1,256,256]{2,1,0:T(8,128)S(1)}, f32[1,256,256]{2,1,0:T(8,128)S(1)}, u32[]{:S(2)}, u32[]{:S(2)}) collective-permute-start(f32[1,256,256]{2,1,0:T(8,128)S(1)} %get-tuple-element.65), channel_id=1, source_target_pairs={{0,24},{8,16},{16,8},{24,0},{1,25},{9,17},{17,9},{25,1},{2,26},{10... | collective-permute-start | bytes 786440 | tf_op jit(solution)/shard_map/ppermute | solution.py:317
  42.4 16.6 %collective-permute-start.5 = (f32[1,256,256]{2,1,0:T(8,128)S(1)}, f32[1,256,256]{2,1,0:T(8,128)S(1)}, u32[]{:S(2)}, u32[]{:S(2)}) collective-permute-start(f32[1,256,256]{2,1,0:T(8,128)S(1)} %get-tuple-element.55), channel_id=1, source_target_pairs={{0,8},{8,0},{16,24},{24,16},{1,9},{9,1},{17,25},{25,17},{2,10},{10... | collective-permute-start | bytes 786440 | tf_op jit(solution)/shard_map/ppermute | solution.py:317
  54.0 12.4 %collective-permute-start.7 = (f32[1,256,256]{2,1,0:T(8,128)S(1)}, f32[1,256,256]{2,1,0:T(8,128)S(1)}, u32[]{:S(2)}, u32[]{:S(2)}) collective-permute-start(f32[1,256,256]{2,1,0:T(8,128)S(1)} %get-tuple-element.57), channel_id=1, source_target_pairs={{0,24},{8,16},{16,8},{24,0},{1,25},{9,17},{17,9},{25,1},{2,26},{10... | collective-permute-start | bytes 786440 | tf_op jit(solution)/shard_map/ppermute | solution.py:317
  54.0 12.9 %collective-permute-start.1 = (f32[1,256,256]{2,1,0:T(8,128)S(1)}, f32[1,256,256]{2,1,0:T(8,128)S(1)}, u32[]{:S(2)}, u32[]{:S(2)}) collective-permute-start(f32[1,256,256]{2,1,0:T(8,128)S(1)} %get-tuple-element.51), channel_id=1, source_target_pairs={{0,8},{8,0},{16,24},{24,16},{1,9},{9,1},{17,25},{25,17},{2,10},{10... | collective-permute-start | bytes 786440 | tf_op jit(solution)/shard_map/ppermute | solution.py:317
  57.6 15.4 %collective-permute-start.2 = (f32[1,256,256]{2,1,0:T(8,128)S(1)}, f32[1,256,256]{2,1,0:T(8,128)S(1)}, u32[]{:S(2)}, u32[]{:S(2)}) collective-permute-start(f32[1,256,256]{2,1,0:T(8,128)S(1)} %get-tuple-element.52), channel_id=1, source_target_pairs={{0,16},{8,24},{16,0},{24,8},{1,17},{9,25},{17,1},{25,9},{2,18},{10... | collective-permute-start | bytes 786440 | tf_op jit(solution)/shard_map/ppermute | solution.py:317
  59.1 18.5 %collective-permute-start.3 = (f32[1,256,256]{2,1,0:T(8,128)S(1)}, f32[1,256,256]{2,1,0:T(8,128)S(1)}, u32[]{:S(2)}, u32[]{:S(2)}) collective-permute-start(f32[1,256,256]{2,1,0:T(8,128)S(1)} %get-tuple-element.53), channel_id=1, source_target_pairs={{0,24},{8,16},{16,8},{24,0},{1,25},{9,17},{17,9},{25,1},{2,26},{10... | collective-permute-start | bytes 786440 | tf_op jit(solution)/shard_map/ppermute | solution.py:317
  61.7 15.9 %collective-permute-start.9 = (f32[1,256,256]{2,1,0:T(8,128)S(1)}, f32[1,256,256]{2,1,0:T(8,128)S(1)}, u32[]{:S(2)}, u32[]{:S(2)}) collective-permute-start(f32[1,256,256]{2,1,0:T(8,128)S(1)} %get-tuple-element.59), channel_id=1, source_target_pairs={{0,8},{8,0},{16,24},{24,16},{1,9},{9,1},{17,25},{25,17},{2,10},{10... | collective-permute-start | bytes 786440 | tf_op jit(solution)/shard_map/ppermute | solution.py:317
  66.4 17.8 %collective-permute-start.10 = (f32[1,256,256]{2,1,0:T(8,128)S(1)}, f32[1,256,256]{2,1,0:T(8,128)S(1)}, u32[]{:S(2)}, u32[]{:S(2)}) collective-permute-start(f32[1,256,256]{2,1,0:T(8,128)S(1)} %get-tuple-element.60), channel_id=1, source_target_pairs={{0,16},{8,24},{16,0},{24,8},{1,17},{9,25},{17,1},{25,9},{2,18},{10... | collective-permute-start | bytes 786440 | tf_op jit(solution)/shard_map/ppermute | solution.py:317
  66.9 19.9 %collective-permute-start.11 = (f32[1,256,256]{2,1,0:T(8,128)S(1)}, f32[1,256,256]{2,1,0:T(8,128)S(1)}, u32[]{:S(2)}, u32[]{:S(2)}) collective-permute-start(f32[1,256,256]{2,1,0:T(8,128)S(1)} %get-tuple-element.61), channel_id=1, source_target_pairs={{0,24},{8,16},{16,8},{24,0},{1,25},{9,17},{17,9},{25,1},{2,26},{10... | collective-permute-start | bytes 786440 | tf_op jit(solution)/shard_map/ppermute | solution.py:317
  107.3 15.8 %collective-permute-start.20 = (f32[1,256,256]{2,1,0:T(8,128)S(1)}, f32[1,256,256]{2,1,0:T(8,128)S(1)}, u32[]{:S(2)}, u32[]{:S(2)}) collective-permute-start(f32[1,256,256]{2,1,0:T(8,128)S(1)} %get-tuple-element.73), channel_id=1, source_target_pairs={{0,8},{8,0},{16,24},{24,16},{1,9},{9,1},{17,25},{25,17},{2,10},{10... | collective-permute-start | bytes 786440 | tf_op jit(solution)/shard_map/ppermute | solution.py:317
  108.1 16.4 %collective-permute-start.21 = (f32[1,256,256]{2,1,0:T(8,128)S(1)}, f32[1,256,256]{2,1,0:T(8,128)S(1)}, u32[]{:S(2)}, u32[]{:S(2)}) collective-permute-start(f32[1,256,256]{2,1,0:T(8,128)S(1)} %get-tuple-element.74), channel_id=1, source_target_pairs={{0,16},{8,24},{16,0},{24,8},{1,17},{9,25},{17,1},{25,9},{2,18},{10... | collective-permute-start | bytes 786440 | tf_op jit(solution)/shard_map/ppermute | solution.py:317
  110.2 11.8 %collective-permute-start.34 = (f32[2,64,256]{2,1,0:T(8,128)S(1)}, f32[2,64,256]{2,1,0:T(8,128)S(1)}, u32[]{:S(2)}, u32[]{:S(2)}) collective-permute-start(f32[2,64,256]{2,1,0:T(8,128)S(1)} %get-tuple-element.93), channel_id=1, source_target_pairs={{0,24},{8,16},{16,8},{24,0},{1,25},{9,17},{17,9},{25,1},{2,26},{10... | collective-permute-start | bytes 393224 | tf_op jit(solution)/shard_map/ppermute | solution.py:317
  111.5 16.1 %collective-permute-start.22 = (f32[1,256,256]{2,1,0:T(8,128)S(1)}, f32[1,256,256]{2,1,0:T(8,128)S(1)}, u32[]{:S(2)}, u32[]{:S(2)}) collective-permute-start(f32[1,256,256]{2,1,0:T(8,128)S(1)} %get-tuple-element.75), channel_id=1, source_target_pairs={{0,24},{8,16},{16,8},{24,0},{1,25},{9,17},{17,9},{25,1},{2,26},{10... | collective-permute-start | bytes 786440 | tf_op jit(solution)/shard_map/ppermute | solution.py:317
  123.0 11.1 %collective-permute-start.29 = (f32[1,256,256]{2,1,0:T(8,128)S(1)}, f32[1,256,256]{2,1,0:T(8,128)S(1)}, u32[]{:S(2)}, u32[]{:S(2)}) collective-permute-start(f32[1,256,256]{2,1,0:T(8,128)S(1)} %get-tuple-element.86), channel_id=1, source_target_pairs={{0,16},{8,24},{16,0},{24,8},{1,17},{9,25},{17,1},{25,9},{2,18},{10... | collective-permute-start | bytes 786440 | tf_op jit(solution)/shard_map/ppermute | solution.py:317
  124.5 14.2 %collective-permute-start.30 = (f32[1,256,256]{2,1,0:T(8,128)S(1)}, f32[1,256,256]{2,1,0:T(8,128)S(1)}, u32[]{:S(2)}, u32[]{:S(2)}) collective-permute-start(f32[1,256,256]{2,1,0:T(8,128)S(1)} %get-tuple-element.87), channel_id=1, source_target_pairs={{0,24},{8,16},{16,8},{24,0},{1,25},{9,17},{17,9},{25,1},{2,26},{10... | collective-permute-start | bytes 786440 | tf_op jit(solution)/shard_map/ppermute | solution.py:317
  127.5 17.8 %collective-permute-start.25 = (f32[1,256,256]{2,1,0:T(8,128)S(1)}, f32[1,256,256]{2,1,0:T(8,128)S(1)}, u32[]{:S(2)}, u32[]{:S(2)}) collective-permute-start(f32[1,256,256]{2,1,0:T(8,128)S(1)} %get-tuple-element.80), channel_id=1, source_target_pairs={{0,16},{8,24},{16,0},{24,8},{1,17},{9,25},{17,1},{25,9},{2,18},{10... | collective-permute-start | bytes 786440 | tf_op jit(solution)/shard_map/ppermute | solution.py:317
  128.3 21.7 %collective-permute-start.26 = (f32[1,256,256]{2,1,0:T(8,128)S(1)}, f32[1,256,256]{2,1,0:T(8,128)S(1)}, u32[]{:S(2)}, u32[]{:S(2)}) collective-permute-start(f32[1,256,256]{2,1,0:T(8,128)S(1)} %get-tuple-element.81), channel_id=1, source_target_pairs={{0,24},{8,16},{16,8},{24,0},{1,25},{9,17},{17,9},{25,1},{2,26},{10... | collective-permute-start | bytes 786440 | tf_op jit(solution)/shard_map/ppermute | solution.py:317
  131.9 22.8 %collective-permute-start.16 = (f32[1,256,256]{2,1,0:T(8,128)S(1)}, f32[1,256,256]{2,1,0:T(8,128)S(1)}, u32[]{:S(2)}, u32[]{:S(2)}) collective-permute-start(f32[1,256,256]{2,1,0:T(8,128)S(1)} %get-tuple-element.67), channel_id=1, source_target_pairs={{0,8},{8,0},{16,24},{24,16},{1,9},{9,1},{17,25},{25,17},{2,10},{10... | collective-permute-start | bytes 786440 | tf_op jit(solution)/shard_map/ppermute | solution.py:317
  134.1 24.9 %collective-permute-start.17 = (f32[1,256,256]{2,1,0:T(8,128)S(1)}, f32[1,256,256]{2,1,0:T(8,128)S(1)}, u32[]{:S(2)}, u32[]{:S(2)}) collective-permute-start(f32[1,256,256]{2,1,0:T(8,128)S(1)} %get-tuple-element.68), channel_id=1, source_target_pairs={{0,16},{8,24},{16,0},{24,8},{1,17},{9,25},{17,1},{25,9},{2,18},{10... | collective-permute-start | bytes 786440 | tf_op jit(solution)/shard_map/ppermute | solution.py:317
  138.8 22.8 %collective-permute-start.18 = (f32[1,256,256]{2,1,0:T(8,128)S(1)}, f32[1,256,256]{2,1,0:T(8,128)S(1)}, u32[]{:S(2)}, u32[]{:S(2)}) collective-permute-start(f32[1,256,256]{2,1,0:T(8,128)S(1)} %get-tuple-element.69), channel_id=1, source_target_pairs={{0,24},{8,16},{16,8},{24,0},{1,25},{9,17},{17,9},{25,1},{2,26},{10... | collective-permute-start | bytes 786440 | tf_op jit(solution)/shard_map/ppermute | solution.py:317
  145.4 22.8 %collective-permute-start.35 = (f32[2,64,256]{2,1,0:T(8,128)S(1)}, f32[2,64,256]{2,1,0:T(8,128)S(1)}, u32[]{:S(2)}, u32[]{:S(2)}) collective-permute-start(f32[2,64,256]{2,1,0:T(8,128)S(1)} %add_add_fusion), channel_id=1, source_target_pairs={{0,1},{1,0},{2,3},{3,2},{4,5},{5,4},{6,7},{7,6},{8,9},{9,8},{10,11... | collective-permute-start | bytes 393224 | tf_op jit(solution)/shard_map/ppermute | solution.py:317
  150.0 61.1 %collective-permute-start.31 = (f32[1,256,512]{2,1,0:T(8,128)S(1)}, f32[1,256,512]{2,1,0:T(8,128)S(1)}, u32[]{:S(2)}, u32[]{:S(2)}) collective-permute-start(f32[1,256,512]{2,1,0:T(8,128)S(1)} %get-tuple-element.89), channel_id=1, source_target_pairs={{0,1},{1,2},{2,3},{3,4},{4,5},{5,6},{6,7},{8,9},{9,10},{10,11},{11... | collective-permute-start | bytes 1572872 | tf_op jit(solution)/shard_map/ppermute | solution.py:322
  154.8 56.4 %collective-permute-start.27 = (f32[1,256,512]{2,1,0:T(8,128)S(1)}, f32[1,256,512]{2,1,0:T(8,128)S(1)}, u32[]{:S(2)}, u32[]{:S(2)}) collective-permute-start(f32[1,256,512]{2,1,0:T(8,128)S(1)} %get-tuple-element.83), channel_id=1, source_target_pairs={{0,1},{1,2},{2,3},{3,4},{4,5},{5,6},{6,7},{8,9},{9,10},{10,11},{11... | collective-permute-start | bytes 1572872 | tf_op jit(solution)/shard_map/ppermute | solution.py:322
  159.1 52.2 %collective-permute-start.23 = (f32[1,256,512]{2,1,0:T(8,128)S(1)}, f32[1,256,512]{2,1,0:T(8,128)S(1)}, u32[]{:S(2)}, u32[]{:S(2)}) collective-permute-start(f32[1,256,512]{2,1,0:T(8,128)S(1)} %get-tuple-element.77), channel_id=1, source_target_pairs={{0,1},{1,2},{2,3},{3,4},{4,5},{5,6},{6,7},{8,9},{9,10},{10,11},{11... | collective-permute-start | bytes 1572872 | tf_op jit(solution)/shard_map/ppermute | solution.py:322
  163.8 47.6 %collective-permute-start.19 = (f32[1,256,512]{2,1,0:T(8,128)S(1)}, f32[1,256,512]{2,1,0:T(8,128)S(1)}, u32[]{:S(2)}, u32[]{:S(2)}) collective-permute-start(f32[1,256,512]{2,1,0:T(8,128)S(1)} %get-tuple-element.71), channel_id=1, source_target_pairs={{0,1},{1,2},{2,3},{3,4},{4,5},{5,6},{6,7},{8,9},{9,10},{10,11},{11... | collective-permute-start | bytes 1572872 | tf_op jit(solution)/shard_map/ppermute | solution.py:322
  168.2 33.0 %collective-permute-start.36 = (f32[2,64,256]{2,1,0:T(8,128)S(1)}, f32[2,64,256]{2,1,0:T(8,128)S(1)}, u32[]{:S(2)}, u32[]{:S(2)}) collective-permute-start(f32[2,64,256]{2,1,0:T(8,128)S(1)} %add.41), channel_id=1, source_target_pairs={{0,2},{1,3},{2,0},{3,1},{4,6},{5,7},{6,4},{7,5},{8,10},{9,11},{10,... | collective-permute-start | bytes 393224 | tf_op jit(solution)/shard_map/ppermute | solution.py:317
  (22 other events, 144.4 us)
where the time goes:
time: 214 us; the launch traced here: 213 us
  waiting for transfers between devices  120 us (56%)
  starting transfers between devices  44.3 us (21%)
  Pallas kernels  39.4 us (18%)
  local copies, waits for them, and re-layouts  5.43 us (3%)
  other arithmetic  2.78 us (1%)
    ppermute x30, waiting for transfers between devices, swap(): return lax.ppermute(x, axis, [(i, i ^ offset) for i in range(peers)])  88 us
    ppermute x8, waiting for transfers between devices, shift(): lax.ppermute(x, axis, [(i, i + by) for i in range(peers) if 0 <= i + by <...  32.2 us
    ppermute x30, starting transfers between devices, swap(): return lax.ppermute(x, axis, [(i, i ^ offset) for i in range(peers)])  22.9 us
    ppermute x8, starting transfers between devices, shift(): lax.ppermute(x, axis, [(i, i + by) for i in range(peers) if 0 <= i + by <...  21.4 us
    pallas_call x1, Pallas kernels, body(): run_kernel(functools.partial(optics_kernel, peers, per_device), 'optics',...  19.8 us
    pallas_call x4, Pallas kernels, body(): run_kernel(functools.partial(crop_kernel, peers), 'crop', (shape(1, size,...  9.22 us
    pallas_call x4, Pallas kernels, body(): run_kernel(functools.partial(place_kernel, peers), 'place', (shape(1, row...  8.8 us
  transfers between devices with their start and end apart: 38, of which 19 were waited for; matrix products, arithmetic and copies ran while one was open for 1% of the time, Pallas kernels for 9%

commit v1 on v0

v1 whole, which is shorter than its diff:
```python
import functools

import jax
import jax.numpy as jnp
import ml_dtypes
import numpy as np
from jax import lax
from jax.experimental import pallas as pl
from jax.experimental.pallas import tpu as pltpu
from jax.sharding import PartitionSpec as P

LANES = 128
F32 = jnp.float32
BF16 = jnp.bfloat16


def split_table(table):
    high = table.astype(np.float32).astype(ml_dtypes.bfloat16)
    low = (table - high.astype(np.float64)).astype(np.float32).astype(ml_dtypes.bfloat16)
    return high, low


def left_form(matrix):
    return np.block([[matrix.real, -matrix.imag], [matrix.imag, matrix.real]])


def folded(matrix):
    half = matrix.shape[0] // 2
    near = matrix[:half, :half]
    mirrored = matrix[:half, half:][:, ::-1]
    return (near + mirrored) / 2, (near - mirrored) / 2


def optics_tables(length):
    index = np.arange(length)
    fourier = np.exp(-2j * np.pi * (index[:, None] * index[None, :] % length) / length)
    frequency = np.where(index < length // 2, index, index - length).astype(np.float64)
    phase = np.exp(-1j * np.pi * frequency**2 / (4 * length))
    fresnel = (np.conj(fourier) * phase[None, :]) @ fourier / length
    odd = 2 * index + 1
    turn = odd[:, None] * odd[None, :] % (4 * length)
    shifted = np.exp(-2j * np.pi * turn / (4 * length)) / np.sqrt(length)
    left, right = [], []
    for matrix in (fresnel, shifted):
        for block in folded(matrix):
            high, low = split_table(left_form(block))
            left.append(np.concatenate([high, high, low], axis=1))
            high, low = split_table(left_form(np.conj(block)))
            left.append(np.concatenate([high, high, low], axis=1))
            high, low = split_table(left_form(np.conj(block)))
            right.append(np.concatenate([high, high, low], axis=0))
            high, low = split_table(left_form(block))
            right.append(np.concatenate([high, high, low], axis=0))
    order = np.concatenate([index[: length // 2], index[length // 2 :][::-1]])
    ramp = np.exp(1j * np.pi * order / length)
    tilt = ramp[:, None] * ramp[None, :]
    return np.stack(left), np.stack(right), np.stack([tilt.real, tilt.imag]).astype(np.float32)


def reversal(size):
    row = lax.broadcasted_iota(jnp.int32, (size, size), 0)
    col = lax.broadcasted_iota(jnp.int32, (size, size), 1)
    return jnp.where(row + col == size - 1, 1.0, 0.0).astype(F32)


def exact_dot(a, b):
    return jnp.dot(a, b, precision=lax.Precision.HIGHEST, preferred_element_type=F32)


def mirror_halves(x, flip):
    half = x.shape[0] // 2
    x = jnp.concatenate([x[:, :half], exact_dot(x[:, half:], flip)], axis=1)
    return jnp.concatenate([x[:half], exact_dot(flip, x[half:])], axis=0)


def prep_kernel(ids, probe, amplitudes, probe_out, amp_out):
    flip = reversal(probe.shape[-1] // 2)
    for part in range(2):
        probe_out[part] = mirror_halves(probe[part], flip)
    amp_out[...] = mirror_halves(amplitudes[ids[0]], flip)


def crop_kernel(peers, plane, waits, ids, positions, strips, rim, *rest):
    rest = rest[waits:]
    own_out, near_out = rest[:2]
    far_outs, rest = rest[2 : peers // 2 + 1], rest[peers // 2 + 1 :]
    outs = [own_out, near_out] + [far.at[i] for far in far_outs for i in range(2)]
    ext, cut, loaded, stored = rest
    rows, cols = rim.shape
    blocks = cols // LANES
    size = own_out.shape[-1]
    loads = []
    for block in range(blocks):
        columns = pl.ds(block * LANES, LANES)
        loads.append(
            pltpu.make_async_copy(
                strips.at[plane[0], plane[1], :, columns], ext.at[block, pl.ds(0, rows)], loaded.at[2 * block]
            )
        )
        loads.append(
            pltpu.make_async_copy(
                rim.at[:, columns], ext.at[block, pl.ds(rows, rows)], loaded.at[2 * block + 1]
            )
        )
    for copy in loads:
        copy.start()
    flip = reversal(size // 2)
    lane = lax.broadcasted_iota(jnp.int32, (size, LANES), 1)
    ext[blocks] = jnp.zeros((2 * rows, LANES), F32)
    for copy in loads:
        copy.wait()
    stores = []
    for offset in sorted(range(peers), key=lambda m: -(m // 2)):
        window = ids[0] ^ offset
        row_first = positions[window, 0] - ids[1] * rows
        col_first = positions[window, 1]
        block_first = col_first >> 7
        within = col_first & (LANES - 1)
        moved = [
            pltpu.roll(ext[block_first + i, pl.ds(row_first, size), :], (LANES - within) & (LANES - 1), 1)
            for i in range(size // LANES + 1)
        ]
        keep = lane < LANES - within
        picked = [jnp.where(keep, moved[i], moved[i + 1]) for i in range(size // LANES)]
        cut[offset] = mirror_halves(jnp.concatenate(picked, axis=1), flip)
        copy = pltpu.make_async_copy(cut.at[offset], outs[offset], stored.at[offset])
        copy.start()
        stores.append(copy)
    for copy in stores:
        copy.wait()


def place_kernel(peers, waits, ids, positions, *rest):
    own_in, near_in = rest[:2]
    far_ins, rest = rest[2:peers], rest[peers + waits :]
    pieces = [own_in, near_in]
    for i in range(0, len(far_ins), 2):
        pieces += [far_ins[i].at[0], far_ins[i + 1]]
    own, rim, ext, got, loaded, stored = rest
    rows, cols = own.shape
    blocks = cols // LANES
    size = own_in.shape[-1]
    loads = [
        pltpu.make_async_copy(pieces[offset], got.at[offset], loaded.at[offset]) for offset in range(peers)
    ]
    for copy in loads:
        copy.start()
    flip = reversal(size // 2)
    lane = lax.broadcasted_iota(jnp.int32, (size, LANES), 1)
    ext[...] = jnp.zeros(ext.shape, F32)
    for offset in range(peers):
        window = ids[0] ^ offset
        row_first = positions[window, 0] - ids[1] * rows
        col_first = positions[window, 1]
        block_first = col_first >> 7
        within = col_first & (LANES - 1)
        loads[offset].wait()
        plain = mirror_halves(got[offset], flip)
        moved = [pltpu.roll(plain[:, i * LANES : (i + 1) * LANES], within, 1) for i in range(size // LANES)]
        keep = lane >= within
        zero = jnp.zeros((size, LANES), F32)
        moved = [zero] + moved + [zero]
        for i in range(size // LANES + 1):
            place = (block_first + i, pl.ds(row_first, size))
            ext[place] = ext[place] + jnp.where(keep, moved[i + 1], moved[i])
    stores = []
    for block in range(blocks):
        columns = pl.ds(block * LANES, LANES)
        stores.append(
            pltpu.make_async_copy(ext.at[block, pl.ds(rows, rows)], rim.at[:, columns], stored.at[2 * block])
        )
        stores.append(
            pltpu.make_async_copy(ext.at[block, pl.ds(0, rows)], own.at[:, columns], stored.at[2 * block + 1])
        )
    for copy in stores:
        copy.start()
    for copy in stores:
        copy.wait()


def split_value(x):
    high = x.astype(BF16)
    low = (x - high.astype(F32)).astype(BF16)
    return high, low


def sandwich(re, im, left, right, base, conj):
    half = re.shape[0] // 2

    def fold(x):
        upper, lower = x[:half], x[half:]
        even, odd = upper + lower, upper - lower
        parts = []
        for y in (even, odd):
            near, far = y[:, :half], y[:, half:]
            parts.append((near + far, near - far))
        return parts

    re_parts, im_parts = fold(re), fold(im)
    middle = []
    for b in range(2):
        field = jnp.concatenate(
            [jnp.concatenate([re_parts[a][b], im_parts[a][b]], axis=1) for a in range(2)], axis=0
        )
        high, low = split_value(field)
        middle.append(
            jnp.dot(
                jnp.concatenate([high, low, high], axis=1),
                right[base + 2 * b + conj],
                preferred_element_type=F32,
            )
        )
    done = []
    for a in range(2):
        rows = slice(a * half, (a + 1) * half)
        field = jnp.concatenate(
            [
                jnp.concatenate([middle[b][rows, :half] for b in range(2)], axis=1),
                jnp.concatenate([middle[b][rows, half:] for b in range(2)], axis=1),
            ],
            axis=0,
        )
        high, low = split_value(field)
        done.append(
            jnp.dot(
                left[base + 2 * a + conj],
                jnp.concatenate([high, low, high], axis=0),
                preferred_element_type=F32,
            )
        )

    def unfold(even, odd):
        rows = jnp.concatenate([even + odd, even - odd], axis=0)
        near, far = rows[:, :half], rows[:, half:]
        return jnp.concatenate([near + far, near - far], axis=1)

    return (
        unfold(done[0][:half], done[1][:half]),
        unfold(done[0][half:], done[1][half:]),
    )


def optics_kernel(peers, per_device, ids, probe, amplitude, left, right, tilt, *rest):
    chunks = 2 * per_device
    groups = peers // 2 + 1
    crops, pieces = [], []
    for chunk in range(chunks):
        got = rest[chunk * peers : (chunk + 1) * peers]
        crops += list(got[:2])
        for i in range(2, peers, 2):
            crops += [got[i].at[0], got[i + 1]]
    rest = rest[chunks * peers :]
    for chunk in range(chunks):
        out = rest[chunk * groups : (chunk + 1) * groups]
        pieces += list(out[:2])
        for far in out[2:]:
            pieces += [far.at[0], far.at[1]]
    kept, handed = rest[chunks * groups : chunks * groups + 2]
    rest = rest[chunks * groups + 2 :]
    trans, history, terms, grad, loaded, stored = rest
    layers = peers * per_device
    me = ids[0]
    for j in range(per_device):
        for offset in range(peers):
            at = (me ^ offset) * per_device + j
            for part in range(2):
                pltpu.make_async_copy(
                    crops[(j * 2 + part) * peers + offset], trans.at[at, part], loaded.at[2 * at + part]
                ).start()
    history[0] = probe[...]

    def mixed(layer):
        for part in range(2):
            pltpu.make_async_copy(crops[0], trans.at[layer, part], loaded.at[2 * layer + part]).wait()
        t_re, t_im = trans[layer, 0], trans[layer, 1]
        w_re, w_im = history[layer, 0], history[layer, 1]
        return t_re * w_re - t_im * w_im, t_re * w_im + t_im * w_re

    def forward(layer, carry):
        re, im = mixed(layer)
        re, im = sandwich(re, im, left, right, 0, 0)
        history[layer + 1, 0] = re
        history[layer + 1, 1] = im
        return carry

    lax.fori_loop(0, layers - 1, forward, 0)
    re, im = mixed(layers - 1)
    d_re, d_im = tilt[0], tilt[1]
    re, im = re * d_re - im * d_im, re * d_im + im * d_re
    re, im = sandwich(re, im, left, right, 4, 0)
    factor = 1.0 - amplitude[...] / jnp.sqrt(re * re + im * im + 1.0)
    re, im = sandwich(re * factor, im * factor, left, right, 4, 1)
    back_re, back_im = re * d_re + im * d_im, im * d_re - re * d_im

    def collect(layer, back_re, back_im):
        w_re, w_im = history[layer, 0], history[layer, 1]
        terms[layer, 0] = w_re * back_re + w_im * back_im
        terms[layer, 1] = w_re * back_im - w_im * back_re
        owner, j_now = lax.div(layer, per_device), lax.rem(layer, per_device)
        for j in range(per_device):
            for offset in range(peers):

                @pl.when((owner == me ^ offset) & (j_now == j))
                def _():
                    for part in range(2):
                        pltpu.make_async_copy(
                            terms.at[layer, part],
                            pieces[(j * 2 + part) * peers + offset],
                            stored.at[2 * layer + part],
                        ).start()

        t_re, t_im = trans[layer, 0], trans[layer, 1]
        grad[0] = t_re * back_re + t_im * back_im
        grad[1] = t_re * back_im - t_im * back_re

    collect(layers - 1, back_re, back_im)

    def backward(step, carry):
        back_re, back_im = sandwich(grad[0], grad[1], left, right, 0, 1)
        collect(layers - 2 - step, back_re, back_im)
        return carry

    lax.fori_loop(0, layers - 1, backward, 0)
    flip = reversal(grad.shape[-1] // 2)
    share_rows = kept.shape[2]
    for part in range(2):
        grad[part] = mirror_halves(grad[part], flip)
    for offset in range(peers):
        first = pl.multiple_of((me ^ offset) * share_rows, share_rows)
        target = handed if offset % 2 else kept
        target[offset // 2] = grad[:, pl.ds(first, share_rows), :]
    for layer in range(layers):
        for part in range(2):
            pltpu.make_async_copy(terms.at[layer, part], pieces[0], stored.at[2 * layer + part]).wait()


SMEM_SPEC = pl.BlockSpec(memory_space=pltpu.SMEM)
VMEM_SPEC = pl.BlockSpec(memory_space=pltpu.VMEM)
HBM_SPEC = pl.BlockSpec(memory_space=pltpu.HBM)


def gate_kernel(*refs):
    pass


def gate(passed, waits):
    total = len(passed)
    if not total or not waits:
        return passed
    return run_kernel(
        gate_kernel,
        "gate",
        tuple(shape(*x.shape) for x in passed),
        [HBM_SPEC] * (total + len(waits)),
        (HBM_SPEC,) * total,
        [],
        0.1,
        aliases={i: i for i in range(total)},
    )(*passed, *waits)


def run_kernel(kernel, name, out_shapes, in_specs, out_specs, scratch, micros, mebibytes=16, aliases={}):
    return pl.pallas_call(
        kernel,
        name=name,
        out_shape=out_shapes,
        in_specs=in_specs,
        out_specs=out_specs,
        scratch_shapes=scratch,
        input_output_aliases=aliases,
        compiler_params=pltpu.CompilerParams(vmem_limit_bytes=mebibytes * 2**20),
        cost_estimate=pl.CostEstimate(
            flops=int(micros * 1e6), bytes_accessed=int(micros * 1e3), transcendentals=0
        ),
    )


def shape(*dims):
    return jax.ShapeDtypeStruct(dims, F32)


def swap(x, axis, offset):
    peers = lax.axis_size(axis)
    return lax.ppermute(x, axis, [(i, i ^ offset) for i in range(peers)])


def exchanged(mine, waits=()):
    got = [mine[0], swap(mine[1], "depth", 1)]
    for i, pair in enumerate(mine[2:]):
        across = swap(pair, "depth", 2 * (i + 1))
        (across,) = gate([across], waits)
        got += [across, swap(across[1], "depth", 1)]
    return got


def echo(x):
    return swap(x[:8, :LANES], "depth", 1)


def shift(x, axis, by):
    peers = lax.axis_size(axis)
    return lax.ppermute(x, axis, [(i, i + by) for i in range(peers) if 0 <= i + by < peers])


def body(transmission, probe_field, scan_positions, amplitudes):
    size = probe_field.shape[-1]
    per_device, _, rows, cols = transmission.shape
    peers = lax.axis_size("depth")
    tiles = lax.axis_size("tile")
    ids = jnp.stack([lax.axis_index("depth"), lax.axis_index("tile")]).astype(jnp.int32)
    left, right, tilt = (jnp.asarray(x) for x in optics_tables(size))

    probe, amplitude = run_kernel(
        prep_kernel,
        "prep",
        (shape(2, size, size), shape(size, size)),
        [SMEM_SPEC, VMEM_SPEC, VMEM_SPEC],
        [VMEM_SPEC, VMEM_SPEC],
        [],
        2,
    )(ids, probe_field, amplitudes)

    chunks = [(j, part) for j in range(per_device) for part in range(2)]
    ahead = 2
    strips = [transmission[c[0], c[1]] for c in chunks]
    group = (shape(size, size),) * 2 + (shape(2, size, size),) * (peers // 2 - 1)
    groups = len(group)
    crops = []
    for k, c in enumerate(chunks):
        rim = shift(strips[k], "tile", -1)
        waits = crops[k - ahead][2::2] if k >= ahead else [probe, amplitude]
        mine = run_kernel(
            functools.partial(crop_kernel, peers, c, len(waits)),
            "crop",
            group,
            [SMEM_SPEC, SMEM_SPEC] + [HBM_SPEC] * (2 + len(waits)),
            (HBM_SPEC,) * groups,
            [
                pltpu.VMEM((cols // LANES + 1, 2 * rows, LANES), F32),
                pltpu.VMEM((peers, size, size), F32),
                pltpu.SemaphoreType.DMA((2 * cols // LANES,)),
                pltpu.SemaphoreType.DMA((peers,)),
            ],
            2,
        )(ids, scan_positions, transmission, rim, *waits)
        strips[k + ahead : k + ahead + 1] = gate(strips[k + ahead : k + ahead + 1], mine[:1])
        crops.append(exchanged(mine))
    layers = per_device * peers
    result = run_kernel(
        functools.partial(optics_kernel, peers, per_device),
        "optics",
        group * len(chunks) + (shape(peers // 2, 2, size // peers, size),) * 2,
        [SMEM_SPEC] + [VMEM_SPEC] * 5 + [HBM_SPEC] * (len(chunks) * peers),
        (HBM_SPEC,) * (len(chunks) * groups) + (VMEM_SPEC,) * 2,
        [
            pltpu.VMEM((layers, 2, size, size), F32),
            pltpu.VMEM((layers, 2, size, size), F32),
            pltpu.VMEM((layers, 2, size, size), F32),
            pltpu.VMEM((2, size, size), F32),
            pltpu.SemaphoreType.DMA((2 * layers,)),
            pltpu.SemaphoreType.DMA((2 * layers,)),
        ],
        15,
        32,
    )(ids, probe, amplitude, left, right, tilt, *[x for got in crops for x in got])

    kept, handed = result[-2:]
    probe_halves = kept + swap(handed, "depth", 1)
    probe_grad = probe_halves
    step = 2
    while step < peers:
        probe_grad = probe_grad[:1] + swap(probe_grad[1:], "depth", step)
        step *= 2
    probe_steps = [probe_grad[0]]
    step = 1
    while step < tiles:
        probe_steps.append(probe_steps[-1] + swap(probe_steps[-1], "tile", step))
        step *= 2

    own, rim_back, returned = {}, {}, []
    order = list(reversed(chunks))
    for k, c in enumerate(order):
        at = chunks.index(c) * groups
        mine = result[at : at + groups]
        if k == 0:
            mine = gate(mine, probe_steps[:1])
        if k >= ahead:
            mine = gate(mine, returned[k - ahead][2::2] + [own[order[k - ahead]]])
        returned.append(exchanged(mine, [own[order[k - 1]]] if k else []))
        waits = [] if k else probe_steps[-1:]
        own[c], outside = run_kernel(
            functools.partial(place_kernel, peers, len(waits)),
            "place",
            (shape(rows, cols), shape(rows, cols)),
            [SMEM_SPEC, SMEM_SPEC] + [HBM_SPEC] * (peers + len(waits)),
            (HBM_SPEC, HBM_SPEC),
            [
                pltpu.VMEM((cols // LANES + 1, 2 * rows, LANES), F32),
                pltpu.VMEM((peers, size, size), F32),
                pltpu.SemaphoreType.DMA((peers,)),
                pltpu.SemaphoreType.DMA((2 * cols // LANES,)),
            ],
            2,
        )(ids, scan_positions, *returned[k], *waits)
        if k >= ahead:
            (outside,) = gate([outside], [echo(rim_back[order[k - ahead]])])
        rim_back[c] = shift(outside, "tile", 1)

    rim_back[order[-2]] = gate([rim_back[order[-2]]], [echo(rim_back[order[-2]])])[0]
    object_grad = jnp.stack(
        [
            jnp.stack([own[(j, part)] + rim_back[(j, part)] for part in range(2)])
            for j in range(per_device)
        ]
    )
    return (object_grad, probe_steps[-1])


def solution(mesh):
    placed = (P("depth", None, "tile", None), P(), P("tile", None), P("tile", None, None))
    return jax.shard_map(
        body,
        mesh=mesh,
        in_specs=placed,
        out_specs=(P("depth", None, "tile", None), P(None, "depth", None)),
        check_vma=False,
    )
```

time: 214 us -> 181 us (0.85)
  waiting for transfers between devices: 120 us -> 81.6 us
  Pallas kernels: 39.4 us -> 51.7 us
  starting transfers between devices: 44.3 us -> 38.6 us
    ppermute x30 -> x32, waiting for transfers between devices: 88 us -> 43.9 us  [swap(): return lax.ppermute(x, axis, [(i, i ^ offset) for i in range(peers)])]
    pallas_call x8 -> x19, Pallas kernels: 18 us -> 33.2 us  [the longest x4 17.6 us: body(): run_kernel(functools.partial(crop_kernel, peers, c, len(waits)), 'crop',...]
    ppermute x8, waiting for transfers between devices: 32.2 us -> 37.7 us  [shift(): lax.ppermute(x, axis, [(i, i + by) for i in range(peers) if 0 <= i + by <...]
    ppermute x8, starting transfers between devices: 21.4 us -> 17.6 us  [shift(): lax.ppermute(x, axis, [(i, i + by) for i in range(peers) if 0 <= i + by <...]
    squeeze x0 -> x9, local copies, waits for them, and re-layouts: none -> 2.97 us  [the longest x1 2.82 us: body(): strips = [transmission[c[0], c[1]] for c in chunks]]
    pallas_call x1, Pallas kernels: 19.8 us -> 16.8 us  [body(): run_kernel(functools.partial(optics_kernel, peers, per_device), 'optics',...]
    ppermute x30 -> x32, starting transfers between devices: 22.9 us -> 21.1 us  [swap(): return lax.ppermute(x, axis, [(i, i ^ offset) for i in range(peers)])]
  transfers between devices with their start and end apart: 38 -> 40, of which waited for: 19 -> 22; matrix products, arithmetic and copies ran while one was open for 1% -> 0% of each run, Pallas kernels for 9% -> 19%
where the time goes in v1:
time: 181 us
  waiting for transfers between devices  81.6 us (45%)
  Pallas kernels  51.7 us (29%)
  starting transfers between devices  38.6 us (21%)
  local copies, waits for them, and re-layouts  5.37 us (3%)
  other arithmetic  2.13 us (1%)
    ppermute x32, waiting for transfers between devices, swap(): return lax.ppermute(x, axis, [(i, i ^ offset) for i in range(peers)])  43.9 us
    ppermute x8, waiting for transfers between devices, shift(): lax.ppermute(x, axis, [(i, i + by) for i in range(peers) if 0 <= i + by <...  37.7 us
    ppermute x32, starting transfers between devices, swap(): return lax.ppermute(x, axis, [(i, i ^ offset) for i in range(peers)])  21.1 us
    pallas_call x4, Pallas kernels, body(): run_kernel(functools.partial(crop_kernel, peers, c, len(waits)), 'crop',...  17.6 us
    ppermute x8, starting transfers between devices, shift(): lax.ppermute(x, axis, [(i, i + by) for i in range(peers) if 0 <= i + by <...  17.6 us
    pallas_call x1, Pallas kernels, body(): run_kernel(functools.partial(optics_kernel, peers, per_device), 'optics',...  16.8 us
    pallas_call x4, Pallas kernels, body(): run_kernel(functools.partial(place_kernel, peers, len(waits)), 'place', (...  15.6 us
  transfers between devices with their start and end apart: 40, of which 22 were waited for; matrix products, arithmetic and copies ran while one was open for 0% of the time, Pallas kernels for 19%

profile of v1, /device:TPU:4, one launch (start us, length us, event | category | flops | bytes accessed | tf_op | source)
XLA Modules:
  0.0 180.5 jit_solution(2871918709118775825)
XLA Ops:
  0.6 2.8 %slice_bitcast_fusion = (f32[256,512]{1,0:T(8,128)S(1)}, f32[256,512]{1,0:T(8,128)S(1)}, f32[256,512]{1,0:T(8,128)}, f32[256,512]{1,0:T(8,128)}) fusion(f32[2,2,256,512]{3,2,1,0:T(8,128)} %strips.7), kind=kLoop, calls=%fused_computation.7 | loop fusion | bytes 4194304 | tf_op jit(solution)/shard_map/squeeze | solution.py:425
  11.4 10.0 %collective-permute-done.4.rim = f32[256,512]{1,0:T(8,128)} collective-permute-done((f32[256,512]{1,0:T(8,128)}, f32[256,512]{1,0:T(8,128)}, u32[]{:S(2)}, u32[]{:S(2)}) %collective-permute-start.4) | collective-permute-done | bytes 524320 | tf_op jit(solution)/shard_map/ppermute | solution.py:402
  21.4 4.9 %crop.5 = (f32[256,256]{1,0:T(8,128)S(1)}, f32[256,256]{1,0:T(8,128)S(1)}, f32[2,256,256]{2,1,0:T(8,128)S(1)}) custom-call(s32[2]{0:T(128)S(1)} %pad_add_fusion.ids, s32[4,2]{1,0:T(4,128)S(1)} %copy.33.positions, f32[2,2,256,512]{3,2,1,0:T(8,128)S(1)} %copy-done, f32[256,512]{1,0:T(8,128)} %collective-permute-done.4.rim, ...), custom_call_target="tpu_custom_call" | custom-call | flops 2000000 | bytes 2000 | tf_op jit(solution)/shard_map/crop/pallas_call | solution.py:432
  29.7 2.3 %collective-permute-done.rim = f32[256,512]{1,0:T(8,128)} collective-permute-done((f32[256,512]{1,0:T(8,128)}, f32[256,512]{1,0:T(8,128)}, u32[]{:S(2)}, u32[]{:S(2)}) %collective-permute-start) | collective-permute-done | bytes 524320 | tf_op jit(solution)/shard_map/ppermute | solution.py:402
  32.0 4.9 %crop.4 = (f32[256,256]{1,0:T(8,128)S(1)}, f32[256,256]{1,0:T(8,128)S(1)}, f32[2,256,256]{2,1,0:T(8,128)S(1)}) custom-call(s32[2]{0:T(128)S(1)} %pad_add_fusion.ids, s32[4,2]{1,0:T(4,128)S(1)} %copy.33.positions, f32[2,2,256,512]{3,2,1,0:T(8,128)S(1)} %copy-done, f32[256,512]{1,0:T(8,128)} %collective-permute-done.rim, ...), custom_call_target="tpu_custom_call" | custom-call | flops 2000000 | bytes 2000 | tf_op jit(solution)/shard_map/crop/pallas_call | solution.py:432
  36.9 2.2 %collective-permute-start.2 = (f32[2,256,256]{2,1,0:T(8,128)S(1)}, f32[2,256,256]{2,1,0:T(8,128)S(1)}, u32[]{:S(2)}, u32[]{:S(2)}) collective-permute-start(f32[2,256,256]{2,1,0:T(8,128)S(1)} %get-tuple-element.51), channel_id=1, source_target_pairs={{0,16},{8,24},{16,0},{24,8},{1,17},{9,25},{17,1},{25,9},{2,18},{10... | collective-permute-start | bytes 1572872 | tf_op jit(solution)/shard_map/ppermute | solution.py:384
  39.1 2.1 %collective-permute-start.8 = (f32[256,512]{1,0:T(8,128)S(1)}, f32[256,512]{1,0:T(8,128)S(1)}, u32[]{:S(2)}, u32[]{:S(2)}) collective-permute-start(f32[256,512]{1,0:T(8,128)S(1)} %gate.11), channel_id=1, source_target_pairs={{1,0},{2,1},{3,2},{4,3},{5,4},{6,5},{7,6},{9,8},{10,9},{11,10},{12... | collective-permute-start | bytes 1572872 | tf_op jit(solution)/shard_map/ppermute | solution.py:402
  41.2 2.0 %collective-permute-done.12.rim = f32[256,512]{1,0:T(8,128)S(1)} collective-permute-done((f32[256,512]{1,0:T(8,128)S(1)}, f32[256,512]{1,0:T(8,128)S(1)}, u32[]{:S(2)}, u32[]{:S(2)}) %collective-permute-start.12) | collective-permute-done | bytes 524320 | tf_op jit(solution)/shard_map/ppermute | solution.py:402
  43.2 3.9 %crop.7 = (f32[256,256]{1,0:T(8,128)S(1)}, f32[256,256]{1,0:T(8,128)S(1)}, f32[2,256,256]{2,1,0:T(8,128)S(1)}) custom-call(s32[2]{0:T(128)S(1)} %pad_add_fusion.ids, s32[4,2]{1,0:T(4,128)S(1)} %copy.33.positions, f32[2,2,256,512]{3,2,1,0:T(8,128)S(1)} %copy-done, f32[256,512]{1,0:T(8,128)S(1)} %collective-permute-done.12.rim, ...), custom_call_target="tpu_custom_call" | custom-call | flops 2000000 | bytes 2000 | tf_op jit(solution)/shard_map/crop/pallas_call | solution.py:432
  47.1 2.5 %collective-permute-start.14 = (f32[2,256,256]{2,1,0:T(8,128)S(1)}, f32[2,256,256]{2,1,0:T(8,128)S(1)}, u32[]{:S(2)}, u32[]{:S(2)}) collective-permute-start(f32[2,256,256]{2,1,0:T(8,128)S(1)} %get-tuple-element.60), channel_id=1, source_target_pairs={{0,16},{8,24},{16,0},{24,8},{1,17},{9,25},{17,1},{25,9},{2,18},{10... | collective-permute-start | bytes 1572872 | tf_op jit(solution)/shard_map/ppermute | solution.py:384
  51.2 2.6 %collective-permute-done.8.rim = f32[256,512]{1,0:T(8,128)S(1)} collective-permute-done((f32[256,512]{1,0:T(8,128)S(1)}, f32[256,512]{1,0:T(8,128)S(1)}, u32[]{:S(2)}, u32[]{:S(2)}) %collective-permute-start.8) | collective-permute-done | bytes 524320 | tf_op jit(solution)/shard_map/ppermute | solution.py:402
  53.8 3.9 %crop.6 = (f32[256,256]{1,0:T(8,128)S(1)}, f32[256,256]{1,0:T(8,128)S(1)}, f32[2,256,256]{2,1,0:T(8,128)S(1)}) custom-call(s32[2]{0:T(128)S(1)} %pad_add_fusion.ids, s32[4,2]{1,0:T(4,128)S(1)} %copy.33.positions, f32[2,2,256,512]{3,2,1,0:T(8,128)S(1)} %copy-done, f32[256,512]{1,0:T(8,128)S(1)} %collective-permute-done.8.rim, ...), custom_call_target="tpu_custom_call" | custom-call | flops 2000000 | bytes 2000 | tf_op jit(solution)/shard_map/crop/pallas_call | solution.py:432
  59.5 2.6 %collective-permute-done.14.rest_14_ = f32[2,256,256]{2,1,0:T(8,128)S(1)} collective-permute-done((f32[2,256,256]{2,1,0:T(8,128)S(1)}, f32[2,256,256]{2,1,0:T(8,128)S(1)}, u32[]{:S(2)}, u32[]{:S(2)}) %collective-permute-start.14) | collective-permute-done | bytes 524320 | tf_op jit(solution)/shard_map/ppermute | solution.py:384
  62.1 9.6 %collective-permute-done.10.rest_10_ = f32[2,256,256]{2,1,0:T(8,128)S(1)} collective-permute-done((f32[2,256,256]{2,1,0:T(8,128)S(1)}, f32[2,256,256]{2,1,0:T(8,128)S(1)}, u32[]{:S(2)}, u32[]{:S(2)}) %collective-permute-start.10) | collective-permute-done | bytes 524320 | tf_op jit(solution)/shard_map/ppermute | solution.py:384
  74.4 16.8 %optics.1 = (f32[256,256]{1,0:T(8,128)S(1)}, f32[256,256]{1,0:T(8,128)S(1)}, f32[2,256,256]{2,1,0:T(8,128)S(1)}, f32[256,256]{1,0:T(8,128)S(1)}, f32[256,256]{1,...) custom-call(s32[2]{0:T(128)S(1)} %pad_add_fusion.ids, ...), custom_call_target="tpu_custom_call" | custom-call | flops 15000000 | bytes 15000 | tf_op jit(solution)/shard_map/optics/pallas_call | solution.py:449
  94.4 4.1 %collective-permute-done.18 = f32[1,2,64,256]{3,2,1,0:T(8,128)S(1)} collective-permute-done((f32[1,2,64,256]{3,2,1,0:T(8,128)S(1)}, f32[1,2,64,256]{3,2,1,0:T(8,128)S(1)}, u32[]{:S(2)}, u32[]{:S(2)}) %collective-permute-start.18) | collective-permute-done | bytes 131104 | tf_op jit(solution)/shard_map/ppermute | solution.py:384
  100.7 4.4 %collective-permute-done.22 = f32[2,64,256]{2,1,0:T(8,128)S(1)} collective-permute-done((f32[2,64,256]{2,1,0:T(8,128)S(1)}, f32[2,64,256]{2,1,0:T(8,128)S(1)}, u32[]{:S(2)}, u32[]{:S(2)}) %collective-permute-start.22) | collective-permute-done | bytes 131104 | tf_op jit(solution)/shard_map/ppermute | solution.py:384
  106.8 6.7 %collective-permute-done.20.rest_2_.refs_3_ = f32[2,256,256]{2,1,0:T(8,128)S(1)} collective-permute-done((f32[2,256,256]{2,1,0:T(8,128)S(1)}, f32[2,256,256]{2,1,0:T(8,128)S(1)}, u32[]{:S(2)}, u32[]{:S(2)}) %collective-permute-start.20) | collective-permute-done | bytes 524320 | tf_op jit(solution)/shard_map/ppermute | solution.py:384
  113.7 2.6 %collective-permute-start.24 = (f32[2,64,256]{2,1,0:T(8,128)S(1)}, f32[2,64,256]{2,1,0:T(8,128)S(1)}, u32[]{:S(2)}, u32[]{:S(2)}) collective-permute-start(f32[2,64,256]{2,1,0:T(8,128)S(1)} %add.30), channel_id=1, source_target_pairs={{0,4},{1,5},{2,6},{3,7},{4,0},{5,1},{6,2},{7,3},{8,12},{9,13},{10,... | collective-permute-start | bytes 393224 | tf_op jit(solution)/shard_map/ppermute | solution.py:384
  116.5 6.8 %collective-permute-done.24 = f32[2,64,256]{2,1,0:T(8,128)S(1)} collective-permute-done((f32[2,64,256]{2,1,0:T(8,128)S(1)}, f32[2,64,256]{2,1,0:T(8,128)S(1)}, u32[]{:S(2)}, u32[]{:S(2)}) %collective-permute-start.24) | collective-permute-done | bytes 131104 | tf_op jit(solution)/shard_map/ppermute | solution.py:384
  123.4 3.9 %place.4 = (f32[256,512]{1,0:T(8,128)S(1)}, f32[256,512]{1,0:T(8,128)S(1)}) custom-call(s32[2]{0:T(128)S(1)} %pad_add_fusion.ids, s32[4,2]{1,0:T(4,128)S(1)} %copy.33.positions, f32[256,256]{1,0:T(8,128)S(1)} %get-tuple-element.70.rest_0_, f32[256,256]{1,0:T(8,128)S(1)} %collective-permute-done.19.rest_1_, ...), custom_call_target="tpu_custom_call" | custom-call | flops 2000000 | bytes 2000 | tf_op jit(solution)/shard_map/place/pallas_call | solution.py:491
  130.9 3.9 %place.5 = (f32[256,512]{1,0:T(8,128)S(1)}, f32[256,512]{1,0:T(8,128)S(1)}) custom-call(s32[2]{0:T(128)S(1)} %pad_add_fusion.ids, s32[4,2]{1,0:T(4,128)S(1)} %copy.33.positions, f32[256,256]{1,0:T(8,128)S(1)} %get-tuple-element.74.rest_0_, f32[256,256]{1,0:T(8,128)S(1)} %collective-permute-done.25.rest_1_, f32[2,256,256]{2,1,0:T(8,128)S(1)} %gate.14.rest_2_.refs_3_, ...), custom_call_target="tpu_custom_call" | custom-call | flops 2000000 | bytes 2000 | tf_op jit(solution)/shard_map/place/pallas_call | solution.py:491
  135.7 2.0 %collective-permute-start.33 = (f32[256,512]{1,0:T(8,128)S(1)}, f32[256,512]{1,0:T(8,128)S(1)}, u32[]{:S(2)}, u32[]{:S(2)}) collective-permute-start(f32[256,512]{1,0:T(8,128)S(1)} %get-tuple-element.89), channel_id=1, source_target_pairs={{0,1},{1,2},{2,3},{3,4},{4,5},{5,6},{6,7},{8,9},{9,10},{10,11},{11... | collective-permute-start | bytes 1572872 | tf_op jit(solution)/shard_map/ppermute | solution.py:402
  137.7 4.5 %collective-permute-done.30.refs_0_ = f32[2,256,256]{2,1,0:T(8,128)S(1)} collective-permute-done((f32[2,256,256]{2,1,0:T(8,128)S(1)}, f32[2,256,256]{2,1,0:T(8,128)S(1)}, u32[]{:S(2)}, u32[]{:S(2)}) %collective-permute-start.30) | collective-permute-done | bytes 524320 | tf_op jit(solution)/shard_map/ppermute | solution.py:384
  142.3 3.3 %collective-permute-done.36 = f32[256,512]{1,0:T(8,128)S(1)} collective-permute-done((f32[256,512]{1,0:T(8,128)S(1)}, f32[256,512]{1,0:T(8,128)S(1)}, u32[]{:S(2)}, u32[]{:S(2)}) %collective-permute-start.36) | collective-permute-done | bytes 524320 | tf_op jit(solution)/shard_map/ppermute | solution.py:402
  146.1 3.9 %place.6 = (f32[256,512]{1,0:T(8,128)S(1)}, f32[256,512]{1,0:T(8,128)S(1)}) custom-call(s32[2]{0:T(128)S(1)} %pad_add_fusion.ids, s32[4,2]{1,0:T(4,128)S(1)} %copy.33.positions, f32[256,256]{1,0:T(8,128)S(1)} %get-tuple-element.83.rest_0_, f32[256,256]{1,0:T(8,128)S(1)} %collective-permute-done.29.rest_1_, f32[2,256,256]{2,1,0:T(8,128)S(1)} %gate.17.rest_2_, ...), custom_call_target="tpu_custom_call" | custom-call | flops 2000000 | bytes 2000 | tf_op jit(solution)/shard_map/place/pallas_call | solution.py:491
  150.0 2.9 %collective-permute-start.38 = (f32[256,512]{1,0:T(8,128)S(1)}, f32[256,512]{1,0:T(8,128)S(1)}, u32[]{:S(2)}, u32[]{:S(2)}) collective-permute-start(f32[256,512]{1,0:T(8,128)S(1)} %gate.20), channel_id=1, source_target_pairs={{0,1},{1,2},{2,3},{3,4},{4,5},{5,6},{6,7},{8,9},{9,10},{10,11},{11... | collective-permute-start | bytes 1572872 | tf_op jit(solution)/shard_map/ppermute | solution.py:402
  153.1 3.8 %collective-permute-done.33 = f32[256,512]{1,0:T(8,128)S(1)} collective-permute-done((f32[256,512]{1,0:T(8,128)S(1)}, f32[256,512]{1,0:T(8,128)S(1)}, u32[]{:S(2)}, u32[]{:S(2)}) %collective-permute-start.33) | collective-permute-done | bytes 524320 | tf_op jit(solution)/shard_map/ppermute | solution.py:402
  156.9 3.9 %place.7 = (f32[256,512]{1,0:T(8,128)S(1)}, f32[256,512]{1,0:T(8,128)S(1)}) custom-call(s32[2]{0:T(128)S(1)} %pad_add_fusion.ids, s32[4,2]{1,0:T(4,128)S(1)} %copy.33.positions, f32[256,256]{1,0:T(8,128)S(1)} %get-tuple-element.77.rest_0_, f32[256,256]{1,0:T(8,128)S(1)} %collective-permute-done.27.rest_1_, f32[2,256,256]{2,1,0:T(8,128)S(1)} %gate.18.rest_2_, ...), custom_call_target="tpu_custom_call" | custom-call | flops 2000000 | bytes 2000 | tf_op jit(solution)/shard_map/place/pallas_call | solution.py:491
  160.9 2.9 %collective-permute-start.35 = (f32[256,512]{1,0:T(8,128)S(1)}, f32[256,512]{1,0:T(8,128)S(1)}, u32[]{:S(2)}, u32[]{:S(2)}) collective-permute-start(f32[256,512]{1,0:T(8,128)S(1)} %gate.19), channel_id=1, source_target_pairs={{0,1},{1,2},{2,3},{3,4},{4,5},{5,6},{6,7},{8,9},{9,10},{10,11},{11... | collective-permute-start | bytes 1572872 | tf_op jit(solution)/shard_map/ppermute | solution.py:402
  163.8 4.2 %collective-permute-done.38.refs_0_ = f32[256,512]{1,0:T(8,128)S(1)} collective-permute-done((f32[256,512]{1,0:T(8,128)S(1)}, f32[256,512]{1,0:T(8,128)S(1)}, u32[]{:S(2)}, u32[]{:S(2)}) %collective-permute-start.38) | collective-permute-done | bytes 524320 | tf_op jit(solution)/shard_map/ppermute | solution.py:402
  169.3 9.6 %collective-permute-done.35 = f32[256,512]{1,0:T(8,128)S(1)} collective-permute-done((f32[256,512]{1,0:T(8,128)S(1)}, f32[256,512]{1,0:T(8,128)S(1)}, u32[]{:S(2)}, u32[]{:S(2)}) %collective-permute-start.35) | collective-permute-done | bytes 524320 | tf_op jit(solution)/shard_map/ppermute | solution.py:402
  (112 shorter events, 32.8 us)
Async XLA Ops:
  3.5 17.9 %collective-permute-start.4 = (f32[256,512]{1,0:T(8,128)}, f32[256,512]{1,0:T(8,128)}, u32[]{:S(2)}, u32[]{:S(2)}) collective-permute-start(f32[256,512]{1,0:T(8,128)} %get-tuple-element.94), channel_id=1, source_target_pairs={{1,0},{2,1},{3,2},{4,3},{5,4},{6,5},{7,6},{9,8},{10,9},{11,10},{12... | collective-permute-start | bytes 1572872 | tf_op jit(solution)/shard_map/ppermute | solution.py:402
  5.4 26.6 %collective-permute-start = (f32[256,512]{1,0:T(8,128)}, f32[256,512]{1,0:T(8,128)}, u32[]{:S(2)}, u32[]{:S(2)}) collective-permute-start(f32[256,512]{1,0:T(8,128)} %get-tuple-element.95), channel_id=1, source_target_pairs={{1,0},{2,1},{3,2},{4,3},{5,4},{6,5},{7,6},{9,8},{10,9},{11,10},{12... | collective-permute-start | bytes 1572872 | tf_op jit(solution)/shard_map/ppermute | solution.py:402
  26.3 14.9 %collective-permute-start.6 = (f32[2,256,256]{2,1,0:T(8,128)S(1)}, f32[2,256,256]{2,1,0:T(8,128)S(1)}, u32[]{:S(2)}, u32[]{:S(2)}) collective-permute-start(f32[2,256,256]{2,1,0:T(8,128)S(1)} %get-tuple-element.54), channel_id=1, source_target_pairs={{0,16},{8,24},{16,0},{24,8},{1,17},{9,25},{17,1},{25,9},{2,18},{10... | collective-permute-start | bytes 1572872 | tf_op jit(solution)/shard_map/ppermute | solution.py:384
  27.8 15.3 %collective-permute-start.12 = (f32[256,512]{1,0:T(8,128)S(1)}, f32[256,512]{1,0:T(8,128)S(1)}, u32[]{:S(2)}, u32[]{:S(2)}) collective-permute-start(f32[256,512]{1,0:T(8,128)S(1)} %gate.12), channel_id=1, source_target_pairs={{1,0},{2,1},{3,2},{4,3},{5,4},{6,5},{7,6},{9,8},{10,9},{11,10},{12... | collective-permute-start | bytes 1572872 | tf_op jit(solution)/shard_map/ppermute | solution.py:402
  36.9 14.3 %collective-permute-start.2 = (f32[2,256,256]{2,1,0:T(8,128)S(1)}, f32[2,256,256]{2,1,0:T(8,128)S(1)}, u32[]{:S(2)}, u32[]{:S(2)}) collective-permute-start(f32[2,256,256]{2,1,0:T(8,128)S(1)} %get-tuple-element.51), channel_id=1, source_target_pairs={{0,16},{8,24},{16,0},{24,8},{1,17},{9,25},{17,1},{25,9},{2,18},{10... | collective-permute-start | bytes 1572872 | tf_op jit(solution)/shard_map/ppermute | solution.py:384
  39.1 14.8 %collective-permute-start.8 = (f32[256,512]{1,0:T(8,128)S(1)}, f32[256,512]{1,0:T(8,128)S(1)}, u32[]{:S(2)}, u32[]{:S(2)}) collective-permute-start(f32[256,512]{1,0:T(8,128)S(1)} %gate.11), channel_id=1, source_target_pairs={{1,0},{2,1},{3,2},{4,3},{5,4},{6,5},{7,6},{9,8},{10,9},{11,10},{12... | collective-permute-start | bytes 1572872 | tf_op jit(solution)/shard_map/ppermute | solution.py:402
  47.1 15.0 %collective-permute-start.14 = (f32[2,256,256]{2,1,0:T(8,128)S(1)}, f32[2,256,256]{2,1,0:T(8,128)S(1)}, u32[]{:S(2)}, u32[]{:S(2)}) collective-permute-start(f32[2,256,256]{2,1,0:T(8,128)S(1)} %get-tuple-element.60), channel_id=1, source_target_pairs={{0,16},{8,24},{16,0},{24,8},{1,17},{9,25},{17,1},{25,9},{2,18},{10... | collective-permute-start | bytes 1572872 | tf_op jit(solution)/shard_map/ppermute | solution.py:384
  49.6 22.1 %collective-permute-start.5 = (f32[256,256]{1,0:T(8,128)S(1)}, f32[256,256]{1,0:T(8,128)S(1)}, u32[]{:S(2)}, u32[]{:S(2)}) collective-permute-start(f32[256,256]{1,0:T(8,128)S(1)} %get-tuple-element.53), channel_id=1, source_target_pairs={{0,8},{8,0},{16,24},{24,16},{1,9},{9,1},{17,25},{25,17},{2,10},{10... | collective-permute-start | bytes 786440 | tf_op jit(solution)/shard_map/ppermute | solution.py:384
  49.6 22.7 %collective-permute-start.1 = (f32[256,256]{1,0:T(8,128)S(1)}, f32[256,256]{1,0:T(8,128)S(1)}, u32[]{:S(2)}, u32[]{:S(2)}) collective-permute-start(f32[256,256]{1,0:T(8,128)S(1)} %get-tuple-element.50), channel_id=1, source_target_pairs={{0,8},{8,0},{16,24},{24,16},{1,9},{9,1},{17,25},{25,17},{2,10},{10... | collective-permute-start | bytes 786440 | tf_op jit(solution)/shard_map/ppermute | solution.py:384
  57.8 13.9 %collective-permute-start.10 = (f32[2,256,256]{2,1,0:T(8,128)S(1)}, f32[2,256,256]{2,1,0:T(8,128)S(1)}, u32[]{:S(2)}, u32[]{:S(2)}) collective-permute-start(f32[2,256,256]{2,1,0:T(8,128)S(1)} %get-tuple-element.57), channel_id=1, source_target_pairs={{0,16},{8,24},{16,0},{24,8},{1,17},{9,25},{17,1},{25,9},{2,18},{10... | collective-permute-start | bytes 1572872 | tf_op jit(solution)/shard_map/ppermute | solution.py:384
  59.4 13.0 %collective-permute-start.7 = (f32[256,256]{1,0:T(8,128)S(1)}, f32[256,256]{1,0:T(8,128)S(1)}, u32[]{:S(2)}, u32[]{:S(2)}) collective-permute-start(f32[256,256]{1,0:T(8,128)S(1)} %slice_bitcast_fusion.10), channel_id=1, source_target_pairs={{0,8},{8,0},{16,24},{24,16},{1,9},{9,1},{17,25},{25,17},{2,10},{10... | collective-permute-start | bytes 786440 | tf_op jit(solution)/shard_map/ppermute | solution.py:384
  62.1 10.8 %collective-permute-start.13 = (f32[256,256]{1,0:T(8,128)S(1)}, f32[256,256]{1,0:T(8,128)S(1)}, u32[]{:S(2)}, u32[]{:S(2)}) collective-permute-start(f32[256,256]{1,0:T(8,128)S(1)} %get-tuple-element.59), channel_id=1, source_target_pairs={{0,8},{8,0},{16,24},{24,16},{1,9},{9,1},{17,25},{25,17},{2,10},{10... | collective-permute-start | bytes 786440 | tf_op jit(solution)/shard_map/ppermute | solution.py:384
  92.9 5.7 %collective-permute-start.18 = (f32[1,2,64,256]{3,2,1,0:T(8,128)S(1)}, f32[1,2,64,256]{3,2,1,0:T(8,128)S(1)}, u32[]{:S(2)}, u32[]{:S(2)}) collective-permute-start(f32[1,2,64,256]{3,2,1,0:T(8,128)S(1)} %slice.73), channel_id=1, source_target_pairs={{0,16},{8,24},{16,0},{24,8},{1,17},{9,25},{17,1},{25,9},{2,18},{10... | collective-permute-start | bytes 393224 | tf_op jit(solution)/shard_map/ppermute | solution.py:384
  98.6 14.9 %collective-permute-start.20 = (f32[2,256,256]{2,1,0:T(8,128)S(1)}, f32[2,256,256]{2,1,0:T(8,128)S(1)}, u32[]{:S(2)}, u32[]{:S(2)}) collective-permute-start(f32[2,256,256]{2,1,0:T(8,128)S(1)} %get-tuple-element.72), channel_id=1, source_target_pairs={{0,16},{8,24},{16,0},{24,8},{1,17},{9,25},{17,1},{25,9},{2,18},{10... | collective-permute-start | bytes 1572872 | tf_op jit(solution)/shard_map/ppermute | solution.py:384
  100.2 5.0 %collective-permute-start.22 = (f32[2,64,256]{2,1,0:T(8,128)S(1)}, f32[2,64,256]{2,1,0:T(8,128)S(1)}, u32[]{:S(2)}, u32[]{:S(2)}) collective-permute-start(f32[2,64,256]{2,1,0:T(8,128)S(1)} %fusion.refs_3_), channel_id=1, source_target_pairs={{0,1},{1,0},{2,3},{3,2},{4,5},{5,4},{6,7},{7,6},{8,9},{9,8},{10,11... | collective-permute-start | bytes 393224 | tf_op jit(solution)/shard_map/ppermute | solution.py:384
  100.2 28.7 %collective-permute-start.16 = (f32[2,256,256]{2,1,0:T(8,128)S(1)}, f32[2,256,256]{2,1,0:T(8,128)S(1)}, u32[]{:S(2)}, u32[]{:S(2)}) collective-permute-start(f32[2,256,256]{2,1,0:T(8,128)S(1)} %get-tuple-element.64), channel_id=1, source_target_pairs={{0,16},{8,24},{16,0},{24,8},{1,17},{9,25},{17,1},{25,9},{2,18},{10... | collective-permute-start | bytes 1572872 | tf_op jit(solution)/shard_map/ppermute | solution.py:384
  100.7 22.7 %collective-permute-start.19 = (f32[256,256]{1,0:T(8,128)S(1)}, f32[256,256]{1,0:T(8,128)S(1)}, u32[]{:S(2)}, u32[]{:S(2)}) collective-permute-start(f32[256,256]{1,0:T(8,128)S(1)} %get-tuple-element.71), channel_id=1, source_target_pairs={{0,8},{8,0},{16,24},{24,16},{1,9},{9,1},{17,25},{25,17},{2,10},{10... | collective-permute-start | bytes 786440 | tf_op jit(solution)/shard_map/ppermute | solution.py:384
  105.2 8.5 %collective-permute-start.23 = (f32[2,64,256]{2,1,0:T(8,128)S(1)}, f32[2,64,256]{2,1,0:T(8,128)S(1)}, u32[]{:S(2)}, u32[]{:S(2)}) collective-permute-start(f32[2,64,256]{2,1,0:T(8,128)S(1)} %add.29), channel_id=1, source_target_pairs={{0,2},{1,3},{2,0},{3,1},{4,6},{5,7},{6,4},{7,5},{8,10},{9,11},{10,... | collective-permute-start | bytes 393224 | tf_op jit(solution)/shard_map/ppermute | solution.py:384
  113.6 9.8 %collective-permute-start.21 = (f32[256,256]{1,0:T(8,128)S(1)}, f32[256,256]{1,0:T(8,128)S(1)}, u32[]{:S(2)}, u32[]{:S(2)}) collective-permute-start(f32[256,256]{1,0:T(8,128)S(1)} %slice_bitcast_fusion.7), channel_id=1, source_target_pairs={{0,8},{8,0},{16,24},{24,16},{1,9},{9,1},{17,25},{25,17},{2,10},{10... | collective-permute-start | bytes 786440 | tf_op jit(solution)/shard_map/ppermute | solution.py:384
  113.7 9.7 %collective-permute-start.24 = (f32[2,64,256]{2,1,0:T(8,128)S(1)}, f32[2,64,256]{2,1,0:T(8,128)S(1)}, u32[]{:S(2)}, u32[]{:S(2)}) collective-permute-start(f32[2,64,256]{2,1,0:T(8,128)S(1)} %add.30), channel_id=1, source_target_pairs={{0,4},{1,5},{2,6},{3,7},{4,0},{5,1},{6,2},{7,3},{8,12},{9,13},{10,... | collective-permute-start | bytes 393224 | tf_op jit(solution)/shard_map/ppermute | solution.py:384
  116.3 14.6 %collective-permute-start.25 = (f32[256,256]{1,0:T(8,128)S(1)}, f32[256,256]{1,0:T(8,128)S(1)}, u32[]{:S(2)}, u32[]{:S(2)}) collective-permute-start(f32[256,256]{1,0:T(8,128)S(1)} %get-tuple-element.75), channel_id=1, source_target_pairs={{0,8},{8,0},{16,24},{24,16},{1,9},{9,1},{17,25},{25,17},{2,10},{10... | collective-permute-start | bytes 786440 | tf_op jit(solution)/shard_map/ppermute | solution.py:384
  127.3 14.9 %collective-permute-start.30 = (f32[2,256,256]{2,1,0:T(8,128)S(1)}, f32[2,256,256]{2,1,0:T(8,128)S(1)}, u32[]{:S(2)}, u32[]{:S(2)}) collective-permute-start(f32[2,256,256]{2,1,0:T(8,128)S(1)} %get-tuple-element.85), channel_id=1, source_target_pairs={{0,16},{8,24},{16,0},{24,8},{1,17},{9,25},{17,1},{25,9},{2,18},{10... | collective-permute-start | bytes 1572872 | tf_op jit(solution)/shard_map/ppermute | solution.py:384
  129.0 16.6 %collective-permute-start.36 = (f32[256,512]{1,0:T(8,128)S(1)}, f32[256,512]{1,0:T(8,128)S(1)}, u32[]{:S(2)}, u32[]{:S(2)}) collective-permute-start(f32[256,512]{1,0:T(8,128)S(1)} %get-tuple-element.91), channel_id=1, source_target_pairs={{0,1},{1,2},{2,3},{3,4},{4,5},{5,6},{6,7},{8,9},{9,10},{10,11},{11... | collective-permute-start | bytes 1572872 | tf_op jit(solution)/shard_map/ppermute | solution.py:402
  134.8 18.1 %collective-permute-start.28 = (f32[2,256,256]{2,1,0:T(8,128)S(1)}, f32[2,256,256]{2,1,0:T(8,128)S(1)}, u32[]{:S(2)}, u32[]{:S(2)}) collective-permute-start(f32[2,256,256]{2,1,0:T(8,128)S(1)} %get-tuple-element.79), channel_id=1, source_target_pairs={{0,16},{8,24},{16,0},{24,8},{1,17},{9,25},{17,1},{25,9},{2,18},{10... | collective-permute-start | bytes 1572872 | tf_op jit(solution)/shard_map/ppermute | solution.py:384
  135.4 10.1 %collective-permute-start.29 = (f32[256,256]{1,0:T(8,128)S(1)}, f32[256,256]{1,0:T(8,128)S(1)}, u32[]{:S(2)}, u32[]{:S(2)}) collective-permute-start(f32[256,256]{1,0:T(8,128)S(1)} %get-tuple-element.84), channel_id=1, source_target_pairs={{0,8},{8,0},{16,24},{24,16},{1,9},{9,1},{17,25},{25,17},{2,10},{10... | collective-permute-start | bytes 786440 | tf_op jit(solution)/shard_map/ppermute | solution.py:384
  135.7 21.2 %collective-permute-start.33 = (f32[256,512]{1,0:T(8,128)S(1)}, f32[256,512]{1,0:T(8,128)S(1)}, u32[]{:S(2)}, u32[]{:S(2)}) collective-permute-start(f32[256,512]{1,0:T(8,128)S(1)} %get-tuple-element.89), channel_id=1, source_target_pairs={{0,1},{1,2},{2,3},{3,4},{4,5},{5,6},{6,7},{8,9},{9,10},{10,11},{11... | collective-permute-start | bytes 1572872 | tf_op jit(solution)/shard_map/ppermute | solution.py:402
  145.6 4.4 %collective-permute-start.37 = (f32[8,128]{1,0:T(8,128)S(1)}, f32[8,128]{1,0:T(8,128)S(1)}, u32[]{:S(2)}, u32[]{:S(2)}) collective-permute-start(f32[8,128]{1,0:T(8,128)S(1)} %slice.79), channel_id=1, source_target_pairs={{0,8},{8,0},{16,24},{24,16},{1,9},{9,1},{17,25},{25,17},{2,10},{10... | collective-permute-start | bytes 12296 | tf_op jit(solution)/shard_map/ppermute | solution.py:384
  145.6 11.3 %collective-permute-start.27 = (f32[256,256]{1,0:T(8,128)S(1)}, f32[256,256]{1,0:T(8,128)S(1)}, u32[]{:S(2)}, u32[]{:S(2)}) collective-permute-start(f32[256,256]{1,0:T(8,128)S(1)} %get-tuple-element.78), channel_id=1, source_target_pairs={{0,8},{8,0},{16,24},{24,16},{1,9},{9,1},{17,25},{25,17},{2,10},{10... | collective-permute-start | bytes 786440 | tf_op jit(solution)/shard_map/ppermute | solution.py:384
  150.0 18.0 %collective-permute-start.38 = (f32[256,512]{1,0:T(8,128)S(1)}, f32[256,512]{1,0:T(8,128)S(1)}, u32[]{:S(2)}, u32[]{:S(2)}) collective-permute-start(f32[256,512]{1,0:T(8,128)S(1)} %gate.20), channel_id=1, source_target_pairs={{0,1},{1,2},{2,3},{3,4},{4,5},{5,6},{6,7},{8,9},{9,10},{10,11},{11... | collective-permute-start | bytes 1572872 | tf_op jit(solution)/shard_map/ppermute | solution.py:402
  153.0 3.9 %collective-permute-start.32 = (f32[256,256]{1,0:T(8,128)S(1)}, f32[256,256]{1,0:T(8,128)S(1)}, u32[]{:S(2)}, u32[]{:S(2)}) collective-permute-start(f32[256,256]{1,0:T(8,128)S(1)} %slice_bitcast_fusion.4), channel_id=1, source_target_pairs={{0,8},{8,0},{16,24},{24,16},{1,9},{9,1},{17,25},{25,17},{2,10},{10... | collective-permute-start | bytes 786440 | tf_op jit(solution)/shard_map/ppermute | solution.py:384
  156.8 4.0 %collective-permute-start.34 = (f32[8,128]{1,0:T(8,128)S(1)}, f32[8,128]{1,0:T(8,128)S(1)}, u32[]{:S(2)}, u32[]{:S(2)}) collective-permute-start(f32[8,128]{1,0:T(8,128)S(1)} %slice.78), channel_id=1, source_target_pairs={{0,8},{8,0},{16,24},{24,16},{1,9},{9,1},{17,25},{25,17},{2,10},{10... | collective-permute-start | bytes 12296 | tf_op jit(solution)/shard_map/ppermute | solution.py:384
  160.9 18.0 %collective-permute-start.35 = (f32[256,512]{1,0:T(8,128)S(1)}, f32[256,512]{1,0:T(8,128)S(1)}, u32[]{:S(2)}, u32[]{:S(2)}) collective-permute-start(f32[256,512]{1,0:T(8,128)S(1)} %gate.19), channel_id=1, source_target_pairs={{0,1},{1,2},{2,3},{3,4},{4,5},{5,6},{6,7},{8,9},{9,10},{10,11},{11... | collective-permute-start | bytes 1572872 | tf_op jit(solution)/shard_map/ppermute | solution.py:402
  (16 other events, 131.6 us)

commit v2 on v1

--- a/solution.py
+++ b/solution.py
@@ -40,44 +40,50 @@
     odd = 2 * index + 1
     turn = odd[:, None] * odd[None, :] % (4 * length)
     shifted = np.exp(-2j * np.pi * turn / (4 * length)) / np.sqrt(length)
-    left, right = [], []
+    tables = []
     for matrix in (fresnel, shifted):
         for block in folded(matrix):
-            high, low = split_table(left_form(block))
-            left.append(np.concatenate([high, high, low], axis=1))
-            high, low = split_table(left_form(np.conj(block)))
-            left.append(np.concatenate([high, high, low], axis=1))
-            high, low = split_table(left_form(np.conj(block)))
-            right.append(np.concatenate([high, high, low], axis=0))
-            high, low = split_table(left_form(block))
-            right.append(np.concatenate([high, high, low], axis=0))
+            for form in (left_form(block), left_form(np.conj(block))):
+                tables.append(np.stack(split_table(form)))
     order = np.concatenate([index[: length // 2], index[length // 2 :][::-1]])
     ramp = np.exp(1j * np.pi * order / length)
     tilt = ramp[:, None] * ramp[None, :]
-    return np.stack(left), np.stack(right), np.stack([tilt.real, tilt.imag]).astype(np.float32)
+    return np.stack(tables), np.stack([tilt.real, tilt.imag]).astype(np.float32)
 
 
 def reversal(size):
     row = lax.broadcasted_iota(jnp.int32, (size, size), 0)
     col = lax.broadcasted_iota(jnp.int32, (size, size), 1)
-    return jnp.where(row + col == size - 1, 1.0, 0.0).astype(F32)
+    return jnp.where(row + col == size - 1, 1.0, 0.0).astype(BF16)
 
 
 def exact_dot(a, b):
-    return jnp.dot(a, b, precision=lax.Precision.HIGHEST, preferred_element_type=F32)
-
-
-def mirror_halves(x, flip):
-    half = x.shape[0] // 2
-    x = jnp.concatenate([x[:, :half], exact_dot(x[:, half:], flip)], axis=1)
-    return jnp.concatenate([x[:half], exact_dot(flip, x[half:])], axis=0)
+    moving, table = (a, b) if b.dtype == BF16 else (b, a)
+    total = None
+    for part in range(3):
+        piece = moving.astype(BF16)
+        moving = moving - piece.astype(F32)
+        done = jnp.dot(*((piece, b) if b.dtype == BF16 else (a, piece)), preferred_element_type=F32)
+        total = done if total is None else total + done
+    return total
+
+
+def mirror_halves(fields, flip):
+    count, size = len(fields), fields[0].shape[0]
+    half = size // 2
+    right = exact_dot(jnp.concatenate([x[:, half:] for x in fields], axis=0), flip)
+    fields = [
+        jnp.concatenate([x[:, :half], right[i * size : (i + 1) * size]], axis=1) for i, x in enumerate(fields)
+    ]
+    lower = exact_dot(flip, jnp.concatenate([x[half:] for x in fields], axis=1))
+    return [
+        jnp.concatenate([x[:half], lower[:, i * size : (i + 1) * size]], axis=0) for i, x in enumerate(fields)
+    ]
 
 
 def prep_kernel(ids, probe, amplitudes, probe_out, amp_out):
     flip = reversal(probe.shape[-1] // 2)
-    for part in range(2):
-        probe_out[part] = mirror_halves(probe[part], flip)
-    amp_out[...] = mirror_halves(amplitudes[ids[0]], flip)
+    probe_out[0], probe_out[1], amp_out[...] = mirror_halves([probe[0], probe[1], amplitudes[ids[0]]], flip)
 
 
 def crop_kernel(peers, plane, waits, ids, positions, strips, rim, *rest):
@@ -110,33 +116,40 @@
     for copy in loads:
         copy.wait()
     stores = []
-    for offset in sorted(range(peers), key=lambda m: -(m // 2)):
-        window = ids[0] ^ offset
-        row_first = positions[window, 0] - ids[1] * rows
-        col_first = positions[window, 1]
-        block_first = col_first >> 7
-        within = col_first & (LANES - 1)
-        moved = [
-            pltpu.roll(ext[block_first + i, pl.ds(row_first, size), :], (LANES - within) & (LANES - 1), 1)
-            for i in range(size // LANES + 1)
-        ]
-        keep = lane < LANES - within
-        picked = [jnp.where(keep, moved[i], moved[i + 1]) for i in range(size // LANES)]
-        cut[offset] = mirror_halves(jnp.concatenate(picked, axis=1), flip)
-        copy = pltpu.make_async_copy(cut.at[offset], outs[offset], stored.at[offset])
-        copy.start()
-        stores.append(copy)
+    for pair in sorted(range(0, peers, 2), reverse=True):
+        fields = []
+        for offset in (pair, pair + 1):
+            window = ids[0] ^ offset
+            row_first = positions[window, 0] - ids[1] * rows
+            col_first = positions[window, 1]
+            block_first = col_first >> 7
+            within = col_first & (LANES - 1)
+            moved = [
+                pltpu.roll(
+                    ext[block_first + i, pl.ds(row_first, size), :], (LANES - within) & (LANES - 1), 1
+                )
+                for i in range(size // LANES + 1)
+            ]
+            keep = lane < LANES - within
+            picked = [jnp.where(keep, moved[i], moved[i + 1]) for i in range(size // LANES)]
+            fields.append(jnp.concatenate(picked, axis=1))
+        fields = mirror_halves(fields, flip)
+        for i, offset in enumerate((pair, pair + 1)):
+            cut[offset] = fields[i]
+            copy = pltpu.make_async_copy(cut.at[offset], outs[offset], stored.at[offset])
+            copy.start()
+            stores.append(copy)
     for copy in stores:
         copy.wait()
 
 
-def place_kernel(peers, waits, ids, positions, *rest):
+def place_kernel(peers, ids, positions, *rest):
     own_in, near_in = rest[:2]
-    far_ins, rest = rest[2:peers], rest[peers + waits :]
+    far_ins = rest[2:peers]
     pieces = [own_in, near_in]
     for i in range(0, len(far_ins), 2):
         pieces += [far_ins[i].at[0], far_ins[i + 1]]
-    own, rim, ext, got, loaded, stored = rest
+    own, rim, ext, got, loaded, stored = rest[peers:]
     rows, cols = own.shape
     blocks = cols // LANES
     size = own_in.shape[-1]
@@ -148,15 +161,18 @@
     flip = reversal(size // 2)
     lane = lax.broadcasted_iota(jnp.int32, (size, LANES), 1)
     ext[...] = jnp.zeros(ext.shape, F32)
+    for copy in loads:
+        copy.wait()
+    fields = mirror_halves([got[offset] for offset in range(peers)], flip)
     for offset in range(peers):
         window = ids[0] ^ offset
         row_first = positions[window, 0] - ids[1] * rows
         col_first = positions[window, 1]
         block_first = col_first >> 7
         within = col_first & (LANES - 1)
-        loads[offset].wait()
-        plain = mirror_halves(got[offset], flip)
-        moved = [pltpu.roll(plain[:, i * LANES : (i + 1) * LANES], within, 1) for i in range(size // LANES)]
+        moved = [
+            pltpu.roll(fields[offset][:, i * LANES : (i + 1) * LANES], within, 1) for i in range(size // LANES)
+        ]
         keep = lane >= within
         zero = jnp.zeros((size, LANES), F32)
         moved = [zero] + moved + [zero]
@@ -184,7 +200,11 @@
     return high, low
 
 
-def sandwich(re, im, left, right, base, conj):
+def dot32(a, b):
+    return jnp.dot(a, b, preferred_element_type=F32)
+
+
+def sandwich(re, im, tables, base, conj):
     half = re.shape[0] // 2
 
     def fold(x):
@@ -204,11 +224,9 @@
         )
         high, low = split_value(field)
         middle.append(
-            jnp.dot(
-                jnp.concatenate([high, low, high], axis=1),
-                right[base + 2 * b + conj],
-                preferred_element_type=F32,
-            )
+            dot32(high, tables[base + 2 * b + 1 - conj, 0])
+            + dot32(low, tables[base + 2 * b + 1 - conj, 0])
+            + dot32(high, tables[base + 2 * b + 1 - conj, 1])
         )
     done = []
     for a in range(2):
@@ -222,11 +240,9 @@
         )
         high, low = split_value(field)
         done.append(
-            jnp.dot(
-                left[base + 2 * a + conj],
-                jnp.concatenate([high, low, high], axis=0),
-                preferred_element_type=F32,
-            )
+            dot32(tables[base + 2 * a + conj, 0], high)
+            + dot32(tables[base + 2 * a + conj, 0], low)
+            + dot32(tables[base + 2 * a + conj, 1], high)
         )
 
     def unfold(even, odd):
@@ -240,7 +256,7 @@
     )
 
 
-def optics_kernel(peers, per_device, ids, probe, amplitude, left, right, tilt, *rest):
+def optics_kernel(peers, per_device, ids, probe_in, amplitude_in, tables_in, tilt_in, *rest):
     chunks = 2 * per_device
     groups = peers // 2 + 1
     crops, pieces = [], []
@@ -257,9 +273,21 @@
             pieces += [far.at[0], far.at[1]]
     kept, handed = rest[chunks * groups : chunks * groups + 2]
     rest = rest[chunks * groups + 2 :]
-    trans, history, terms, grad, loaded, stored = rest
+    trans, history, terms, grad, tables, tilt, amplitude, fixed, loaded, stored = rest
+    size = grad.shape[-1]
+    share = size // peers
     layers = peers * per_device
     me = ids[0]
+    half = tables.shape[0] // 2
+    settings = [
+        pltpu.make_async_copy(probe_in, history.at[0], fixed.at[0]),
+        pltpu.make_async_copy(tables_in.at[pl.ds(0, half)], tables.at[pl.ds(0, half)], fixed.at[1]),
+        pltpu.make_async_copy(tables_in.at[pl.ds(half, half)], tables.at[pl.ds(half, half)], fixed.at[2]),
+        pltpu.make_async_copy(tilt_in, tilt, fixed.at[3]),
+        pltpu.make_async_copy(amplitude_in, amplitude, fixed.at[4]),
+    ]
+    for copy in settings[:2]:
+        copy.start()
     for j in range(per_device):
         for offset in range(peers):
             at = (me ^ offset) * per_device + j
@@ -267,7 +295,10 @@
                 pltpu.make_async_copy(
                     crops[(j * 2 + part) * peers + offset], trans.at[at, part], loaded.at[2 * at + part]
                 ).start()
-    history[0] = probe[...]
+    for copy in settings[2:]:
+        copy.start()
+    for copy in settings[:2]:
+        copy.wait()
 
     def mixed(layer):
         for part in range(2):
@@ -278,18 +309,20 @@
 
     def forward(layer, carry):
         re, im = mixed(layer)
-        re, im = sandwich(re, im, left, right, 0, 0)
+        re, im = sandwich(re, im, tables, 0, 0)
         history[layer + 1, 0] = re
         history[layer + 1, 1] = im
         return carry
 
     lax.fori_loop(0, layers - 1, forward, 0)
     re, im = mixed(layers - 1)
+    for copy in settings[2:]:
+        copy.wait()
     d_re, d_im = tilt[0], tilt[1]
     re, im = re * d_re - im * d_im, re * d_im + im * d_re
-    re, im = sandwich(re, im, left, right, 4, 0)
+    re, im = sandwich(re, im, tables, 4, 0)
     factor = 1.0 - amplitude[...] / jnp.sqrt(re * re + im * im + 1.0)
-    re, im = sandwich(re * factor, im * factor, left, right, 4, 1)
+    re, im = sandwich(re * factor, im * factor, tables, 4, 1)
     back_re, back_im = re * d_re + im * d_im, im * d_re - re * d_im
 
     def collect(layer, back_re, back_im):
@@ -305,7 +338,7 @@
                     for part in range(2):
                         pltpu.make_async_copy(
                             terms.at[layer, part],
-                            pieces[(j * 2 + part) * peers + offset],
+                            pieces[(j * 2 + part) * peers + offset].at[pl.ds(0, size)],
                             stored.at[2 * layer + part],
                         ).start()
 
@@ -316,22 +349,32 @@
     collect(layers - 1, back_re, back_im)
 
     def backward(step, carry):
-        back_re, back_im = sandwich(grad[0], grad[1], left, right, 0, 1)
+        back_re, back_im = sandwich(grad[0], grad[1], tables, 0, 1)
         collect(layers - 2 - step, back_re, back_im)
         return carry
 
     lax.fori_loop(0, layers - 1, backward, 0)
-    flip = reversal(grad.shape[-1] // 2)
-    share_rows = kept.shape[2]
-    for part in range(2):
-        grad[part] = mirror_halves(grad[part], flip)
+    grad[0], grad[1] = mirror_halves([grad[0], grad[1]], reversal(size // 2))
+    shares = []
     for offset in range(peers):
-        first = pl.multiple_of((me ^ offset) * share_rows, share_rows)
-        target = handed if offset % 2 else kept
-        target[offset // 2] = grad[:, pl.ds(first, share_rows), :]
+        first = pl.multiple_of((me ^ offset) * share, share)
+        for part in range(2):
+            shares.append(
+                pltpu.make_async_copy(
+                    grad.at[part, pl.ds(first, share)],
+                    (kept, handed)[offset % 2].at[offset // 2, part],
+                    fixed.at[2 * offset + part],
+                )
+            )
+    for copy in shares:
+        copy.start()
     for layer in range(layers):
         for part in range(2):
-            pltpu.make_async_copy(terms.at[layer, part], pieces[0], stored.at[2 * layer + part]).wait()
+            pltpu.make_async_copy(
+                terms.at[layer, part], pieces[0].at[pl.ds(0, size)], stored.at[2 * layer + part]
+            ).wait()
+    for copy in shares:
+        copy.wait()
 
 
 SMEM_SPEC = pl.BlockSpec(memory_space=pltpu.SMEM)
@@ -408,7 +451,7 @@
     peers = lax.axis_size("depth")
     tiles = lax.axis_size("tile")
     ids = jnp.stack([lax.axis_index("depth"), lax.axis_index("tile")]).astype(jnp.int32)
-    left, right, tilt = (jnp.asarray(x) for x in optics_tables(size))
+    tables, tilt = (jnp.asarray(x) for x in optics_tables(size))
 
     probe, amplitude = run_kernel(
         prep_kernel,
@@ -450,19 +493,23 @@
         functools.partial(optics_kernel, peers, per_device),
         "optics",
         group * len(chunks) + (shape(peers // 2, 2, size // peers, size),) * 2,
-        [SMEM_SPEC] + [VMEM_SPEC] * 5 + [HBM_SPEC] * (len(chunks) * peers),
-        (HBM_SPEC,) * (len(chunks) * groups) + (VMEM_SPEC,) * 2,
+        [SMEM_SPEC] + [HBM_SPEC] * (4 + len(chunks) * peers),
+        (HBM_SPEC,) * (len(chunks) * groups + 2),
         [
             pltpu.VMEM((layers, 2, size, size), F32),
             pltpu.VMEM((layers, 2, size, size), F32),
             pltpu.VMEM((layers, 2, size, size), F32),
             pltpu.VMEM((2, size, size), F32),
+            pltpu.VMEM(tables.shape, BF16),
+            pltpu.VMEM(tilt.shape, F32),
+            pltpu.VMEM((size, size), F32),
+            pltpu.SemaphoreType.DMA((max(5, 2 * peers),)),
             pltpu.SemaphoreType.DMA((2 * layers,)),
             pltpu.SemaphoreType.DMA((2 * layers,)),
         ],
         15,
         32,
-    )(ids, probe, amplitude, left, right, tilt, *[x for got in crops for x in got])
+    )(ids, probe, amplitude, tables, tilt, *[x for got in crops for x in got])
 
     kept, handed = result[-2:]
     probe_halves = kept + swap(handed, "depth", 1)
@@ -472,10 +519,10 @@
         probe_grad = probe_grad[:1] + swap(probe_grad[1:], "depth", step)
         step *= 2
     probe_steps = [probe_grad[0]]
-    step = 1
-    while step < tiles:
+    step = tiles // 2
+    while step:
         probe_steps.append(probe_steps[-1] + swap(probe_steps[-1], "tile", step))
-        step *= 2
+        step //= 2
 
     own, rim_back, returned = {}, {}, []
     order = list(reversed(chunks))
@@ -483,16 +530,18 @@
         at = chunks.index(c) * groups
         mine = result[at : at + groups]
         if k == 0:
-            mine = gate(mine, probe_steps[:1])
+            mine = gate(mine, [probe_steps[0]])
         if k >= ahead:
             mine = gate(mine, returned[k - ahead][2::2] + [own[order[k - ahead]]])
-        returned.append(exchanged(mine, [own[order[k - 1]]] if k else []))
-        waits = [] if k else probe_steps[-1:]
-        own[c], outside = run_kernel(
-            functools.partial(place_kernel, peers, len(waits)),
+        before = [own[order[k - 1]]] if k else probe_steps[-2:-1]
+        if k == 1:
+            before.append(probe_steps[-1])
+        returned.append(exchanged(mine, before))
+        mine = run_kernel(
+            functools.partial(place_kernel, peers),
             "place",
             (shape(rows, cols), shape(rows, cols)),
-            [SMEM_SPEC, SMEM_SPEC] + [HBM_SPEC] * (peers + len(waits)),
+            [SMEM_SPEC, SMEM_SPEC] + [HBM_SPEC] * peers,
             (HBM_SPEC, HBM_SPEC),
             [
                 pltpu.VMEM((cols // LANES + 1, 2 * rows, LANES), F32),
@@ -501,9 +550,10 @@
                 pltpu.SemaphoreType.DMA((2 * cols // LANES,)),
             ],
             2,
-        )(ids, scan_positions, *returned[k], *waits)
+        )(ids, scan_positions, *returned[k])
+        own[c], outside = mine[:2]
         if k >= ahead:
-            (outside,) = gate([outside], [echo(rim_back[order[k - ahead]])])
+            (outside,) = gate([outside], [echo(echo(rim_back[order[k - ahead]]))])
         rim_back[c] = shift(outside, "tile", 1)
 
     rim_back[order[-2]] = gate([rim_back[order[-2]]], [echo(rim_back[order[-2]])])[0]

time: 181 us -> 175 us (0.967)
  Pallas kernels: 51.7 us -> 38.8 us
  starting transfers between devices: 38.6 us -> 41.9 us
  waiting for transfers between devices: 81.6 us -> 84.7 us
    pallas_call x4, Pallas kernels: 15.6 us -> 8.2 us  [body(): run_kernel(functools.partial(place_kernel, peers), 'place', (shape(rows,...]
    ppermute x8, waiting for transfers between devices: 37.7 us -> 44.4 us  [shift(): lax.ppermute(x, axis, [(i, i + by) for i in range(peers) if 0 <= i + by <...]
    pallas_call x4, Pallas kernels: 17.6 us -> 11.8 us  [body(): run_kernel(functools.partial(crop_kernel, peers, c, len(waits)), 'crop',...]
    ppermute x8, starting transfers between devices: 17.6 us -> 22.7 us  [shift(): lax.ppermute(x, axis, [(i, i + by) for i in range(peers) if 0 <= i + by <...]
    ppermute x32 -> x34, waiting for transfers between devices: 43.9 us -> 40.3 us  [swap(): return lax.ppermute(x, axis, [(i, i ^ offset) for i in range(peers)])]
    ppermute x32 -> x34, starting transfers between devices: 21.1 us -> 19.2 us  [swap(): return lax.ppermute(x, axis, [(i, i ^ offset) for i in range(peers)])]
  transfers between devices with their start and end apart: 40 -> 42, of which waited for: 22 -> 25; matrix products, arithmetic and copies ran while one was open for 0% -> 0% of each run, Pallas kernels for 19% -> 12%
where the time goes in v2:
time: 175 us; the launch traced here: 174 us
  waiting for transfers between devices  84.7 us (48%)
  starting transfers between devices  41.9 us (24%)
  Pallas kernels  38.8 us (22%)
  local copies, waits for them, and re-layouts  5.36 us (3%)
  other arithmetic  2.16 us (1%)
    ppermute x8, waiting for transfers between devices, shift(): lax.ppermute(x, axis, [(i, i + by) for i in range(peers) if 0 <= i + by <...  44.4 us
    ppermute x34, waiting for transfers between devices, swap(): return lax.ppermute(x, axis, [(i, i ^ offset) for i in range(peers)])  40.3 us
    ppermute x8, starting transfers between devices, shift(): lax.ppermute(x, axis, [(i, i + by) for i in range(peers) if 0 <= i + by <...  22.7 us
    ppermute x34, starting transfers between devices, swap(): return lax.ppermute(x, axis, [(i, i ^ offset) for i in range(peers)])  19.2 us
    pallas_call x1, Pallas kernels, body(): run_kernel(functools.partial(optics_kernel, peers, per_device), 'optics',...  17.4 us
    pallas_call x4, Pallas kernels, body(): run_kernel(functools.partial(crop_kernel, peers, c, len(waits)), 'crop',...  11.8 us
    pallas_call x4, Pallas kernels, body(): run_kernel(functools.partial(place_kernel, peers), 'place', (shape(rows,...  8.2 us
  transfers between devices with their start and end apart: 42, of which 25 were waited for; matrix products, arithmetic and copies ran while one was open for 0% of the time, Pallas kernels for 12%

profile of v2, /device:TPU:4, one launch (start us, length us, event | category | flops | bytes accessed | tf_op | source)
XLA Modules:
  0.0 174.0 jit_solution(9799133118183425962)
XLA Ops:
  0.6 2.8 %slice_bitcast_fusion = (f32[256,512]{1,0:T(8,128)S(1)}, f32[256,512]{1,0:T(8,128)S(1)}, f32[256,512]{1,0:T(8,128)}, f32[256,512]{1,0:T(8,128)}) fusion(f32[2,2,256,512]{3,2,1,0:T(8,128)} %strips.7), kind=kLoop, calls=%fused_computation.7 | loop fusion | bytes 4194304 | tf_op jit(solution)/shard_map/squeeze | solution.py:468
  3.5 1.9 %collective-permute-start.4 = (f32[256,512]{1,0:T(8,128)}, f32[256,512]{1,0:T(8,128)}, u32[]{:S(2)}, u32[]{:S(2)}) collective-permute-start(f32[256,512]{1,0:T(8,128)} %get-tuple-element.94), channel_id=1, source_target_pairs={{1,0},{2,1},{3,2},{4,3},{5,4},{6,5},{7,6},{9,8},{10,9},{11,10},{12... | collective-permute-start | bytes 1572872 | tf_op jit(solution)/shard_map/ppermute | solution.py:445
  5.4 1.9 %collective-permute-start = (f32[256,512]{1,0:T(8,128)}, f32[256,512]{1,0:T(8,128)}, u32[]{:S(2)}, u32[]{:S(2)}) collective-permute-start(f32[256,512]{1,0:T(8,128)} %get-tuple-element.95), channel_id=1, source_target_pairs={{1,0},{2,1},{3,2},{4,3},{5,4},{6,5},{7,6},{9,8},{10,9},{11,10},{12... | collective-permute-start | bytes 1572872 | tf_op jit(solution)/shard_map/ppermute | solution.py:445
  11.1 10.3 %collective-permute-done.4.rim = f32[256,512]{1,0:T(8,128)} collective-permute-done((f32[256,512]{1,0:T(8,128)}, f32[256,512]{1,0:T(8,128)}, u32[]{:S(2)}, u32[]{:S(2)}) %collective-permute-start.4) | collective-permute-done | bytes 524320 | tf_op jit(solution)/shard_map/ppermute | solution.py:445
  21.4 3.4 %crop.5 = (f32[256,256]{1,0:T(8,128)S(1)}, f32[256,256]{1,0:T(8,128)S(1)}, f32[2,256,256]{2,1,0:T(8,128)S(1)}) custom-call(s32[2]{0:T(128)S(1)} %pad_add_fusion.ids, s32[4,2]{1,0:T(4,128)S(1)} %copy.33.positions, f32[2,2,256,512]{3,2,1,0:T(8,128)S(1)} %copy-done, f32[256,512]{1,0:T(8,128)} %collective-permute-done.4.rim, ...), custom_call_target="tpu_custom_call" | custom-call | flops 2000000 | bytes 2000 | tf_op jit(solution)/shard_map/crop/pallas_call | solution.py:475
  26.4 1.9 %collective-permute-start.12 = (f32[256,512]{1,0:T(8,128)S(1)}, f32[256,512]{1,0:T(8,128)S(1)}, u32[]{:S(2)}, u32[]{:S(2)}) collective-permute-start(f32[256,512]{1,0:T(8,128)S(1)} %gate.13), channel_id=1, source_target_pairs={{1,0},{2,1},{3,2},{4,3},{5,4},{6,5},{7,6},{9,8},{10,9},{11,10},{12... | collective-permute-start | bytes 1572872 | tf_op jit(solution)/shard_map/ppermute | solution.py:445
  28.3 4.3 %collective-permute-done.rim = f32[256,512]{1,0:T(8,128)} collective-permute-done((f32[256,512]{1,0:T(8,128)}, f32[256,512]{1,0:T(8,128)}, u32[]{:S(2)}, u32[]{:S(2)}) %collective-permute-start) | collective-permute-done | bytes 524320 | tf_op jit(solution)/shard_map/ppermute | solution.py:445
  32.6 3.4 %crop.4 = (f32[256,256]{1,0:T(8,128)S(1)}, f32[256,256]{1,0:T(8,128)S(1)}, f32[2,256,256]{2,1,0:T(8,128)S(1)}) custom-call(s32[2]{0:T(128)S(1)} %pad_add_fusion.ids, s32[4,2]{1,0:T(4,128)S(1)} %copy.33.positions, f32[2,2,256,512]{3,2,1,0:T(8,128)S(1)} %copy-done, f32[256,512]{1,0:T(8,128)} %collective-permute-done.rim, ...), custom_call_target="tpu_custom_call" | custom-call | flops 2000000 | bytes 2000 | tf_op jit(solution)/shard_map/crop/pallas_call | solution.py:475
  39.5 4.5 %collective-permute-done.12.rim = f32[256,512]{1,0:T(8,128)S(1)} collective-permute-done((f32[256,512]{1,0:T(8,128)S(1)}, f32[256,512]{1,0:T(8,128)S(1)}, u32[]{:S(2)}, u32[]{:S(2)}) %collective-permute-start.12) | collective-permute-done | bytes 524320 | tf_op jit(solution)/shard_map/ppermute | solution.py:445
  44.0 2.5 %crop.7 = (f32[256,256]{1,0:T(8,128)S(1)}, f32[256,256]{1,0:T(8,128)S(1)}, f32[2,256,256]{2,1,0:T(8,128)S(1)}) custom-call(s32[2]{0:T(128)S(1)} %pad_add_fusion.ids, s32[4,2]{1,0:T(4,128)S(1)} %copy.33.positions, f32[2,2,256,512]{3,2,1,0:T(8,128)S(1)} %copy-done, f32[256,512]{1,0:T(8,128)S(1)} %collective-permute-done.12.rim, ...), custom_call_target="tpu_custom_call" | custom-call | flops 2000000 | bytes 2000 | tf_op jit(solution)/shard_map/crop/pallas_call | solution.py:475
  49.0 4.8 %collective-permute-done.8.rim = f32[256,512]{1,0:T(8,128)S(1)} collective-permute-done((f32[256,512]{1,0:T(8,128)S(1)}, f32[256,512]{1,0:T(8,128)S(1)}, u32[]{:S(2)}, u32[]{:S(2)}) %collective-permute-start.8) | collective-permute-done | bytes 524320 | tf_op jit(solution)/shard_map/ppermute | solution.py:445
  53.8 2.5 %crop.6 = (f32[256,256]{1,0:T(8,128)S(1)}, f32[256,256]{1,0:T(8,128)S(1)}, f32[2,256,256]{2,1,0:T(8,128)S(1)}) custom-call(s32[2]{0:T(128)S(1)} %pad_add_fusion.ids, s32[4,2]{1,0:T(4,128)S(1)} %copy.33.positions, f32[2,2,256,512]{3,2,1,0:T(8,128)S(1)} %copy-done, f32[256,512]{1,0:T(8,128)S(1)} %collective-permute-done.8.rim, ...), custom_call_target="tpu_custom_call" | custom-call | flops 2000000 | bytes 2000 | tf_op jit(solution)/shard_map/crop/pallas_call | solution.py:475
  58.0 2.2 %collective-permute-done.14.rest_14_ = f32[2,256,256]{2,1,0:T(8,128)S(1)} collective-permute-done((f32[2,256,256]{2,1,0:T(8,128)S(1)}, f32[2,256,256]{2,1,0:T(8,128)S(1)}, u32[]{:S(2)}, u32[]{:S(2)}) %collective-permute-start.14) | collective-permute-done | bytes 524320 | tf_op jit(solution)/shard_map/ppermute | solution.py:427
  60.3 10.0 %collective-permute-done.10.rest_10_ = f32[2,256,256]{2,1,0:T(8,128)S(1)} collective-permute-done((f32[2,256,256]{2,1,0:T(8,128)S(1)}, f32[2,256,256]{2,1,0:T(8,128)S(1)}, u32[]{:S(2)}, u32[]{:S(2)}) %collective-permute-start.10) | collective-permute-done | bytes 524320 | tf_op jit(solution)/shard_map/ppermute | solution.py:427
  72.9 17.4 %optics.1 = (f32[256,256]{1,0:T(8,128)S(1)}, f32[256,256]{1,0:T(8,128)S(1)}, f32[2,256,256]{2,1,0:T(8,128)S(1)}, f32[256,256]{1,0:T(8,128)S(1)}, f32[256,256]{1,...) custom-call(s32[2]{0:T(128)S(1)} %pad_add_fusion.ids, ...), custom_call_target="tpu_custom_call" | custom-call | flops 15000000 | bytes 15000 | tf_op jit(solution)/shard_map/optics/pallas_call | solution.py:492
  93.5 4.1 %collective-permute-done.18 = f32[1,2,64,256]{3,2,1,0:T(8,128)S(1)} collective-permute-done((f32[1,2,64,256]{3,2,1,0:T(8,128)S(1)}, f32[1,2,64,256]{3,2,1,0:T(8,128)S(1)}, u32[]{:S(2)}, u32[]{:S(2)}) %collective-permute-start.18) | collective-permute-done | bytes 131104 | tf_op jit(solution)/shard_map/ppermute | solution.py:427
  99.2 2.6 %collective-permute-start.21 = (f32[2,64,256]{2,1,0:T(8,128)S(1)}, f32[2,64,256]{2,1,0:T(8,128)S(1)}, u32[]{:S(2)}, u32[]{:S(2)}) collective-permute-start(f32[2,64,256]{2,1,0:T(8,128)S(1)} %fusion.refs_3_), channel_id=1, source_target_pairs={{0,4},{1,5},{2,6},{3,7},{4,0},{5,1},{6,2},{7,3},{8,12},{9,13},{10,... | collective-permute-start | bytes 393224 | tf_op jit(solution)/shard_map/ppermute | solution.py:427
  101.8 5.7 %collective-permute-done.21 = f32[2,64,256]{2,1,0:T(8,128)S(1)} collective-permute-done((f32[2,64,256]{2,1,0:T(8,128)S(1)}, f32[2,64,256]{2,1,0:T(8,128)S(1)}, u32[]{:S(2)}, u32[]{:S(2)}) %collective-permute-start.21) | collective-permute-done | bytes 131104 | tf_op jit(solution)/shard_map/ppermute | solution.py:427
  108.1 4.4 %collective-permute-done.22 = f32[2,64,256]{2,1,0:T(8,128)S(1)} collective-permute-done((f32[2,64,256]{2,1,0:T(8,128)S(1)}, f32[2,64,256]{2,1,0:T(8,128)S(1)}, u32[]{:S(2)}, u32[]{:S(2)}) %collective-permute-start.22) | collective-permute-done | bytes 131104 | tf_op jit(solution)/shard_map/ppermute | solution.py:427
  113.2 5.4 %collective-permute-done.24 = f32[2,64,256]{2,1,0:T(8,128)S(1)} collective-permute-done((f32[2,64,256]{2,1,0:T(8,128)S(1)}, f32[2,64,256]{2,1,0:T(8,128)S(1)}, u32[]{:S(2)}, u32[]{:S(2)}) %collective-permute-start.24) | collective-permute-done | bytes 131104 | tf_op jit(solution)/shard_map/ppermute | solution.py:427
  118.7 2.1 %place.4 = (f32[256,512]{1,0:T(8,128)S(1)}, f32[256,512]{1,0:T(8,128)S(1)}) custom-call(s32[2]{0:T(128)S(1)} %pad_add_fusion.ids, s32[4,2]{1,0:T(4,128)S(1)} %copy.33.positions, f32[256,256]{1,0:T(8,128)S(1)} %get-tuple-element.70.rest_0_, f32[256,256]{1,0:T(8,128)S(1)} %collective-permute-done.19.rest_1_, f32[2,256,256]{2,1,0:T(8,128)S(1)} %gate.15.rest_2_.refs_3_, ...), custom_call_target="tpu_custom_call" | custom-call | flops 2000000 | bytes 2000 | tf_op jit(solution)/shard_map/place/pallas_call | solution.py:540
  122.4 3.2 %collective-permute-start.37 = (f32[256,512]{1,0:T(8,128)S(1)}, f32[256,512]{1,0:T(8,128)S(1)}, u32[]{:S(2)}, u32[]{:S(2)}) collective-permute-start(f32[256,512]{1,0:T(8,128)S(1)} %get-tuple-element.91), channel_id=1, source_target_pairs={{0,1},{1,2},{2,3},{3,4},{4,5},{5,6},{6,7},{8,9},{9,10},{10,11},{11... | collective-permute-start | bytes 1572872 | tf_op jit(solution)/shard_map/ppermute | solution.py:445
  125.6 2.1 %place.5 = (f32[256,512]{1,0:T(8,128)S(1)}, f32[256,512]{1,0:T(8,128)S(1)}) custom-call(s32[2]{0:T(128)S(1)} %pad_add_fusion.ids, s32[4,2]{1,0:T(4,128)S(1)} %copy.33.positions, f32[256,256]{1,0:T(8,128)S(1)} %get-tuple-element.74.rest_0_, f32[256,256]{1,0:T(8,128)S(1)} %collective-permute-done.25.rest_1_, f32[2,256,256]{2,1,0:T(8,128)S(1)} %gate.16.rest_2_.refs_3_, ...), custom_call_target="tpu_custom_call" | custom-call | flops 2000000 | bytes 2000 | tf_op jit(solution)/shard_map/place/pallas_call | solution.py:540
  127.7 3.7 %collective-permute-start.33 = (f32[256,512]{1,0:T(8,128)S(1)}, f32[256,512]{1,0:T(8,128)S(1)}, u32[]{:S(2)}, u32[]{:S(2)}) collective-permute-start(f32[256,512]{1,0:T(8,128)S(1)} %get-tuple-element.89), channel_id=1, source_target_pairs={{0,1},{1,2},{2,3},{3,4},{4,5},{5,6},{6,7},{8,9},{9,10},{10,11},{11... | collective-permute-start | bytes 1572872 | tf_op jit(solution)/shard_map/ppermute | solution.py:445
  134.7 4.3 %collective-permute-done.37 = f32[256,512]{1,0:T(8,128)S(1)} collective-permute-done((f32[256,512]{1,0:T(8,128)S(1)}, f32[256,512]{1,0:T(8,128)S(1)}, u32[]{:S(2)}, u32[]{:S(2)}) %collective-permute-start.37) | collective-permute-done | bytes 524320 | tf_op jit(solution)/shard_map/ppermute | solution.py:445
  140.7 2.0 %place.6 = (f32[256,512]{1,0:T(8,128)S(1)}, f32[256,512]{1,0:T(8,128)S(1)}) custom-call(s32[2]{0:T(128)S(1)} %pad_add_fusion.ids, s32[4,2]{1,0:T(4,128)S(1)} %copy.33.positions, f32[256,256]{1,0:T(8,128)S(1)} %get-tuple-element.83.rest_0_, f32[256,256]{1,0:T(8,128)S(1)} %collective-permute-done.29.rest_1_, f32[2,256,256]{2,1,0:T(8,128)S(1)} %gate.19.rest_2_, ...), custom_call_target="tpu_custom_call" | custom-call | flops 2000000 | bytes 2000 | tf_op jit(solution)/shard_map/place/pallas_call | solution.py:540
  142.8 4.1 %collective-permute-start.40 = (f32[256,512]{1,0:T(8,128)S(1)}, f32[256,512]{1,0:T(8,128)S(1)}, u32[]{:S(2)}, u32[]{:S(2)}) collective-permute-start(f32[256,512]{1,0:T(8,128)S(1)} %gate.22), channel_id=1, source_target_pairs={{0,1},{1,2},{2,3},{3,4},{4,5},{5,6},{6,7},{8,9},{9,10},{10,11},{11... | collective-permute-start | bytes 1572872 | tf_op jit(solution)/shard_map/ppermute | solution.py:445
  146.9 3.4 %collective-permute-done.33 = f32[256,512]{1,0:T(8,128)S(1)} collective-permute-done((f32[256,512]{1,0:T(8,128)S(1)}, f32[256,512]{1,0:T(8,128)S(1)}, u32[]{:S(2)}, u32[]{:S(2)}) %collective-permute-start.33) | collective-permute-done | bytes 524320 | tf_op jit(solution)/shard_map/ppermute | solution.py:445
  152.0 2.0 %place.7 = (f32[256,512]{1,0:T(8,128)S(1)}, f32[256,512]{1,0:T(8,128)S(1)}) custom-call(s32[2]{0:T(128)S(1)} %pad_add_fusion.ids, s32[4,2]{1,0:T(4,128)S(1)} %copy.33.positions, f32[256,256]{1,0:T(8,128)S(1)} %get-tuple-element.77.rest_0_, f32[256,256]{1,0:T(8,128)S(1)} %collective-permute-done.27.rest_1_, f32[2,256,256]{2,1,0:T(8,128)S(1)} %gate.20.rest_2_, ...), custom_call_target="tpu_custom_call" | custom-call | flops 2000000 | bytes 2000 | tf_op jit(solution)/shard_map/place/pallas_call | solution.py:540
  154.1 4.1 %collective-permute-start.36 = (f32[256,512]{1,0:T(8,128)S(1)}, f32[256,512]{1,0:T(8,128)S(1)}, u32[]{:S(2)}, u32[]{:S(2)}) collective-permute-start(f32[256,512]{1,0:T(8,128)S(1)} %gate.21), channel_id=1, source_target_pairs={{0,1},{1,2},{2,3},{3,4},{4,5},{5,6},{6,7},{8,9},{9,10},{10,11},{11... | collective-permute-start | bytes 1572872 | tf_op jit(solution)/shard_map/ppermute | solution.py:445
  158.3 3.2 %collective-permute-done.40.refs_0_ = f32[256,512]{1,0:T(8,128)S(1)} collective-permute-done((f32[256,512]{1,0:T(8,128)S(1)}, f32[256,512]{1,0:T(8,128)S(1)}, u32[]{:S(2)}, u32[]{:S(2)}) %collective-permute-start.40) | collective-permute-done | bytes 524320 | tf_op jit(solution)/shard_map/ppermute | solution.py:445
  162.8 9.6 %collective-permute-done.36 = f32[256,512]{1,0:T(8,128)S(1)} collective-permute-done((f32[256,512]{1,0:T(8,128)S(1)}, f32[256,512]{1,0:T(8,128)S(1)}, u32[]{:S(2)}, u32[]{:S(2)}) %collective-permute-start.36) | collective-permute-done | bytes 524320 | tf_op jit(solution)/shard_map/ppermute | solution.py:445
  (115 shorter events, 33.0 us)
Async XLA Ops:
  3.5 17.9 %collective-permute-start.4 = (f32[256,512]{1,0:T(8,128)}, f32[256,512]{1,0:T(8,128)}, u32[]{:S(2)}, u32[]{:S(2)}) collective-permute-start(f32[256,512]{1,0:T(8,128)} %get-tuple-element.94), channel_id=1, source_target_pairs={{1,0},{2,1},{3,2},{4,3},{5,4},{6,5},{7,6},{9,8},{10,9},{11,10},{12... | collective-permute-start | bytes 1572872 | tf_op jit(solution)/shard_map/ppermute | solution.py:445
  5.4 27.2 %collective-permute-start = (f32[256,512]{1,0:T(8,128)}, f32[256,512]{1,0:T(8,128)}, u32[]{:S(2)}, u32[]{:S(2)}) collective-permute-start(f32[256,512]{1,0:T(8,128)} %get-tuple-element.95), channel_id=1, source_target_pairs={{1,0},{2,1},{3,2},{4,3},{5,4},{6,5},{7,6},{9,8},{10,9},{11,10},{12... | collective-permute-start | bytes 1572872 | tf_op jit(solution)/shard_map/ppermute | solution.py:445
  24.8 14.7 %collective-permute-start.6 = (f32[2,256,256]{2,1,0:T(8,128)S(1)}, f32[2,256,256]{2,1,0:T(8,128)S(1)}, u32[]{:S(2)}, u32[]{:S(2)}) collective-permute-start(f32[2,256,256]{2,1,0:T(8,128)S(1)} %get-tuple-element.54), channel_id=1, source_target_pairs={{0,16},{8,24},{16,0},{24,8},{1,17},{9,25},{17,1},{25,9},{2,18},{10... | collective-permute-start | bytes 1572872 | tf_op jit(solution)/shard_map/ppermute | solution.py:427
  26.4 17.6 %collective-permute-start.12 = (f32[256,512]{1,0:T(8,128)S(1)}, f32[256,512]{1,0:T(8,128)S(1)}, u32[]{:S(2)}, u32[]{:S(2)}) collective-permute-start(f32[256,512]{1,0:T(8,128)S(1)} %gate.13), channel_id=1, source_target_pairs={{1,0},{2,1},{3,2},{4,3},{5,4},{6,5},{7,6},{9,8},{10,9},{11,10},{12... | collective-permute-start | bytes 1572872 | tf_op jit(solution)/shard_map/ppermute | solution.py:445
  36.0 13.0 %collective-permute-start.2 = (f32[2,256,256]{2,1,0:T(8,128)S(1)}, f32[2,256,256]{2,1,0:T(8,128)S(1)}, u32[]{:S(2)}, u32[]{:S(2)}) collective-permute-start(f32[2,256,256]{2,1,0:T(8,128)S(1)} %get-tuple-element.51), channel_id=1, source_target_pairs={{0,16},{8,24},{16,0},{24,8},{1,17},{9,25},{17,1},{25,9},{2,18},{10... | collective-permute-start | bytes 1572872 | tf_op jit(solution)/shard_map/ppermute | solution.py:427
  37.6 16.2 %collective-permute-start.8 = (f32[256,512]{1,0:T(8,128)S(1)}, f32[256,512]{1,0:T(8,128)S(1)}, u32[]{:S(2)}, u32[]{:S(2)}) collective-permute-start(f32[256,512]{1,0:T(8,128)S(1)} %gate.12), channel_id=1, source_target_pairs={{1,0},{2,1},{3,2},{4,3},{5,4},{6,5},{7,6},{9,8},{10,9},{11,10},{12... | collective-permute-start | bytes 1572872 | tf_op jit(solution)/shard_map/ppermute | solution.py:445
  46.5 13.7 %collective-permute-start.14 = (f32[2,256,256]{2,1,0:T(8,128)S(1)}, f32[2,256,256]{2,1,0:T(8,128)S(1)}, u32[]{:S(2)}, u32[]{:S(2)}) collective-permute-start(f32[2,256,256]{2,1,0:T(8,128)S(1)} %get-tuple-element.60), channel_id=1, source_target_pairs={{0,16},{8,24},{16,0},{24,8},{1,17},{9,25},{17,1},{25,9},{2,18},{10... | collective-permute-start | bytes 1572872 | tf_op jit(solution)/shard_map/ppermute | solution.py:427
  47.8 22.5 %collective-permute-start.5 = (f32[256,256]{1,0:T(8,128)S(1)}, f32[256,256]{1,0:T(8,128)S(1)}, u32[]{:S(2)}, u32[]{:S(2)}) collective-permute-start(f32[256,256]{1,0:T(8,128)S(1)} %get-tuple-element.53), channel_id=1, source_target_pairs={{0,8},{8,0},{16,24},{24,16},{1,9},{9,1},{17,25},{25,17},{2,10},{10... | collective-permute-start | bytes 786440 | tf_op jit(solution)/shard_map/ppermute | solution.py:427
  47.8 23.1 %collective-permute-start.1 = (f32[256,256]{1,0:T(8,128)S(1)}, f32[256,256]{1,0:T(8,128)S(1)}, u32[]{:S(2)}, u32[]{:S(2)}) collective-permute-start(f32[256,256]{1,0:T(8,128)S(1)} %get-tuple-element.50), channel_id=1, source_target_pairs={{0,8},{8,0},{16,24},{24,16},{1,9},{9,1},{17,25},{25,17},{2,10},{10... | collective-permute-start | bytes 786440 | tf_op jit(solution)/shard_map/ppermute | solution.py:427
  56.3 13.9 %collective-permute-start.10 = (f32[2,256,256]{2,1,0:T(8,128)S(1)}, f32[2,256,256]{2,1,0:T(8,128)S(1)}, u32[]{:S(2)}, u32[]{:S(2)}) collective-permute-start(f32[2,256,256]{2,1,0:T(8,128)S(1)} %get-tuple-element.57), channel_id=1, source_target_pairs={{0,16},{8,24},{16,0},{24,8},{1,17},{9,25},{17,1},{25,9},{2,18},{10... | collective-permute-start | bytes 1572872 | tf_op jit(solution)/shard_map/ppermute | solution.py:427
  57.9 13.0 %collective-permute-start.7 = (f32[256,256]{1,0:T(8,128)S(1)}, f32[256,256]{1,0:T(8,128)S(1)}, u32[]{:S(2)}, u32[]{:S(2)}) collective-permute-start(f32[256,256]{1,0:T(8,128)S(1)} %slice_bitcast_fusion.10), channel_id=1, source_target_pairs={{0,8},{8,0},{16,24},{24,16},{1,9},{9,1},{17,25},{25,17},{2,10},{10... | collective-permute-start | bytes 786440 | tf_op jit(solution)/shard_map/ppermute | solution.py:427
  60.2 11.1 %collective-permute-start.13 = (f32[256,256]{1,0:T(8,128)S(1)}, f32[256,256]{1,0:T(8,128)S(1)}, u32[]{:S(2)}, u32[]{:S(2)}) collective-permute-start(f32[256,256]{1,0:T(8,128)S(1)} %get-tuple-element.59), channel_id=1, source_target_pairs={{0,8},{8,0},{16,24},{24,16},{1,9},{9,1},{17,25},{25,17},{2,10},{10... | collective-permute-start | bytes 786440 | tf_op jit(solution)/shard_map/ppermute | solution.py:427
  92.0 5.7 %collective-permute-start.18 = (f32[1,2,64,256]{3,2,1,0:T(8,128)S(1)}, f32[1,2,64,256]{3,2,1,0:T(8,128)S(1)}, u32[]{:S(2)}, u32[]{:S(2)}) collective-permute-start(f32[1,2,64,256]{3,2,1,0:T(8,128)S(1)} %slice.73), channel_id=1, source_target_pairs={{0,16},{8,24},{16,0},{24,8},{1,17},{9,25},{17,1},{25,9},{2,18},{10... | collective-permute-start | bytes 393224 | tf_op jit(solution)/shard_map/ppermute | solution.py:427
  97.7 14.9 %collective-permute-start.20 = (f32[2,256,256]{2,1,0:T(8,128)S(1)}, f32[2,256,256]{2,1,0:T(8,128)S(1)}, u32[]{:S(2)}, u32[]{:S(2)}) collective-permute-start(f32[2,256,256]{2,1,0:T(8,128)S(1)} %get-tuple-element.72), channel_id=1, source_target_pairs={{0,16},{8,24},{16,0},{24,8},{1,17},{9,25},{17,1},{25,9},{2,18},{10... | collective-permute-start | bytes 1572872 | tf_op jit(solution)/shard_map/ppermute | solution.py:427
  99.2 8.3 %collective-permute-start.21 = (f32[2,64,256]{2,1,0:T(8,128)S(1)}, f32[2,64,256]{2,1,0:T(8,128)S(1)}, u32[]{:S(2)}, u32[]{:S(2)}) collective-permute-start(f32[2,64,256]{2,1,0:T(8,128)S(1)} %fusion.refs_3_), channel_id=1, source_target_pairs={{0,4},{1,5},{2,6},{3,7},{4,0},{5,1},{6,2},{7,3},{8,12},{9,13},{10,... | collective-permute-start | bytes 393224 | tf_op jit(solution)/shard_map/ppermute | solution.py:427
  107.5 5.0 %collective-permute-start.22 = (f32[2,64,256]{2,1,0:T(8,128)S(1)}, f32[2,64,256]{2,1,0:T(8,128)S(1)}, u32[]{:S(2)}, u32[]{:S(2)}) collective-permute-start(f32[2,64,256]{2,1,0:T(8,128)S(1)} %add.29), channel_id=1, source_target_pairs={{0,2},{1,3},{2,0},{3,1},{4,6},{5,7},{6,4},{7,5},{8,10},{9,11},{10,... | collective-permute-start | bytes 393224 | tf_op jit(solution)/shard_map/ppermute | solution.py:427
  107.6 14.7 %collective-permute-start.16 = (f32[2,256,256]{2,1,0:T(8,128)S(1)}, f32[2,256,256]{2,1,0:T(8,128)S(1)}, u32[]{:S(2)}, u32[]{:S(2)}) collective-permute-start(f32[2,256,256]{2,1,0:T(8,128)S(1)} %get-tuple-element.64), channel_id=1, source_target_pairs={{0,16},{8,24},{16,0},{24,8},{1,17},{9,25},{17,1},{25,9},{2,18},{10... | collective-permute-start | bytes 1572872 | tf_op jit(solution)/shard_map/ppermute | solution.py:427
  108.1 10.5 %collective-permute-start.19 = (f32[256,256]{1,0:T(8,128)S(1)}, f32[256,256]{1,0:T(8,128)S(1)}, u32[]{:S(2)}, u32[]{:S(2)}) collective-permute-start(f32[256,256]{1,0:T(8,128)S(1)} %get-tuple-element.71), channel_id=1, source_target_pairs={{0,8},{8,0},{16,24},{24,16},{1,9},{9,1},{17,25},{25,17},{2,10},{10... | collective-permute-start | bytes 786440 | tf_op jit(solution)/shard_map/ppermute | solution.py:427
  112.6 6.0 %collective-permute-start.23 = (f32[256,256]{1,0:T(8,128)S(1)}, f32[256,256]{1,0:T(8,128)S(1)}, u32[]{:S(2)}, u32[]{:S(2)}) collective-permute-start(f32[256,256]{1,0:T(8,128)S(1)} %slice_bitcast_fusion.7), channel_id=1, source_target_pairs={{0,8},{8,0},{16,24},{24,16},{1,9},{9,1},{17,25},{25,17},{2,10},{10... | collective-permute-start | bytes 786440 | tf_op jit(solution)/shard_map/ppermute | solution.py:427
  112.7 5.9 %collective-permute-start.24 = (f32[2,64,256]{2,1,0:T(8,128)S(1)}, f32[2,64,256]{2,1,0:T(8,128)S(1)}, u32[]{:S(2)}, u32[]{:S(2)}) collective-permute-start(f32[2,64,256]{2,1,0:T(8,128)S(1)} %add.30.refs_1_), channel_id=1, source_target_pairs={{0,1},{1,0},{2,3},{3,2},{4,5},{5,4},{6,7},{7,6},{8,9},{9,8},{10,11... | collective-permute-start | bytes 393224 | tf_op jit(solution)/shard_map/ppermute | solution.py:427
  112.8 12.8 %collective-permute-start.25 = (f32[256,256]{1,0:T(8,128)S(1)}, f32[256,256]{1,0:T(8,128)S(1)}, u32[]{:S(2)}, u32[]{:S(2)}) collective-permute-start(f32[256,256]{1,0:T(8,128)S(1)} %get-tuple-element.75), channel_id=1, source_target_pairs={{0,8},{8,0},{16,24},{24,16},{1,9},{9,1},{17,25},{25,17},{2,10},{10... | collective-permute-start | bytes 786440 | tf_op jit(solution)/shard_map/ppermute | solution.py:427
  120.8 13.8 %collective-permute-start.30 = (f32[2,256,256]{2,1,0:T(8,128)S(1)}, f32[2,256,256]{2,1,0:T(8,128)S(1)}, u32[]{:S(2)}, u32[]{:S(2)}) collective-permute-start(f32[2,256,256]{2,1,0:T(8,128)S(1)} %get-tuple-element.85), channel_id=1, source_target_pairs={{0,16},{8,24},{16,0},{24,8},{1,17},{9,25},{17,1},{25,9},{2,18},{10... | collective-permute-start | bytes 1572872 | tf_op jit(solution)/shard_map/ppermute | solution.py:427
  122.3 3.3 %collective-permute-start.26 = (f32[256,256]{1,0:T(8,128)S(1)}, f32[256,256]{1,0:T(8,128)S(1)}, u32[]{:S(2)}, u32[]{:S(2)}) collective-permute-start(f32[256,256]{1,0:T(8,128)S(1)} %slice_bitcast_fusion.6), channel_id=1, source_target_pairs={{0,8},{8,0},{16,24},{24,16},{1,9},{9,1},{17,25},{25,17},{2,10},{10... | collective-permute-start | bytes 786440 | tf_op jit(solution)/shard_map/ppermute | solution.py:427
  122.4 16.6 %collective-permute-start.37 = (f32[256,512]{1,0:T(8,128)S(1)}, f32[256,512]{1,0:T(8,128)S(1)}, u32[]{:S(2)}, u32[]{:S(2)}) collective-permute-start(f32[256,512]{1,0:T(8,128)S(1)} %get-tuple-element.91), channel_id=1, source_target_pairs={{0,1},{1,2},{2,3},{3,4},{4,5},{5,6},{6,7},{8,9},{9,10},{10,11},{11... | collective-permute-start | bytes 1572872 | tf_op jit(solution)/shard_map/ppermute | solution.py:445
  127.7 22.6 %collective-permute-start.33 = (f32[256,512]{1,0:T(8,128)S(1)}, f32[256,512]{1,0:T(8,128)S(1)}, u32[]{:S(2)}, u32[]{:S(2)}) collective-permute-start(f32[256,512]{1,0:T(8,128)S(1)} %get-tuple-element.89), channel_id=1, source_target_pairs={{0,1},{1,2},{2,3},{3,4},{4,5},{5,6},{6,7},{8,9},{9,10},{10,11},{11... | collective-permute-start | bytes 1572872 | tf_op jit(solution)/shard_map/ppermute | solution.py:445
  131.4 18.9 %collective-permute-start.28 = (f32[2,256,256]{2,1,0:T(8,128)S(1)}, f32[2,256,256]{2,1,0:T(8,128)S(1)}, u32[]{:S(2)}, u32[]{:S(2)}) collective-permute-start(f32[2,256,256]{2,1,0:T(8,128)S(1)} %get-tuple-element.79), channel_id=1, source_target_pairs={{0,16},{8,24},{16,0},{24,8},{1,17},{9,25},{17,1},{25,9},{2,18},{10... | collective-permute-start | bytes 1572872 | tf_op jit(solution)/shard_map/ppermute | solution.py:427
  132.9 7.5 %collective-permute-start.29 = (f32[256,256]{1,0:T(8,128)S(1)}, f32[256,256]{1,0:T(8,128)S(1)}, u32[]{:S(2)}, u32[]{:S(2)}) collective-permute-start(f32[256,256]{1,0:T(8,128)S(1)} %get-tuple-element.84), channel_id=1, source_target_pairs={{0,8},{8,0},{16,24},{24,16},{1,9},{9,1},{17,25},{25,17},{2,10},{10... | collective-permute-start | bytes 786440 | tf_op jit(solution)/shard_map/ppermute | solution.py:427
  134.6 6.1 %collective-permute-start.31 = (f32[256,256]{1,0:T(8,128)S(1)}, f32[256,256]{1,0:T(8,128)S(1)}, u32[]{:S(2)}, u32[]{:S(2)}) collective-permute-start(f32[256,256]{1,0:T(8,128)S(1)} %slice_bitcast_fusion.5), channel_id=1, source_target_pairs={{0,8},{8,0},{16,24},{24,16},{1,9},{9,1},{17,25},{25,17},{2,10},{10... | collective-permute-start | bytes 786440 | tf_op jit(solution)/shard_map/ppermute | solution.py:427
  140.4 11.3 %collective-permute-start.27 = (f32[256,256]{1,0:T(8,128)S(1)}, f32[256,256]{1,0:T(8,128)S(1)}, u32[]{:S(2)}, u32[]{:S(2)}) collective-permute-start(f32[256,256]{1,0:T(8,128)S(1)} %get-tuple-element.78), channel_id=1, source_target_pairs={{0,8},{8,0},{16,24},{24,16},{1,9},{9,1},{17,25},{25,17},{2,10},{10... | collective-permute-start | bytes 786440 | tf_op jit(solution)/shard_map/ppermute | solution.py:427
  142.8 18.7 %collective-permute-start.40 = (f32[256,512]{1,0:T(8,128)S(1)}, f32[256,512]{1,0:T(8,128)S(1)}, u32[]{:S(2)}, u32[]{:S(2)}) collective-permute-start(f32[256,512]{1,0:T(8,128)S(1)} %gate.22), channel_id=1, source_target_pairs={{0,1},{1,2},{2,3},{3,4},{4,5},{5,6},{6,7},{8,9},{9,10},{10,11},{11... | collective-permute-start | bytes 1572872 | tf_op jit(solution)/shard_map/ppermute | solution.py:445
  151.4 2.7 %collective-permute-start.35 = (f32[8,128]{1,0:T(8,128)S(1)}, f32[8,128]{1,0:T(8,128)S(1)}, u32[]{:S(2)}, u32[]{:S(2)}) collective-permute-start(f32[8,128]{1,0:T(8,128)S(1)} %collective-permute-done.34), channel_id=1, source_target_pairs={{0,8},{8,0},{16,24},{24,16},{1,9},{9,1},{17,25},{25,17},{2,10},{10... | collective-permute-start | bytes 12296 | tf_op jit(solution)/shard_map/ppermute | solution.py:427
  154.1 18.2 %collective-permute-start.36 = (f32[256,512]{1,0:T(8,128)S(1)}, f32[256,512]{1,0:T(8,128)S(1)}, u32[]{:S(2)}, u32[]{:S(2)}) collective-permute-start(f32[256,512]{1,0:T(8,128)S(1)} %gate.21), channel_id=1, source_target_pairs={{0,1},{1,2},{2,3},{3,4},{4,5},{5,6},{6,7},{8,9},{9,10},{10,11},{11... | collective-permute-start | bytes 1572872 | tf_op jit(solution)/shard_map/ppermute | solution.py:445
  (17 other events, 100.0 us)

commit v3 on v2

--- a/solution.py
+++ b/solution.py
@@ -143,13 +143,29 @@
         copy.wait()
 
 
-def place_kernel(peers, ids, positions, *rest):
+def strip_kernel(planes, waits, strips, *rest):
+    outs = rest[waits : waits + len(planes)]
+    held, moved = rest[waits + len(planes) :]
+    loads, stores = [], []
+    for i, plane in enumerate(planes):
+        loads.append(pltpu.make_async_copy(strips.at[plane[0], plane[1]], held.at[i], moved.at[i]))
+        stores.append(pltpu.make_async_copy(held.at[i], outs[i], moved.at[i]))
+    for copy in loads:
+        copy.start()
+    for load, store in zip(loads, stores):
+        load.wait()
+        store.start()
+    for copy in stores:
+        copy.wait()
+
+
+def place_kernel(peers, waits, ids, positions, *rest):
     own_in, near_in = rest[:2]
     far_ins = rest[2:peers]
     pieces = [own_in, near_in]
     for i in range(0, len(far_ins), 2):
         pieces += [far_ins[i].at[0], far_ins[i + 1]]
-    own, rim, ext, got, loaded, stored = rest[peers:]
+    own, rim, ext, got, loaded, stored = rest[peers + waits :]
     rows, cols = own.shape
     blocks = cols // LANES
     size = own_in.shape[-1]
@@ -465,7 +481,21 @@
 
     chunks = [(j, part) for j in range(per_device) for part in range(2)]
     ahead = 2
-    strips = [transmission[c[0], c[1]] for c in chunks]
+
+    def strips_of(planes, waits):
+        return run_kernel(
+            functools.partial(strip_kernel, planes, len(waits)),
+            "strip",
+            (shape(rows, cols),) * len(planes),
+            [HBM_SPEC] * (1 + len(waits)),
+            (HBM_SPEC,) * len(planes),
+            [pltpu.VMEM((len(planes), rows, cols), F32), pltpu.SemaphoreType.DMA((len(planes),))],
+            1,
+            56,
+        )(transmission, *waits)
+
+    strips = list(strips_of(chunks[:1], []))
+    strips += strips_of(chunks[1:], strips[:1])
     group = (shape(size, size),) * 2 + (shape(2, size, size),) * (peers // 2 - 1)
     groups = len(group)
     crops = []
@@ -487,7 +517,8 @@
             2,
         )(ids, scan_positions, transmission, rim, *waits)
         strips[k + ahead : k + ahead + 1] = gate(strips[k + ahead : k + ahead + 1], mine[:1])
-        crops.append(exchanged(mine))
+        early = [x for got in crops[:-1] for x in got[1:2] + got[3::2]] if k == len(chunks) - 1 else []
+        crops.append(exchanged(mine, early))
     layers = per_device * peers
     result = run_kernel(
         functools.partial(optics_kernel, peers, per_device),
@@ -534,14 +565,15 @@
         if k >= ahead:
             mine = gate(mine, returned[k - ahead][2::2] + [own[order[k - ahead]]])
         before = [own[order[k - 1]]] if k else probe_steps[-2:-1]
-        if k == 1:
-            before.append(probe_steps[-1])
+        if k >= ahead:
+            before.append(rim_back[order[k - ahead]])
         returned.append(exchanged(mine, before))
+        waits = [swap(probe_steps[-1], "depth", 1)] if k == 1 else []
         mine = run_kernel(
-            functools.partial(place_kernel, peers),
+            functools.partial(place_kernel, peers, len(waits)),
             "place",
             (shape(rows, cols), shape(rows, cols)),
-            [SMEM_SPEC, SMEM_SPEC] + [HBM_SPEC] * peers,
+            [SMEM_SPEC, SMEM_SPEC] + [HBM_SPEC] * (peers + len(waits)),
             (HBM_SPEC, HBM_SPEC),
             [
                 pltpu.VMEM((cols // LANES + 1, 2 * rows, LANES), F32),
@@ -550,7 +582,7 @@
                 pltpu.SemaphoreType.DMA((2 * cols // LANES,)),
             ],
             2,
-        )(ids, scan_positions, *returned[k])
+        )(ids, scan_positions, *returned[k], *waits)
         own[c], outside = mine[:2]
         if k >= ahead:
             (outside,) = gate([outside], [echo(echo(rim_back[order[k - ahead]]))])

time: 175 us -> 169 us (0.966)
  waiting for transfers between devices: 84.7 us -> 76 us
  Pallas kernels: 38.8 us -> 43.5 us
  local copies, waits for them, and re-layouts: 5.36 us -> 1.34 us
    ppermute x8, waiting for transfers between devices: 44.4 us -> 38 us  [shift(): lax.ppermute(x, axis, [(i, i + by) for i in range(peers) if 0 <= i + by <...]
    pallas_call x4 -> x6, Pallas kernels: 8.2 us -> 12.4 us  [the longest x4 8.2 us: body(): run_kernel(functools.partial(place_kernel, peers, len(waits)), 'place', (...]
    squeeze x1 -> x0, local copies, waits for them, and re-layouts: 2.81 us -> none  [body(): strips = [transmission[c[0], c[1]] for c in chunks]]
    ppermute x34 -> x35, waiting for transfers between devices: 40.3 us -> 38 us  [swap(): return lax.ppermute(x, axis, [(i, i ^ offset) for i in range(peers)])]
    ppermute x34 -> x35, starting transfers between devices: 19.2 us -> 20.3 us  [swap(): return lax.ppermute(x, axis, [(i, i ^ offset) for i in range(peers)])]
  transfers between devices with their start and end apart: 42 -> 43, of which waited for: 25 -> 26; matrix products, arithmetic and copies ran while one was open for 0% -> 0% of each run, Pallas kernels for 12% -> 14%
where the time goes in v3:
time: 169 us; the launch traced here: 167 us
  waiting for transfers between devices  76 us (45%)
  Pallas kernels  43.5 us (26%)
  starting transfers between devices  43.3 us (26%)
  other arithmetic  2.16 us (1%)
    ppermute x8, waiting for transfers between devices, shift(): lax.ppermute(x, axis, [(i, i + by) for i in range(peers) if 0 <= i + by <...  38 us
    ppermute x35, waiting for transfers between devices, swap(): return lax.ppermute(x, axis, [(i, i ^ offset) for i in range(peers)])  38 us
    ppermute x8, starting transfers between devices, shift(): lax.ppermute(x, axis, [(i, i + by) for i in range(peers) if 0 <= i + by <...  23.1 us
    ppermute x35, starting transfers between devices, swap(): return lax.ppermute(x, axis, [(i, i ^ offset) for i in range(peers)])  20.3 us
    pallas_call x1, Pallas kernels, body(): run_kernel(functools.partial(optics_kernel, peers, per_device), 'optics',...  17.9 us
    pallas_call x4, Pallas kernels, body(): run_kernel(functools.partial(crop_kernel, peers, c, len(waits)), 'crop',...  11.8 us
    pallas_call x4, Pallas kernels, body(): run_kernel(functools.partial(place_kernel, peers, len(waits)), 'place', (...  8.2 us
    pallas_call x2, Pallas kernels, strips_of(): run_kernel(functools.partial(strip_kernel, planes, len(waits)), 'strip',...  4.18 us
  transfers between devices with their start and end apart: 43, of which 26 were waited for; matrix products, arithmetic and copies ran while one was open for 0% of the time, Pallas kernels for 14%

profile of v3, /device:TPU:4, one launch (start us, length us, event | category | flops | bytes accessed | tf_op | source)
XLA Modules:
  0.0 167.4 jit_solution(18089319354367229473)
XLA Ops:
  0.6 1.9 %strip.2.rest_0_ = f32[256,512]{1,0:T(8,128)} custom-call(f32[2,2,256,512]{3,2,1,0:T(8,128)} %strips.11), custom_call_target="tpu_custom_call" | custom-call | flops 1000000 | bytes 1000 | tf_op jit(solution)/shard_map/strip/pallas_call | solution.py:486
  2.6 2.1 %collective-permute-start = (f32[256,512]{1,0:T(8,128)}, f32[256,512]{1,0:T(8,128)}, u32[]{:S(2)}, u32[]{:S(2)}) collective-permute-start(f32[256,512]{1,0:T(8,128)} %strip.2.rest_0_), channel_id=1, source_target_pairs={{1,0},{2,1},{3,2},{4,3},{5,4},{6,5},{7,6},{9,8},{10,9},{11,10},{12... | collective-permute-start | bytes 1572872 | tf_op jit(solution)/shard_map/ppermute | solution.py:461
  4.7 2.3 %strip.3 = (f32[256,512]{1,0:T(8,128)}, f32[256,512]{1,0:T(8,128)}, f32[256,512]{1,0:T(8,128)}) custom-call(f32[2,2,256,512]{3,2,1,0:T(8,128)} %strips.11, f32[256,512]{1,0:T(8,128)} %strip.2.rest_0_), custom_call_target="tpu_custom_call" | custom-call | flops 1000000 | bytes 1000 | tf_op jit(solution)/shard_map/strip/pallas_call | solution.py:486
  6.9 1.9 %collective-permute-start.4 = (f32[256,512]{1,0:T(8,128)}, f32[256,512]{1,0:T(8,128)}, u32[]{:S(2)}, u32[]{:S(2)}) collective-permute-start(f32[256,512]{1,0:T(8,128)} %get-tuple-element.55), channel_id=1, source_target_pairs={{1,0},{2,1},{3,2},{4,3},{5,4},{6,5},{7,6},{9,8},{10,9},{11,10},{12... | collective-permute-start | bytes 1572872 | tf_op jit(solution)/shard_map/ppermute | solution.py:461
  11.4 9.2 %collective-permute-done.rim = f32[256,512]{1,0:T(8,128)} collective-permute-done((f32[256,512]{1,0:T(8,128)}, f32[256,512]{1,0:T(8,128)}, u32[]{:S(2)}, u32[]{:S(2)}) %collective-permute-start) | collective-permute-done | bytes 524320 | tf_op jit(solution)/shard_map/ppermute | solution.py:461
  20.7 3.4 %crop.4 = (f32[256,256]{1,0:T(8,128)S(1)}, f32[256,256]{1,0:T(8,128)S(1)}, f32[2,256,256]{2,1,0:T(8,128)S(1)}) custom-call(s32[2]{0:T(128)S(1)} %pad_add_fusion.ids, s32[4,2]{1,0:T(4,128)S(1)} %copy.34.positions, f32[2,2,256,512]{3,2,1,0:T(8,128)S(1)} %copy-done, f32[256,512]{1,0:T(8,128)} %collective-permute-done.rim, ...), custom_call_target="tpu_custom_call" | custom-call | flops 2000000 | bytes 2000 | tf_op jit(solution)/shard_map/crop/pallas_call | solution.py:505
  25.7 2.0 %collective-permute-start.8 = (f32[256,512]{1,0:T(8,128)S(1)}, f32[256,512]{1,0:T(8,128)S(1)}, u32[]{:S(2)}, u32[]{:S(2)}) collective-permute-start(f32[256,512]{1,0:T(8,128)S(1)} %gate.13), channel_id=1, source_target_pairs={{1,0},{2,1},{3,2},{4,3},{5,4},{6,5},{7,6},{9,8},{10,9},{11,10},{12... | collective-permute-start | bytes 1572872 | tf_op jit(solution)/shard_map/ppermute | solution.py:461
  27.7 4.2 %collective-permute-done.4.rim = f32[256,512]{1,0:T(8,128)} collective-permute-done((f32[256,512]{1,0:T(8,128)}, f32[256,512]{1,0:T(8,128)}, u32[]{:S(2)}, u32[]{:S(2)}) %collective-permute-start.4) | collective-permute-done | bytes 524320 | tf_op jit(solution)/shard_map/ppermute | solution.py:461
  31.9 3.4 %crop.5 = (f32[256,256]{1,0:T(8,128)S(1)}, f32[256,256]{1,0:T(8,128)S(1)}, f32[2,256,256]{2,1,0:T(8,128)S(1)}) custom-call(s32[2]{0:T(128)S(1)} %pad_add_fusion.ids, s32[4,2]{1,0:T(4,128)S(1)} %copy.34.positions, f32[2,2,256,512]{3,2,1,0:T(8,128)S(1)} %copy-done, f32[256,512]{1,0:T(8,128)} %collective-permute-done.4.rim, ...), custom_call_target="tpu_custom_call" | custom-call | flops 2000000 | bytes 2000 | tf_op jit(solution)/shard_map/crop/pallas_call | solution.py:505
  38.8 4.6 %collective-permute-done.8.rim = f32[256,512]{1,0:T(8,128)S(1)} collective-permute-done((f32[256,512]{1,0:T(8,128)S(1)}, f32[256,512]{1,0:T(8,128)S(1)}, u32[]{:S(2)}, u32[]{:S(2)}) %collective-permute-start.8) | collective-permute-done | bytes 524320 | tf_op jit(solution)/shard_map/ppermute | solution.py:461
  43.4 2.5 %crop.6 = (f32[256,256]{1,0:T(8,128)S(1)}, f32[256,256]{1,0:T(8,128)S(1)}, f32[2,256,256]{2,1,0:T(8,128)S(1)}) custom-call(s32[2]{0:T(128)S(1)} %pad_add_fusion.ids, s32[4,2]{1,0:T(4,128)S(1)} %copy.34.positions, f32[2,2,256,512]{3,2,1,0:T(8,128)S(1)} %copy-done, f32[256,512]{1,0:T(8,128)S(1)} %collective-permute-done.8.rim, ...), custom_call_target="tpu_custom_call" | custom-call | flops 2000000 | bytes 2000 | tf_op jit(solution)/shard_map/crop/pallas_call | solution.py:505
  48.3 4.8 %collective-permute-done.12.rim = f32[256,512]{1,0:T(8,128)S(1)} collective-permute-done((f32[256,512]{1,0:T(8,128)S(1)}, f32[256,512]{1,0:T(8,128)S(1)}, u32[]{:S(2)}, u32[]{:S(2)}) %collective-permute-start.12) | collective-permute-done | bytes 524320 | tf_op jit(solution)/shard_map/ppermute | solution.py:461
  53.1 2.5 %crop.7 = (f32[256,256]{1,0:T(8,128)S(1)}, f32[256,256]{1,0:T(8,128)S(1)}, f32[2,256,256]{2,1,0:T(8,128)S(1)}) custom-call(s32[2]{0:T(128)S(1)} %pad_add_fusion.ids, s32[4,2]{1,0:T(4,128)S(1)} %copy.34.positions, f32[2,2,256,512]{3,2,1,0:T(8,128)S(1)} %copy-done, f32[256,512]{1,0:T(8,128)S(1)} %collective-permute-done.12.rim, ...), custom_call_target="tpu_custom_call" | custom-call | flops 2000000 | bytes 2000 | tf_op jit(solution)/shard_map/crop/pallas_call | solution.py:505
  57.3 2.2 %collective-permute-done.10.rest_10_ = f32[2,256,256]{2,1,0:T(8,128)S(1)} collective-permute-done((f32[2,256,256]{2,1,0:T(8,128)S(1)}, f32[2,256,256]{2,1,0:T(8,128)S(1)}, u32[]{:S(2)}, u32[]{:S(2)}) %collective-permute-start.10) | collective-permute-done | bytes 524320 | tf_op jit(solution)/shard_map/ppermute | solution.py:443
  61.0 8.5 %collective-permute-done.14.refs_0_ = f32[2,256,256]{2,1,0:T(8,128)S(1)} collective-permute-done((f32[2,256,256]{2,1,0:T(8,128)S(1)}, f32[2,256,256]{2,1,0:T(8,128)S(1)}, u32[]{:S(2)}, u32[]{:S(2)}) %collective-permute-start.14) | collective-permute-done | bytes 524320 | tf_op jit(solution)/shard_map/ppermute | solution.py:443
  71.1 17.9 %optics.1 = (f32[256,256]{1,0:T(8,128)S(1)}, f32[256,256]{1,0:T(8,128)S(1)}, f32[2,256,256]{2,1,0:T(8,128)S(1)}, f32[256,256]{1,0:T(8,128)S(1)}, f32[256,256]{1,...) custom-call(s32[2]{0:T(128)S(1)} %pad_add_fusion.ids, ...), custom_call_target="tpu_custom_call" | custom-call | flops 15000000 | bytes 15000 | tf_op jit(solution)/shard_map/optics/pallas_call | solution.py:523
  92.3 4.1 %collective-permute-done.18 = f32[1,2,64,256]{3,2,1,0:T(8,128)S(1)} collective-permute-done((f32[1,2,64,256]{3,2,1,0:T(8,128)S(1)}, f32[1,2,64,256]{3,2,1,0:T(8,128)S(1)}, u32[]{:S(2)}, u32[]{:S(2)}) %collective-permute-start.18) | collective-permute-done | bytes 131104 | tf_op jit(solution)/shard_map/ppermute | solution.py:443
  97.9 2.6 %collective-permute-start.21 = (f32[2,64,256]{2,1,0:T(8,128)S(1)}, f32[2,64,256]{2,1,0:T(8,128)S(1)}, u32[]{:S(2)}, u32[]{:S(2)}) collective-permute-start(f32[2,64,256]{2,1,0:T(8,128)S(1)} %fusion.refs_3_), channel_id=1, source_target_pairs={{0,4},{1,5},{2,6},{3,7},{4,0},{5,1},{6,2},{7,3},{8,12},{9,13},{10,... | collective-permute-start | bytes 393224 | tf_op jit(solution)/shard_map/ppermute | solution.py:443
  100.5 5.6 %collective-permute-done.21 = f32[2,64,256]{2,1,0:T(8,128)S(1)} collective-permute-done((f32[2,64,256]{2,1,0:T(8,128)S(1)}, f32[2,64,256]{2,1,0:T(8,128)S(1)}, u32[]{:S(2)}, u32[]{:S(2)}) %collective-permute-start.21) | collective-permute-done | bytes 131104 | tf_op jit(solution)/shard_map/ppermute | solution.py:443
  106.8 4.3 %collective-permute-done.22 = f32[2,64,256]{2,1,0:T(8,128)S(1)} collective-permute-done((f32[2,64,256]{2,1,0:T(8,128)S(1)}, f32[2,64,256]{2,1,0:T(8,128)S(1)}, u32[]{:S(2)}, u32[]{:S(2)}) %collective-permute-start.22) | collective-permute-done | bytes 131104 | tf_op jit(solution)/shard_map/ppermute | solution.py:443
  112.9 2.0 %place.4 = (f32[256,512]{1,0:T(8,128)S(1)}, f32[256,512]{1,0:T(8,128)S(1)}) custom-call(s32[2]{0:T(128)S(1)} %pad_add_fusion.ids, s32[4,2]{1,0:T(4,128)S(1)} %copy.34.positions, f32[256,256]{1,0:T(8,128)S(1)} %get-tuple-element.76.rest_0_, f32[256,256]{1,0:T(8,128)S(1)} %collective-permute-done.19.rest_1_, f32[2,256,256]{2,1,0:T(8,128)S(1)} %gate.17.rest_2_.refs_3_, ...), custom_call_target="tpu_custom_call" | custom-call | flops 2000000 | bytes 2000 | tf_op jit(solution)/shard_map/place/pallas_call | solution.py:572
  116.5 3.9 %collective-permute-start.32 = (f32[256,512]{1,0:T(8,128)S(1)}, f32[256,512]{1,0:T(8,128)S(1)}, u32[]{:S(2)}, u32[]{:S(2)}) collective-permute-start(f32[256,512]{1,0:T(8,128)S(1)} %get-tuple-element.92), channel_id=1, source_target_pairs={{0,1},{1,2},{2,3},{3,4},{4,5},{5,6},{6,7},{8,9},{9,10},{10,11},{11... | collective-permute-start | bytes 1572872 | tf_op jit(solution)/shard_map/ppermute | solution.py:461
  120.4 2.1 %collective-permute-done.16.refs_0_ = f32[2,256,256]{2,1,0:T(8,128)S(1)} collective-permute-done((f32[2,256,256]{2,1,0:T(8,128)S(1)}, f32[2,256,256]{2,1,0:T(8,128)S(1)}, u32[]{:S(2)}, u32[]{:S(2)}) %collective-permute-start.16) | collective-permute-done | bytes 524320 | tf_op jit(solution)/shard_map/ppermute | solution.py:443
  124.3 2.0 %place.5 = (f32[256,512]{1,0:T(8,128)S(1)}, f32[256,512]{1,0:T(8,128)S(1)}) custom-call(s32[2]{0:T(128)S(1)} %pad_add_fusion.ids, s32[4,2]{1,0:T(4,128)S(1)} %copy.34.positions, f32[256,256]{1,0:T(8,128)S(1)} %get-tuple-element.80.rest_0_, f32[256,256]{1,0:T(8,128)S(1)} %collective-permute-done.24.rest_1_, f32[2,256,256]{2,1,0:T(8,128)S(1)} %gate.18.rest_2_.refs_3_, ...), custom_call_target="tpu_custom_call" | custom-call | flops 2000000 | bytes 2000 | tf_op jit(solution)/shard_map/place/pallas_call | solution.py:572
  126.4 2.5 %collective-permute-start.34 = (f32[256,512]{1,0:T(8,128)S(1)}, f32[256,512]{1,0:T(8,128)S(1)}, u32[]{:S(2)}, u32[]{:S(2)}) collective-permute-start(f32[256,512]{1,0:T(8,128)S(1)} %get-tuple-element.94), channel_id=1, source_target_pairs={{0,1},{1,2},{2,3},{3,4},{4,5},{5,6},{6,7},{8,9},{9,10},{10,11},{11... | collective-permute-start | bytes 1572872 | tf_op jit(solution)/shard_map/ppermute | solution.py:461
  130.5 2.0 %collective-permute-done.31.refs_0_ = f32[2,256,256]{2,1,0:T(8,128)S(1)} collective-permute-done((f32[2,256,256]{2,1,0:T(8,128)S(1)}, f32[2,256,256]{2,1,0:T(8,128)S(1)}, u32[]{:S(2)}, u32[]{:S(2)}) %collective-permute-start.31) | collective-permute-done | bytes 524320 | tf_op jit(solution)/shard_map/ppermute | solution.py:443
  135.1 2.0 %place.6 = (f32[256,512]{1,0:T(8,128)S(1)}, f32[256,512]{1,0:T(8,128)S(1)}) custom-call(s32[2]{0:T(128)S(1)} %pad_add_fusion.ids, s32[4,2]{1,0:T(4,128)S(1)} %copy.34.positions, f32[256,256]{1,0:T(8,128)S(1)} %get-tuple-element.89.rest_0_, f32[256,256]{1,0:T(8,128)S(1)} %collective-permute-done.30.rest_1_, f32[2,256,256]{2,1,0:T(8,128)S(1)} %gate.21.rest_2_, ...), custom_call_target="tpu_custom_call" | custom-call | flops 2000000 | bytes 2000 | tf_op jit(solution)/shard_map/place/pallas_call | solution.py:572
  137.2 5.1 %collective-permute-start.41 = (f32[256,512]{1,0:T(8,128)S(1)}, f32[256,512]{1,0:T(8,128)S(1)}, u32[]{:S(2)}, u32[]{:S(2)}) collective-permute-start(f32[256,512]{1,0:T(8,128)S(1)} %gate.24), channel_id=1, source_target_pairs={{0,1},{1,2},{2,3},{3,4},{4,5},{5,6},{6,7},{8,9},{9,10},{10,11},{11... | collective-permute-start | bytes 1572872 | tf_op jit(solution)/shard_map/ppermute | solution.py:461
  146.0 2.0 %place.7 = (f32[256,512]{1,0:T(8,128)S(1)}, f32[256,512]{1,0:T(8,128)S(1)}) custom-call(s32[2]{0:T(128)S(1)} %pad_add_fusion.ids, s32[4,2]{1,0:T(4,128)S(1)} %copy.34.positions, f32[256,256]{1,0:T(8,128)S(1)} %get-tuple-element.83.rest_0_, f32[256,256]{1,0:T(8,128)S(1)} %collective-permute-done.28.rest_1_, f32[2,256,256]{2,1,0:T(8,128)S(1)} %gate.22.rest_2_, ...), custom_call_target="tpu_custom_call" | custom-call | flops 2000000 | bytes 2000 | tf_op jit(solution)/shard_map/place/pallas_call | solution.py:572
  148.1 3.6 %collective-permute-start.38 = (f32[256,512]{1,0:T(8,128)S(1)}, f32[256,512]{1,0:T(8,128)S(1)}, u32[]{:S(2)}, u32[]{:S(2)}) collective-permute-start(f32[256,512]{1,0:T(8,128)S(1)} %gate.23), channel_id=1, source_target_pairs={{0,1},{1,2},{2,3},{3,4},{4,5},{5,6},{6,7},{8,9},{9,10},{10,11},{11... | collective-permute-start | bytes 1572872 | tf_op jit(solution)/shard_map/ppermute | solution.py:461
  151.8 3.7 %collective-permute-done.41.refs_0_ = f32[256,512]{1,0:T(8,128)S(1)} collective-permute-done((f32[256,512]{1,0:T(8,128)S(1)}, f32[256,512]{1,0:T(8,128)S(1)}, u32[]{:S(2)}, u32[]{:S(2)}) %collective-permute-start.41) | collective-permute-done | bytes 524320 | tf_op jit(solution)/shard_map/ppermute | solution.py:461
  156.7 9.1 %collective-permute-done.38 = f32[256,512]{1,0:T(8,128)S(1)} collective-permute-done((f32[256,512]{1,0:T(8,128)S(1)}, f32[256,512]{1,0:T(8,128)S(1)}, u32[]{:S(2)}, u32[]{:S(2)}) %collective-permute-start.38) | collective-permute-done | bytes 524320 | tf_op jit(solution)/shard_map/ppermute | solution.py:461
  (123 shorter events, 36.2 us)
Async XLA Ops:
  2.6 18.1 %collective-permute-start = (f32[256,512]{1,0:T(8,128)}, f32[256,512]{1,0:T(8,128)}, u32[]{:S(2)}, u32[]{:S(2)}) collective-permute-start(f32[256,512]{1,0:T(8,128)} %strip.2.rest_0_), channel_id=1, source_target_pairs={{1,0},{2,1},{3,2},{4,3},{5,4},{6,5},{7,6},{9,8},{10,9},{11,10},{12... | collective-permute-start | bytes 1572872 | tf_op jit(solution)/shard_map/ppermute | solution.py:461
  6.9 25.0 %collective-permute-start.4 = (f32[256,512]{1,0:T(8,128)}, f32[256,512]{1,0:T(8,128)}, u32[]{:S(2)}, u32[]{:S(2)}) collective-permute-start(f32[256,512]{1,0:T(8,128)} %get-tuple-element.55), channel_id=1, source_target_pairs={{1,0},{2,1},{3,2},{4,3},{5,4},{6,5},{7,6},{9,8},{10,9},{11,10},{12... | collective-permute-start | bytes 1572872 | tf_op jit(solution)/shard_map/ppermute | solution.py:461
  24.1 14.7 %collective-permute-start.2 = (f32[2,256,256]{2,1,0:T(8,128)S(1)}, f32[2,256,256]{2,1,0:T(8,128)S(1)}, u32[]{:S(2)}, u32[]{:S(2)}) collective-permute-start(f32[2,256,256]{2,1,0:T(8,128)S(1)} %get-tuple-element.54), channel_id=1, source_target_pairs={{0,16},{8,24},{16,0},{24,8},{1,17},{9,25},{17,1},{25,9},{2,18},{10... | collective-permute-start | bytes 1572872 | tf_op jit(solution)/shard_map/ppermute | solution.py:443
  25.7 17.8 %collective-permute-start.8 = (f32[256,512]{1,0:T(8,128)S(1)}, f32[256,512]{1,0:T(8,128)S(1)}, u32[]{:S(2)}, u32[]{:S(2)}) collective-permute-start(f32[256,512]{1,0:T(8,128)S(1)} %gate.13), channel_id=1, source_target_pairs={{1,0},{2,1},{3,2},{4,3},{5,4},{6,5},{7,6},{9,8},{10,9},{11,10},{12... | collective-permute-start | bytes 1572872 | tf_op jit(solution)/shard_map/ppermute | solution.py:461
  35.3 13.0 %collective-permute-start.6 = (f32[2,256,256]{2,1,0:T(8,128)S(1)}, f32[2,256,256]{2,1,0:T(8,128)S(1)}, u32[]{:S(2)}, u32[]{:S(2)}) collective-permute-start(f32[2,256,256]{2,1,0:T(8,128)S(1)} %get-tuple-element.58), channel_id=1, source_target_pairs={{0,16},{8,24},{16,0},{24,8},{1,17},{9,25},{17,1},{25,9},{2,18},{10... | collective-permute-start | bytes 1572872 | tf_op jit(solution)/shard_map/ppermute | solution.py:443
  36.9 16.2 %collective-permute-start.12 = (f32[256,512]{1,0:T(8,128)S(1)}, f32[256,512]{1,0:T(8,128)S(1)}, u32[]{:S(2)}, u32[]{:S(2)}) collective-permute-start(f32[256,512]{1,0:T(8,128)S(1)} %gate.14), channel_id=1, source_target_pairs={{1,0},{2,1},{3,2},{4,3},{5,4},{6,5},{7,6},{9,8},{10,9},{11,10},{12... | collective-permute-start | bytes 1572872 | tf_op jit(solution)/shard_map/ppermute | solution.py:461
  45.9 13.6 %collective-permute-start.10 = (f32[2,256,256]{2,1,0:T(8,128)S(1)}, f32[2,256,256]{2,1,0:T(8,128)S(1)}, u32[]{:S(2)}, u32[]{:S(2)}) collective-permute-start(f32[2,256,256]{2,1,0:T(8,128)S(1)} %get-tuple-element.62), channel_id=1, source_target_pairs={{0,16},{8,24},{16,0},{24,8},{1,17},{9,25},{17,1},{25,9},{2,18},{10... | collective-permute-start | bytes 1572872 | tf_op jit(solution)/shard_map/ppermute | solution.py:443
  47.1 12.5 %collective-permute-start.1 = (f32[256,256]{1,0:T(8,128)S(1)}, f32[256,256]{1,0:T(8,128)S(1)}, u32[]{:S(2)}, u32[]{:S(2)}) collective-permute-start(f32[256,256]{1,0:T(8,128)S(1)} %get-tuple-element.53), channel_id=1, source_target_pairs={{0,8},{8,0},{16,24},{24,16},{1,9},{9,1},{17,25},{25,17},{2,10},{10... | collective-permute-start | bytes 786440 | tf_op jit(solution)/shard_map/ppermute | solution.py:443
  47.1 13.0 %collective-permute-start.5 = (f32[256,256]{1,0:T(8,128)S(1)}, f32[256,256]{1,0:T(8,128)S(1)}, u32[]{:S(2)}, u32[]{:S(2)}) collective-permute-start(f32[256,256]{1,0:T(8,128)S(1)} %get-tuple-element.57), channel_id=1, source_target_pairs={{0,8},{8,0},{16,24},{24,16},{1,9},{9,1},{17,25},{25,17},{2,10},{10... | collective-permute-start | bytes 786440 | tf_op jit(solution)/shard_map/ppermute | solution.py:443
  55.6 13.9 %collective-permute-start.14 = (f32[2,256,256]{2,1,0:T(8,128)S(1)}, f32[2,256,256]{2,1,0:T(8,128)S(1)}, u32[]{:S(2)}, u32[]{:S(2)}) collective-permute-start(f32[2,256,256]{2,1,0:T(8,128)S(1)} %get-tuple-element.66), channel_id=1, source_target_pairs={{0,16},{8,24},{16,0},{24,8},{1,17},{9,25},{17,1},{25,9},{2,18},{10... | collective-permute-start | bytes 1572872 | tf_op jit(solution)/shard_map/ppermute | solution.py:443
  57.2 3.0 %collective-permute-start.3 = (f32[256,256]{1,0:T(8,128)S(1)}, f32[256,256]{1,0:T(8,128)S(1)}, u32[]{:S(2)}, u32[]{:S(2)}) collective-permute-start(f32[256,256]{1,0:T(8,128)S(1)} %slice_bitcast_fusion.7), channel_id=1, source_target_pairs={{0,8},{8,0},{16,24},{24,16},{1,9},{9,1},{17,25},{25,17},{2,10},{10... | collective-permute-start | bytes 786440 | tf_op jit(solution)/shard_map/ppermute | solution.py:443
  59.5 10.1 %collective-permute-start.9 = (f32[256,256]{1,0:T(8,128)S(1)}, f32[256,256]{1,0:T(8,128)S(1)}, u32[]{:S(2)}, u32[]{:S(2)}) collective-permute-start(f32[256,256]{1,0:T(8,128)S(1)} %get-tuple-element.61), channel_id=1, source_target_pairs={{0,8},{8,0},{16,24},{24,16},{1,9},{9,1},{17,25},{25,17},{2,10},{10... | collective-permute-start | bytes 786440 | tf_op jit(solution)/shard_map/ppermute | solution.py:443
  60.1 9.5 %collective-permute-start.13 = (f32[256,256]{1,0:T(8,128)S(1)}, f32[256,256]{1,0:T(8,128)S(1)}, u32[]{:S(2)}, u32[]{:S(2)}) collective-permute-start(f32[256,256]{1,0:T(8,128)S(1)} %get-tuple-element.65), channel_id=1, source_target_pairs={{0,8},{8,0},{16,24},{24,16},{1,9},{9,1},{17,25},{25,17},{2,10},{10... | collective-permute-start | bytes 786440 | tf_op jit(solution)/shard_map/ppermute | solution.py:443
  60.2 9.4 %collective-permute-start.11 = (f32[256,256]{1,0:T(8,128)S(1)}, f32[256,256]{1,0:T(8,128)S(1)}, u32[]{:S(2)}, u32[]{:S(2)}) collective-permute-start(f32[256,256]{1,0:T(8,128)S(1)} %slice_bitcast_fusion.5), channel_id=1, source_target_pairs={{0,8},{8,0},{16,24},{24,16},{1,9},{9,1},{17,25},{25,17},{2,10},{10... | collective-permute-start | bytes 786440 | tf_op jit(solution)/shard_map/ppermute | solution.py:443
  90.7 5.6 %collective-permute-start.18 = (f32[1,2,64,256]{3,2,1,0:T(8,128)S(1)}, f32[1,2,64,256]{3,2,1,0:T(8,128)S(1)}, u32[]{:S(2)}, u32[]{:S(2)}) collective-permute-start(f32[1,2,64,256]{3,2,1,0:T(8,128)S(1)} %slice.57), channel_id=1, source_target_pairs={{0,16},{8,24},{16,0},{24,8},{1,17},{9,25},{17,1},{25,9},{2,18},{10... | collective-permute-start | bytes 393224 | tf_op jit(solution)/shard_map/ppermute | solution.py:443
  96.3 14.9 %collective-permute-start.20 = (f32[2,256,256]{2,1,0:T(8,128)S(1)}, f32[2,256,256]{2,1,0:T(8,128)S(1)}, u32[]{:S(2)}, u32[]{:S(2)}) collective-permute-start(f32[2,256,256]{2,1,0:T(8,128)S(1)} %get-tuple-element.78), channel_id=1, source_target_pairs={{0,16},{8,24},{16,0},{24,8},{1,17},{9,25},{17,1},{25,9},{2,18},{10... | collective-permute-start | bytes 1572872 | tf_op jit(solution)/shard_map/ppermute | solution.py:443
  97.9 8.1 %collective-permute-start.21 = (f32[2,64,256]{2,1,0:T(8,128)S(1)}, f32[2,64,256]{2,1,0:T(8,128)S(1)}, u32[]{:S(2)}, u32[]{:S(2)}) collective-permute-start(f32[2,64,256]{2,1,0:T(8,128)S(1)} %fusion.refs_3_), channel_id=1, source_target_pairs={{0,4},{1,5},{2,6},{3,7},{4,0},{5,1},{6,2},{7,3},{8,12},{9,13},{10,... | collective-permute-start | bytes 393224 | tf_op jit(solution)/shard_map/ppermute | solution.py:443
  106.1 5.0 %collective-permute-start.22 = (f32[2,64,256]{2,1,0:T(8,128)S(1)}, f32[2,64,256]{2,1,0:T(8,128)S(1)}, u32[]{:S(2)}, u32[]{:S(2)}) collective-permute-start(f32[2,64,256]{2,1,0:T(8,128)S(1)} %add.29), channel_id=1, source_target_pairs={{0,2},{1,3},{2,0},{3,1},{4,6},{5,7},{6,4},{7,5},{8,10},{9,11},{10,... | collective-permute-start | bytes 393224 | tf_op jit(solution)/shard_map/ppermute | solution.py:443
  106.1 16.4 %collective-permute-start.16 = (f32[2,256,256]{2,1,0:T(8,128)S(1)}, f32[2,256,256]{2,1,0:T(8,128)S(1)}, u32[]{:S(2)}, u32[]{:S(2)}) collective-permute-start(f32[2,256,256]{2,1,0:T(8,128)S(1)} %get-tuple-element.70), channel_id=1, source_target_pairs={{0,16},{8,24},{16,0},{24,8},{1,17},{9,25},{17,1},{25,9},{2,18},{10... | collective-permute-start | bytes 1572872 | tf_op jit(solution)/shard_map/ppermute | solution.py:443
  106.8 5.1 %collective-permute-start.19 = (f32[256,256]{1,0:T(8,128)S(1)}, f32[256,256]{1,0:T(8,128)S(1)}, u32[]{:S(2)}, u32[]{:S(2)}) collective-permute-start(f32[256,256]{1,0:T(8,128)S(1)} %get-tuple-element.77), channel_id=1, source_target_pairs={{0,8},{8,0},{16,24},{24,16},{1,9},{9,1},{17,25},{25,17},{2,10},{10... | collective-permute-start | bytes 786440 | tf_op jit(solution)/shard_map/ppermute | solution.py:443
  111.4 11.8 %collective-permute-start.24 = (f32[256,256]{1,0:T(8,128)S(1)}, f32[256,256]{1,0:T(8,128)S(1)}, u32[]{:S(2)}, u32[]{:S(2)}) collective-permute-start(f32[256,256]{1,0:T(8,128)S(1)} %get-tuple-element.81), channel_id=1, source_target_pairs={{0,8},{8,0},{16,24},{24,16},{1,9},{9,1},{17,25},{25,17},{2,10},{10... | collective-permute-start | bytes 786440 | tf_op jit(solution)/shard_map/ppermute | solution.py:443
  111.9 10.7 %collective-permute-start.26 = (f32[2,64,256]{2,1,0:T(8,128)S(1)}, f32[2,64,256]{2,1,0:T(8,128)S(1)}, u32[]{:S(2)}, u32[]{:S(2)}) collective-permute-start(f32[2,64,256]{2,1,0:T(8,128)S(1)} %add.30.refs_1_), channel_id=1, source_target_pairs={{0,1},{1,0},{2,3},{3,2},{4,5},{5,4},{6,7},{7,6},{8,9},{9,8},{10,11... | collective-permute-start | bytes 393224 | tf_op jit(solution)/shard_map/ppermute | solution.py:443
  115.0 17.5 %collective-permute-start.31 = (f32[2,256,256]{2,1,0:T(8,128)S(1)}, f32[2,256,256]{2,1,0:T(8,128)S(1)}, u32[]{:S(2)}, u32[]{:S(2)}) collective-permute-start(f32[2,256,256]{2,1,0:T(8,128)S(1)} %get-tuple-element.91), channel_id=1, source_target_pairs={{0,16},{8,24},{16,0},{24,8},{1,17},{9,25},{17,1},{25,9},{2,18},{10... | collective-permute-start | bytes 1572872 | tf_op jit(solution)/shard_map/ppermute | solution.py:443
  116.5 16.5 %collective-permute-start.32 = (f32[256,512]{1,0:T(8,128)S(1)}, f32[256,512]{1,0:T(8,128)S(1)}, u32[]{:S(2)}, u32[]{:S(2)}) collective-permute-start(f32[256,512]{1,0:T(8,128)S(1)} %get-tuple-element.92), channel_id=1, source_target_pairs={{0,1},{1,2},{2,3},{3,4},{4,5},{5,6},{6,7},{8,9},{9,10},{10,11},{11... | collective-permute-start | bytes 1572872 | tf_op jit(solution)/shard_map/ppermute | solution.py:461
  126.4 17.8 %collective-permute-start.34 = (f32[256,512]{1,0:T(8,128)S(1)}, f32[256,512]{1,0:T(8,128)S(1)}, u32[]{:S(2)}, u32[]{:S(2)}) collective-permute-start(f32[256,512]{1,0:T(8,128)S(1)} %get-tuple-element.94), channel_id=1, source_target_pairs={{0,1},{1,2},{2,3},{3,4},{4,5},{5,6},{6,7},{8,9},{9,10},{10,11},{11... | collective-permute-start | bytes 1572872 | tf_op jit(solution)/shard_map/ppermute | solution.py:461
  128.9 15.3 %collective-permute-start.29 = (f32[2,256,256]{2,1,0:T(8,128)S(1)}, f32[2,256,256]{2,1,0:T(8,128)S(1)}, u32[]{:S(2)}, u32[]{:S(2)}) collective-permute-start(f32[2,256,256]{2,1,0:T(8,128)S(1)} %get-tuple-element.85), channel_id=1, source_target_pairs={{0,16},{8,24},{16,0},{24,8},{1,17},{9,25},{17,1},{25,9},{2,18},{10... | collective-permute-start | bytes 1572872 | tf_op jit(solution)/shard_map/ppermute | solution.py:443
  130.5 4.3 %collective-permute-start.30 = (f32[256,256]{1,0:T(8,128)S(1)}, f32[256,256]{1,0:T(8,128)S(1)}, u32[]{:S(2)}, u32[]{:S(2)}) collective-permute-start(f32[256,256]{1,0:T(8,128)S(1)} %get-tuple-element.90), channel_id=1, source_target_pairs={{0,8},{8,0},{16,24},{24,16},{1,9},{9,1},{17,25},{25,17},{2,10},{10... | collective-permute-start | bytes 786440 | tf_op jit(solution)/shard_map/ppermute | solution.py:443
  134.6 2.6 %collective-permute-start.40 = (f32[8,128]{1,0:T(8,128)S(1)}, f32[8,128]{1,0:T(8,128)S(1)}, u32[]{:S(2)}, u32[]{:S(2)}) collective-permute-start(f32[8,128]{1,0:T(8,128)S(1)} %collective-permute-done.39), channel_id=1, source_target_pairs={{0,8},{8,0},{16,24},{24,16},{1,9},{9,1},{17,25},{25,17},{2,10},{10... | collective-permute-start | bytes 12296 | tf_op jit(solution)/shard_map/ppermute | solution.py:443
  134.8 10.9 %collective-permute-start.28 = (f32[256,256]{1,0:T(8,128)S(1)}, f32[256,256]{1,0:T(8,128)S(1)}, u32[]{:S(2)}, u32[]{:S(2)}) collective-permute-start(f32[256,256]{1,0:T(8,128)S(1)} %get-tuple-element.84), channel_id=1, source_target_pairs={{0,8},{8,0},{16,24},{24,16},{1,9},{9,1},{17,25},{25,17},{2,10},{10... | collective-permute-start | bytes 786440 | tf_op jit(solution)/shard_map/ppermute | solution.py:443
  137.2 18.2 %collective-permute-start.41 = (f32[256,512]{1,0:T(8,128)S(1)}, f32[256,512]{1,0:T(8,128)S(1)}, u32[]{:S(2)}, u32[]{:S(2)}) collective-permute-start(f32[256,512]{1,0:T(8,128)S(1)} %gate.24), channel_id=1, source_target_pairs={{0,1},{1,2},{2,3},{3,4},{4,5},{5,6},{6,7},{8,9},{9,10},{10,11},{11... | collective-permute-start | bytes 1572872 | tf_op jit(solution)/shard_map/ppermute | solution.py:461
  145.4 2.7 %collective-permute-start.37 = (f32[8,128]{1,0:T(8,128)S(1)}, f32[8,128]{1,0:T(8,128)S(1)}, u32[]{:S(2)}, u32[]{:S(2)}) collective-permute-start(f32[8,128]{1,0:T(8,128)S(1)} %collective-permute-done.36), channel_id=1, source_target_pairs={{0,8},{8,0},{16,24},{24,16},{1,9},{9,1},{17,25},{25,17},{2,10},{10... | collective-permute-start | bytes 12296 | tf_op jit(solution)/shard_map/ppermute | solution.py:443
  148.1 17.7 %collective-permute-start.38 = (f32[256,512]{1,0:T(8,128)S(1)}, f32[256,512]{1,0:T(8,128)S(1)}, u32[]{:S(2)}, u32[]{:S(2)}) collective-permute-start(f32[256,512]{1,0:T(8,128)S(1)} %gate.23), channel_id=1, source_target_pairs={{0,1},{1,2},{2,3},{3,4},{4,5},{5,6},{6,7},{8,9},{9,10},{10,11},{11... | collective-permute-start | bytes 1572872 | tf_op jit(solution)/shard_map/ppermute | solution.py:461
  (20 other events, 120.1 us)

commit v4 on v3

--- a/solution.py
+++ b/solution.py
@@ -496,6 +496,7 @@
 
     strips = list(strips_of(chunks[:1], []))
     strips += strips_of(chunks[1:], strips[:1])
+    strips[1:2] = gate(strips[1:2], [amplitude])
     group = (shape(size, size),) * 2 + (shape(2, size, size),) * (peers // 2 - 1)
     groups = len(group)
     crops = []
@@ -563,12 +564,12 @@
         if k == 0:
             mine = gate(mine, [probe_steps[0]])
         if k >= ahead:
-            mine = gate(mine, returned[k - ahead][2::2] + [own[order[k - ahead]]])
+            mine = gate(mine, returned[1][2::2] + [own[order[k - ahead]]])
         before = [own[order[k - 1]]] if k else probe_steps[-2:-1]
-        if k >= ahead:
+        if k == ahead:
             before.append(rim_back[order[k - ahead]])
         returned.append(exchanged(mine, before))
-        waits = [swap(probe_steps[-1], "depth", 1)] if k == 1 else []
+        waits = [swap(swap(probe_steps[-1], "depth", 1), "depth", 1)] if k == 1 else []
         mine = run_kernel(
             functools.partial(place_kernel, peers, len(waits)),
             "place",
@@ -585,10 +586,12 @@
         )(ids, scan_positions, *returned[k], *waits)
         own[c], outside = mine[:2]
         if k >= ahead:
+            earlier = order[k - ahead]
+            (rim_back[earlier],) = gate([rim_back[earlier]], [own[order[k - 1]]])
             (outside,) = gate([outside], [echo(echo(rim_back[order[k - ahead]]))])
         rim_back[c] = shift(outside, "tile", 1)
 
-    rim_back[order[-2]] = gate([rim_back[order[-2]]], [echo(rim_back[order[-2]])])[0]
+    rim_back[order[-2]] = gate([rim_back[order[-2]]], [swap(rim_back[order[-2]][: rows // 2], "depth", 1)])[0]
     object_grad = jnp.stack(
         [
             jnp.stack([own[(j, part)] + rim_back[(j, part)] for part in range(2)])

time: 169 us -> 168 us (level)
  waiting for transfers between devices: 76 us -> 81.9 us
  starting transfers between devices: 43.3 us -> 39.1 us
    ppermute x8, waiting for transfers between devices: 38 us -> 41.4 us  [shift(): lax.ppermute(x, axis, [(i, i + by) for i in range(peers) if 0 <= i + by <...]
    ppermute x8, starting transfers between devices: 23.1 us -> 20 us  [shift(): lax.ppermute(x, axis, [(i, i + by) for i in range(peers) if 0 <= i + by <...]
    ppermute x35 -> x36, waiting for transfers between devices: 38 us -> 40.5 us  [swap(): return lax.ppermute(x, axis, [(i, i ^ offset) for i in range(peers)])]
    ppermute x35 -> x36, starting transfers between devices: 20.3 us -> 19.1 us  [swap(): return lax.ppermute(x, axis, [(i, i ^ offset) for i in range(peers)])]
  transfers between devices with their start and end apart: 43 -> 44, of which waited for: 26 -> 28; matrix products, arithmetic and copies ran while one was open for 0% -> 0% of each run, Pallas kernels for 14% -> 14%
where the time goes in v4:
time: 168 us; the launch traced here: 167 us
  waiting for transfers between devices  81.9 us (49%)
  Pallas kernels  42 us (25%)
  starting transfers between devices  39.1 us (23%)
  other arithmetic  2.13 us (1%)
    ppermute x8, waiting for transfers between devices, shift(): lax.ppermute(x, axis, [(i, i + by) for i in range(peers) if 0 <= i + by <...  41.4 us
    ppermute x36, waiting for transfers between devices, swap(): return lax.ppermute(x, axis, [(i, i ^ offset) for i in range(peers)])  40.5 us
    ppermute x8, starting transfers between devices, shift(): lax.ppermute(x, axis, [(i, i + by) for i in range(peers) if 0 <= i + by <...  20 us
    ppermute x36, starting transfers between devices, swap(): return lax.ppermute(x, axis, [(i, i ^ offset) for i in range(peers)])  19.1 us
    pallas_call x1, Pallas kernels, body(): run_kernel(functools.partial(optics_kernel, peers, per_device), 'optics',...  17.4 us
    pallas_call x4, Pallas kernels, body(): run_kernel(functools.partial(crop_kernel, peers, c, len(waits)), 'crop',...  10.9 us
    pallas_call x4, Pallas kernels, body(): run_kernel(functools.partial(place_kernel, peers, len(waits)), 'place', (...  8.2 us
    pallas_call x2, Pallas kernels, strips_of(): run_kernel(functools.partial(strip_kernel, planes, len(waits)), 'strip',...  4.21 us
  transfers between devices with their start and end apart: 44, of which 28 were waited for; matrix products, arithmetic and copies ran while one was open for 0% of the time, Pallas kernels for 14%

profile of v4, /device:TPU:4, one launch (start us, length us, event | category | flops | bytes accessed | tf_op | source)
XLA Modules:
  0.0 166.7 jit_solution(6398814917591354371)
XLA Ops:
  2.5 1.9 %collective-permute-start = (f32[256,512]{1,0:T(8,128)}, f32[256,512]{1,0:T(8,128)S(1)}, u32[]{:S(2)}, u32[]{:S(2)}) collective-permute-start(f32[256,512]{1,0:T(8,128)} %strip.2.rest_0_), channel_id=1, source_target_pairs={{1,0},{2,1},{3,2},{4,3},{5,4},{6,5},{7,6},{9,8},{10,9},{11,10},{12... | collective-permute-start | bytes 1572872 | tf_op jit(solution)/shard_map/ppermute | solution.py:461
  4.5 2.4 %strip.3 = (f32[256,512]{1,0:T(8,128)}, f32[256,512]{1,0:T(8,128)}, f32[256,512]{1,0:T(8,128)}) custom-call(f32[2,2,256,512]{3,2,1,0:T(8,128)} %strips.11, f32[256,512]{1,0:T(8,128)} %strip.2.rest_0_), custom_call_target="tpu_custom_call" | custom-call | flops 1000000 | bytes 1000 | tf_op jit(solution)/shard_map/strip/pallas_call | solution.py:486
  8.3 1.9 %collective-permute-start.4 = (f32[256,512]{1,0:T(8,128)}, f32[256,512]{1,0:T(8,128)}, u32[]{:S(2)}, u32[]{:S(2)}) collective-permute-start(f32[256,512]{1,0:T(8,128)} %gate.16), channel_id=1, source_target_pairs={{1,0},{2,1},{3,2},{4,3},{5,4},{6,5},{7,6},{9,8},{10,9},{11,10},{12... | collective-permute-start | bytes 1572872 | tf_op jit(solution)/shard_map/ppermute | solution.py:461
  10.3 10.0 %collective-permute-done.rim = f32[256,512]{1,0:T(8,128)S(1)} collective-permute-done((f32[256,512]{1,0:T(8,128)}, f32[256,512]{1,0:T(8,128)S(1)}, u32[]{:S(2)}, u32[]{:S(2)}) %collective-permute-start) | collective-permute-done | bytes 524320 | tf_op jit(solution)/shard_map/ppermute | solution.py:461
  20.3 2.5 %crop.4 = (f32[256,256]{1,0:T(8,128)S(1)}, f32[256,256]{1,0:T(8,128)S(1)}, f32[2,256,256]{2,1,0:T(8,128)S(1)}) custom-call(s32[2]{0:T(128)S(1)} %pad_add_fusion.ids, s32[4,2]{1,0:T(4,128)S(1)} %copy.37.positions, f32[2,2,256,512]{3,2,1,0:T(8,128)S(1)} %copy-done, f32[256,512]{1,0:T(8,128)S(1)} %collective-permute-done.rim, ...), custom_call_target="tpu_custom_call" | custom-call | flops 2000000 | bytes 2000 | tf_op jit(solution)/shard_map/crop/pallas_call | solution.py:506
  24.3 2.0 %collective-permute-start.8 = (f32[256,512]{1,0:T(8,128)S(1)}, f32[256,512]{1,0:T(8,128)S(1)}, u32[]{:S(2)}, u32[]{:S(2)}) collective-permute-start(f32[256,512]{1,0:T(8,128)S(1)} %gate.17), channel_id=1, source_target_pairs={{1,0},{2,1},{3,2},{4,3},{5,4},{6,5},{7,6},{9,8},{10,9},{11,10},{12... | collective-permute-start | bytes 1572872 | tf_op jit(solution)/shard_map/ppermute | solution.py:461
  26.4 5.2 %collective-permute-done.4.rim = f32[256,512]{1,0:T(8,128)} collective-permute-done((f32[256,512]{1,0:T(8,128)}, f32[256,512]{1,0:T(8,128)}, u32[]{:S(2)}, u32[]{:S(2)}) %collective-permute-start.4) | collective-permute-done | bytes 524320 | tf_op jit(solution)/shard_map/ppermute | solution.py:461
  31.6 3.4 %crop.5 = (f32[256,256]{1,0:T(8,128)S(1)}, f32[256,256]{1,0:T(8,128)S(1)}, f32[2,256,256]{2,1,0:T(8,128)S(1)}) custom-call(s32[2]{0:T(128)S(1)} %pad_add_fusion.ids, s32[4,2]{1,0:T(4,128)S(1)} %copy.37.positions, f32[2,2,256,512]{3,2,1,0:T(8,128)S(1)} %copy-done, f32[256,512]{1,0:T(8,128)} %collective-permute-done.4.rim, ...), custom_call_target="tpu_custom_call" | custom-call | flops 2000000 | bytes 2000 | tf_op jit(solution)/shard_map/crop/pallas_call | solution.py:506
  38.6 4.2 %collective-permute-done.8.rim = f32[256,512]{1,0:T(8,128)S(1)} collective-permute-done((f32[256,512]{1,0:T(8,128)S(1)}, f32[256,512]{1,0:T(8,128)S(1)}, u32[]{:S(2)}, u32[]{:S(2)}) %collective-permute-start.8) | collective-permute-done | bytes 524320 | tf_op jit(solution)/shard_map/ppermute | solution.py:461
  42.8 2.5 %crop.6 = (f32[256,256]{1,0:T(8,128)S(1)}, f32[256,256]{1,0:T(8,128)S(1)}, f32[2,256,256]{2,1,0:T(8,128)S(1)}) custom-call(s32[2]{0:T(128)S(1)} %pad_add_fusion.ids, s32[4,2]{1,0:T(4,128)S(1)} %copy.37.positions, f32[2,2,256,512]{3,2,1,0:T(8,128)S(1)} %copy-done, f32[256,512]{1,0:T(8,128)S(1)} %collective-permute-done.8.rim, ...), custom_call_target="tpu_custom_call" | custom-call | flops 2000000 | bytes 2000 | tf_op jit(solution)/shard_map/crop/pallas_call | solution.py:506
  47.8 5.1 %collective-permute-done.12.rim = f32[256,512]{1,0:T(8,128)S(1)} collective-permute-done((f32[256,512]{1,0:T(8,128)S(1)}, f32[256,512]{1,0:T(8,128)S(1)}, u32[]{:S(2)}, u32[]{:S(2)}) %collective-permute-start.12) | collective-permute-done | bytes 524320 | tf_op jit(solution)/shard_map/ppermute | solution.py:461
  52.9 2.5 %crop.7 = (f32[256,256]{1,0:T(8,128)S(1)}, f32[256,256]{1,0:T(8,128)S(1)}, f32[2,256,256]{2,1,0:T(8,128)S(1)}) custom-call(s32[2]{0:T(128)S(1)} %pad_add_fusion.ids, s32[4,2]{1,0:T(4,128)S(1)} %copy.37.positions, f32[2,2,256,512]{3,2,1,0:T(8,128)S(1)} %copy-done, f32[256,512]{1,0:T(8,128)S(1)} %collective-permute-done.12.rim, ...), custom_call_target="tpu_custom_call" | custom-call | flops 2000000 | bytes 2000 | tf_op jit(solution)/shard_map/crop/pallas_call | solution.py:506
  57.1 2.2 %collective-permute-done.10.rest_10_ = f32[2,256,256]{2,1,0:T(8,128)S(1)} collective-permute-done((f32[2,256,256]{2,1,0:T(8,128)S(1)}, f32[2,256,256]{2,1,0:T(8,128)S(1)}, u32[]{:S(2)}, u32[]{:S(2)}) %collective-permute-start.10) | collective-permute-done | bytes 524320 | tf_op jit(solution)/shard_map/ppermute | solution.py:443
  60.8 8.5 %collective-permute-done.14.refs_0_ = f32[2,256,256]{2,1,0:T(8,128)S(1)} collective-permute-done((f32[2,256,256]{2,1,0:T(8,128)S(1)}, f32[2,256,256]{2,1,0:T(8,128)S(1)}, u32[]{:S(2)}, u32[]{:S(2)}) %collective-permute-start.14) | collective-permute-done | bytes 524320 | tf_op jit(solution)/shard_map/ppermute | solution.py:443
  70.9 17.4 %optics.1 = (f32[256,256]{1,0:T(8,128)S(1)}, f32[256,256]{1,0:T(8,128)S(1)}, f32[2,256,256]{2,1,0:T(8,128)S(1)}, f32[256,256]{1,0:T(8,128)S(1)}, f32[256,256]{1,...) custom-call(s32[2]{0:T(128)S(1)} %pad_add_fusion.ids, ...), custom_call_target="tpu_custom_call" | custom-call | flops 15000000 | bytes 15000 | tf_op jit(solution)/shard_map/optics/pallas_call | solution.py:524
  91.5 4.1 %collective-permute-done.18 = f32[1,2,64,256]{3,2,1,0:T(8,128)S(1)} collective-permute-done((f32[1,2,64,256]{3,2,1,0:T(8,128)S(1)}, f32[1,2,64,256]{3,2,1,0:T(8,128)S(1)}, u32[]{:S(2)}, u32[]{:S(2)}) %collective-permute-start.18) | collective-permute-done | bytes 131104 | tf_op jit(solution)/shard_map/ppermute | solution.py:443
  97.1 2.6 %collective-permute-start.21 = (f32[2,64,256]{2,1,0:T(8,128)S(1)}, f32[2,64,256]{2,1,0:T(8,128)S(1)}, u32[]{:S(2)}, u32[]{:S(2)}) collective-permute-start(f32[2,64,256]{2,1,0:T(8,128)S(1)} %fusion.refs_3_), channel_id=1, source_target_pairs={{0,4},{1,5},{2,6},{3,7},{4,0},{5,1},{6,2},{7,3},{8,12},{9,13},{10,... | collective-permute-start | bytes 393224 | tf_op jit(solution)/shard_map/ppermute | solution.py:443
  99.7 5.6 %collective-permute-done.21 = f32[2,64,256]{2,1,0:T(8,128)S(1)} collective-permute-done((f32[2,64,256]{2,1,0:T(8,128)S(1)}, f32[2,64,256]{2,1,0:T(8,128)S(1)}, u32[]{:S(2)}, u32[]{:S(2)}) %collective-permute-start.21) | collective-permute-done | bytes 131104 | tf_op jit(solution)/shard_map/ppermute | solution.py:443
  106.0 4.4 %collective-permute-done.22 = f32[2,64,256]{2,1,0:T(8,128)S(1)} collective-permute-done((f32[2,64,256]{2,1,0:T(8,128)S(1)}, f32[2,64,256]{2,1,0:T(8,128)S(1)}, u32[]{:S(2)}, u32[]{:S(2)}) %collective-permute-start.22) | collective-permute-done | bytes 131104 | tf_op jit(solution)/shard_map/ppermute | solution.py:443
  112.1 2.0 %place.4 = (f32[256,512]{1,0:T(8,128)S(1)}, f32[256,512]{1,0:T(8,128)S(1)}) custom-call(s32[2]{0:T(128)S(1)} %pad_add_fusion.ids, s32[4,2]{1,0:T(4,128)S(1)} %copy.37.positions, f32[256,256]{1,0:T(8,128)S(1)} %get-tuple-element.76.rest_0_, f32[256,256]{1,0:T(8,128)S(1)} %collective-permute-done.19.rest_1_, f32[2,256,256]{2,1,0:T(8,128)S(1)} %gate.21.rest_2_, ...), custom_call_target="tpu_custom_call" | custom-call | flops 2000000 | bytes 2000 | tf_op jit(solution)/shard_map/place/pallas_call | solution.py:573
  114.2 3.5 %collective-permute-start.33 = (f32[256,512]{1,0:T(8,128)S(1)}, f32[256,512]{1,0:T(8,128)S(1)}, u32[]{:S(2)}, u32[]{:S(2)}) collective-permute-start(f32[256,512]{1,0:T(8,128)S(1)} %get-tuple-element.92), channel_id=1, source_target_pairs={{0,1},{1,2},{2,3},{3,4},{4,5},{5,6},{6,7},{8,9},{9,10},{10,11},{11... | collective-permute-start | bytes 1572872 | tf_op jit(solution)/shard_map/ppermute | solution.py:461
  117.7 2.3 %collective-permute-done.16.refs_0_ = f32[2,256,256]{2,1,0:T(8,128)S(1)} collective-permute-done((f32[2,256,256]{2,1,0:T(8,128)S(1)}, f32[2,256,256]{2,1,0:T(8,128)S(1)}, u32[]{:S(2)}, u32[]{:S(2)}) %collective-permute-start.16) | collective-permute-done | bytes 524320 | tf_op jit(solution)/shard_map/ppermute | solution.py:443
  124.6 2.0 %place.5 = (f32[256,512]{1,0:T(8,128)S(1)}, f32[256,512]{1,0:T(8,128)S(1)}) custom-call(s32[2]{0:T(128)S(1)} %pad_add_fusion.ids, s32[4,2]{1,0:T(4,128)S(1)} %copy.37.positions, f32[256,256]{1,0:T(8,128)S(1)} %get-tuple-element.80.rest_0_, f32[256,256]{1,0:T(8,128)S(1)} %collective-permute-done.24.rest_1_, f32[2,256,256]{2,1,0:T(8,128)S(1)} %gate.22.rest_2_.refs_3_, ...), custom_call_target="tpu_custom_call" | custom-call | flops 2000000 | bytes 2000 | tf_op jit(solution)/shard_map/place/pallas_call | solution.py:573
  126.7 2.5 %collective-permute-start.36 = (f32[256,512]{1,0:T(8,128)S(1)}, f32[256,512]{1,0:T(8,128)S(1)}, u32[]{:S(2)}, u32[]{:S(2)}) collective-permute-start(f32[256,512]{1,0:T(8,128)S(1)} %get-tuple-element.96), channel_id=1, source_target_pairs={{0,1},{1,2},{2,3},{3,4},{4,5},{5,6},{6,7},{8,9},{9,10},{10,11},{11... | collective-permute-start | bytes 1572872 | tf_op jit(solution)/shard_map/ppermute | solution.py:461
  130.0 2.5 %collective-permute-done.32.refs_0_ = f32[2,256,256]{2,1,0:T(8,128)S(1)} collective-permute-done((f32[2,256,256]{2,1,0:T(8,128)S(1)}, f32[2,256,256]{2,1,0:T(8,128)S(1)}, u32[]{:S(2)}, u32[]{:S(2)}) %collective-permute-start.32) | collective-permute-done | bytes 524320 | tf_op jit(solution)/shard_map/ppermute | solution.py:443
  134.4 2.0 %place.6 = (f32[256,512]{1,0:T(8,128)S(1)}, f32[256,512]{1,0:T(8,128)S(1)}) custom-call(s32[2]{0:T(128)S(1)} %pad_add_fusion.ids, s32[4,2]{1,0:T(4,128)S(1)} %copy.37.positions, f32[256,256]{1,0:T(8,128)S(1)} %get-tuple-element.89.rest_0_, f32[256,256]{1,0:T(8,128)S(1)} %collective-permute-done.31.rest_1_, f32[2,256,256]{2,1,0:T(8,128)S(1)} %gate.25.rest_2_, ...), custom_call_target="tpu_custom_call" | custom-call | flops 2000000 | bytes 2000 | tf_op jit(solution)/shard_map/place/pallas_call | solution.py:573
  136.5 2.3 %collective-permute-start.42 = (f32[256,512]{1,0:T(8,128)S(1)}, f32[256,512]{1,0:T(8,128)S(1)}, u32[]{:S(2)}, u32[]{:S(2)}) collective-permute-start(f32[256,512]{1,0:T(8,128)S(1)} %gate.30), channel_id=1, source_target_pairs={{0,1},{1,2},{2,3},{3,4},{4,5},{5,6},{6,7},{8,9},{9,10},{10,11},{11... | collective-permute-start | bytes 1572872 | tf_op jit(solution)/shard_map/ppermute | solution.py:461
  138.9 4.4 %collective-permute-done.36.refs_0_ = f32[256,512]{1,0:T(8,128)S(1)} collective-permute-done((f32[256,512]{1,0:T(8,128)S(1)}, f32[256,512]{1,0:T(8,128)S(1)}, u32[]{:S(2)}, u32[]{:S(2)}) %collective-permute-start.36) | collective-permute-done | bytes 524320 | tf_op jit(solution)/shard_map/ppermute | solution.py:461
  145.1 2.0 %place.7 = (f32[256,512]{1,0:T(8,128)S(1)}, f32[256,512]{1,0:T(8,128)S(1)}) custom-call(s32[2]{0:T(128)S(1)} %pad_add_fusion.ids, s32[4,2]{1,0:T(4,128)S(1)} %copy.37.positions, f32[256,256]{1,0:T(8,128)S(1)} %get-tuple-element.83.rest_0_, f32[256,256]{1,0:T(8,128)S(1)} %collective-permute-done.29.rest_1_, f32[2,256,256]{2,1,0:T(8,128)S(1)} %gate.26.rest_2_, ...), custom_call_target="tpu_custom_call" | custom-call | flops 2000000 | bytes 2000 | tf_op jit(solution)/shard_map/place/pallas_call | solution.py:573
  147.2 3.9 %collective-permute-start.39 = (f32[256,512]{1,0:T(8,128)S(1)}, f32[256,512]{1,0:T(8,128)S(1)}, u32[]{:S(2)}, u32[]{:S(2)}) collective-permute-start(f32[256,512]{1,0:T(8,128)S(1)} %gate.28), channel_id=1, source_target_pairs={{0,1},{1,2},{2,3},{3,4},{4,5},{5,6},{6,7},{8,9},{9,10},{10,11},{11... | collective-permute-start | bytes 1572872 | tf_op jit(solution)/shard_map/ppermute | solution.py:461
  151.1 3.4 %collective-permute-done.42.refs_0_ = f32[256,512]{1,0:T(8,128)S(1)} collective-permute-done((f32[256,512]{1,0:T(8,128)S(1)}, f32[256,512]{1,0:T(8,128)S(1)}, u32[]{:S(2)}, u32[]{:S(2)}) %collective-permute-start.42) | collective-permute-done | bytes 524320 | tf_op jit(solution)/shard_map/ppermute | solution.py:461
  156.2 8.8 %collective-permute-done.39 = f32[256,512]{1,0:T(8,128)S(1)} collective-permute-done((f32[256,512]{1,0:T(8,128)S(1)}, f32[256,512]{1,0:T(8,128)S(1)}, u32[]{:S(2)}, u32[]{:S(2)}) %collective-permute-start.39) | collective-permute-done | bytes 524320 | tf_op jit(solution)/shard_map/ppermute | solution.py:461
  (128 shorter events, 35.3 us)
Async XLA Ops:
  2.5 17.8 %collective-permute-start = (f32[256,512]{1,0:T(8,128)}, f32[256,512]{1,0:T(8,128)S(1)}, u32[]{:S(2)}, u32[]{:S(2)}) collective-permute-start(f32[256,512]{1,0:T(8,128)} %strip.2.rest_0_), channel_id=1, source_target_pairs={{1,0},{2,1},{3,2},{4,3},{5,4},{6,5},{7,6},{9,8},{10,9},{11,10},{12... | collective-permute-start | bytes 1572872 | tf_op jit(solution)/shard_map/ppermute | solution.py:461
  8.3 23.4 %collective-permute-start.4 = (f32[256,512]{1,0:T(8,128)}, f32[256,512]{1,0:T(8,128)}, u32[]{:S(2)}, u32[]{:S(2)}) collective-permute-start(f32[256,512]{1,0:T(8,128)} %gate.16), channel_id=1, source_target_pairs={{1,0},{2,1},{3,2},{4,3},{5,4},{6,5},{7,6},{9,8},{10,9},{11,10},{12... | collective-permute-start | bytes 1572872 | tf_op jit(solution)/shard_map/ppermute | solution.py:461
  22.8 15.8 %collective-permute-start.2 = (f32[2,256,256]{2,1,0:T(8,128)S(1)}, f32[2,256,256]{2,1,0:T(8,128)S(1)}, u32[]{:S(2)}, u32[]{:S(2)}) collective-permute-start(f32[2,256,256]{2,1,0:T(8,128)S(1)} %get-tuple-element.54), channel_id=1, source_target_pairs={{0,16},{8,24},{16,0},{24,8},{1,17},{9,25},{17,1},{25,9},{2,18},{10... | collective-permute-start | bytes 1572872 | tf_op jit(solution)/shard_map/ppermute | solution.py:443
  24.3 18.4 %collective-permute-start.8 = (f32[256,512]{1,0:T(8,128)S(1)}, f32[256,512]{1,0:T(8,128)S(1)}, u32[]{:S(2)}, u32[]{:S(2)}) collective-permute-start(f32[256,512]{1,0:T(8,128)S(1)} %gate.17), channel_id=1, source_target_pairs={{1,0},{2,1},{3,2},{4,3},{5,4},{6,5},{7,6},{9,8},{10,9},{11,10},{12... | collective-permute-start | bytes 1572872 | tf_op jit(solution)/shard_map/ppermute | solution.py:461
  35.1 12.7 %collective-permute-start.6 = (f32[2,256,256]{2,1,0:T(8,128)S(1)}, f32[2,256,256]{2,1,0:T(8,128)S(1)}, u32[]{:S(2)}, u32[]{:S(2)}) collective-permute-start(f32[2,256,256]{2,1,0:T(8,128)S(1)} %get-tuple-element.58), channel_id=1, source_target_pairs={{0,16},{8,24},{16,0},{24,8},{1,17},{9,25},{17,1},{25,9},{2,18},{10... | collective-permute-start | bytes 1572872 | tf_op jit(solution)/shard_map/ppermute | solution.py:443
  36.6 16.2 %collective-permute-start.12 = (f32[256,512]{1,0:T(8,128)S(1)}, f32[256,512]{1,0:T(8,128)S(1)}, u32[]{:S(2)}, u32[]{:S(2)}) collective-permute-start(f32[256,512]{1,0:T(8,128)S(1)} %gate.18), channel_id=1, source_target_pairs={{1,0},{2,1},{3,2},{4,3},{5,4},{6,5},{7,6},{9,8},{10,9},{11,10},{12... | collective-permute-start | bytes 1572872 | tf_op jit(solution)/shard_map/ppermute | solution.py:461
  45.3 14.0 %collective-permute-start.10 = (f32[2,256,256]{2,1,0:T(8,128)S(1)}, f32[2,256,256]{2,1,0:T(8,128)S(1)}, u32[]{:S(2)}, u32[]{:S(2)}) collective-permute-start(f32[2,256,256]{2,1,0:T(8,128)S(1)} %get-tuple-element.62), channel_id=1, source_target_pairs={{0,16},{8,24},{16,0},{24,8},{1,17},{9,25},{17,1},{25,9},{2,18},{10... | collective-permute-start | bytes 1572872 | tf_op jit(solution)/shard_map/ppermute | solution.py:443
  46.8 12.5 %collective-permute-start.1 = (f32[256,256]{1,0:T(8,128)S(1)}, f32[256,256]{1,0:T(8,128)S(1)}, u32[]{:S(2)}, u32[]{:S(2)}) collective-permute-start(f32[256,256]{1,0:T(8,128)S(1)} %get-tuple-element.53), channel_id=1, source_target_pairs={{0,8},{8,0},{16,24},{24,16},{1,9},{9,1},{17,25},{25,17},{2,10},{10... | collective-permute-start | bytes 786440 | tf_op jit(solution)/shard_map/ppermute | solution.py:443
  46.8 13.0 %collective-permute-start.5 = (f32[256,256]{1,0:T(8,128)S(1)}, f32[256,256]{1,0:T(8,128)S(1)}, u32[]{:S(2)}, u32[]{:S(2)}) collective-permute-start(f32[256,256]{1,0:T(8,128)S(1)} %get-tuple-element.57), channel_id=1, source_target_pairs={{0,8},{8,0},{16,24},{24,16},{1,9},{9,1},{17,25},{25,17},{2,10},{10... | collective-permute-start | bytes 786440 | tf_op jit(solution)/shard_map/ppermute | solution.py:443
  55.4 13.9 %collective-permute-start.14 = (f32[2,256,256]{2,1,0:T(8,128)S(1)}, f32[2,256,256]{2,1,0:T(8,128)S(1)}, u32[]{:S(2)}, u32[]{:S(2)}) collective-permute-start(f32[2,256,256]{2,1,0:T(8,128)S(1)} %get-tuple-element.66), channel_id=1, source_target_pairs={{0,16},{8,24},{16,0},{24,8},{1,17},{9,25},{17,1},{25,9},{2,18},{10... | collective-permute-start | bytes 1572872 | tf_op jit(solution)/shard_map/ppermute | solution.py:443
  56.9 3.0 %collective-permute-start.3 = (f32[256,256]{1,0:T(8,128)S(1)}, f32[256,256]{1,0:T(8,128)S(1)}, u32[]{:S(2)}, u32[]{:S(2)}) collective-permute-start(f32[256,256]{1,0:T(8,128)S(1)} %slice_bitcast_fusion.7), channel_id=1, source_target_pairs={{0,8},{8,0},{16,24},{24,16},{1,9},{9,1},{17,25},{25,17},{2,10},{10... | collective-permute-start | bytes 786440 | tf_op jit(solution)/shard_map/ppermute | solution.py:443
  59.3 10.1 %collective-permute-start.9 = (f32[256,256]{1,0:T(8,128)S(1)}, f32[256,256]{1,0:T(8,128)S(1)}, u32[]{:S(2)}, u32[]{:S(2)}) collective-permute-start(f32[256,256]{1,0:T(8,128)S(1)} %get-tuple-element.61), channel_id=1, source_target_pairs={{0,8},{8,0},{16,24},{24,16},{1,9},{9,1},{17,25},{25,17},{2,10},{10... | collective-permute-start | bytes 786440 | tf_op jit(solution)/shard_map/ppermute | solution.py:443
  59.8 9.5 %collective-permute-start.13 = (f32[256,256]{1,0:T(8,128)S(1)}, f32[256,256]{1,0:T(8,128)S(1)}, u32[]{:S(2)}, u32[]{:S(2)}) collective-permute-start(f32[256,256]{1,0:T(8,128)S(1)} %get-tuple-element.65), channel_id=1, source_target_pairs={{0,8},{8,0},{16,24},{24,16},{1,9},{9,1},{17,25},{25,17},{2,10},{10... | collective-permute-start | bytes 786440 | tf_op jit(solution)/shard_map/ppermute | solution.py:443
  59.9 9.4 %collective-permute-start.11 = (f32[256,256]{1,0:T(8,128)S(1)}, f32[256,256]{1,0:T(8,128)S(1)}, u32[]{:S(2)}, u32[]{:S(2)}) collective-permute-start(f32[256,256]{1,0:T(8,128)S(1)} %slice_bitcast_fusion.5), channel_id=1, source_target_pairs={{0,8},{8,0},{16,24},{24,16},{1,9},{9,1},{17,25},{25,17},{2,10},{10... | collective-permute-start | bytes 786440 | tf_op jit(solution)/shard_map/ppermute | solution.py:443
  89.9 5.6 %collective-permute-start.18 = (f32[1,2,64,256]{3,2,1,0:T(8,128)S(1)}, f32[1,2,64,256]{3,2,1,0:T(8,128)S(1)}, u32[]{:S(2)}, u32[]{:S(2)}) collective-permute-start(f32[1,2,64,256]{3,2,1,0:T(8,128)S(1)} %slice.57), channel_id=1, source_target_pairs={{0,16},{8,24},{16,0},{24,8},{1,17},{9,25},{17,1},{25,9},{2,18},{10... | collective-permute-start | bytes 393224 | tf_op jit(solution)/shard_map/ppermute | solution.py:443
  95.6 14.9 %collective-permute-start.20 = (f32[2,256,256]{2,1,0:T(8,128)S(1)}, f32[2,256,256]{2,1,0:T(8,128)S(1)}, u32[]{:S(2)}, u32[]{:S(2)}) collective-permute-start(f32[2,256,256]{2,1,0:T(8,128)S(1)} %get-tuple-element.78), channel_id=1, source_target_pairs={{0,16},{8,24},{16,0},{24,8},{1,17},{9,25},{17,1},{25,9},{2,18},{10... | collective-permute-start | bytes 1572872 | tf_op jit(solution)/shard_map/ppermute | solution.py:443
  97.1 8.1 %collective-permute-start.21 = (f32[2,64,256]{2,1,0:T(8,128)S(1)}, f32[2,64,256]{2,1,0:T(8,128)S(1)}, u32[]{:S(2)}, u32[]{:S(2)}) collective-permute-start(f32[2,64,256]{2,1,0:T(8,128)S(1)} %fusion.refs_3_), channel_id=1, source_target_pairs={{0,4},{1,5},{2,6},{3,7},{4,0},{5,1},{6,2},{7,3},{8,12},{9,13},{10,... | collective-permute-start | bytes 393224 | tf_op jit(solution)/shard_map/ppermute | solution.py:443
  105.3 5.0 %collective-permute-start.22 = (f32[2,64,256]{2,1,0:T(8,128)S(1)}, f32[2,64,256]{2,1,0:T(8,128)S(1)}, u32[]{:S(2)}, u32[]{:S(2)}) collective-permute-start(f32[2,64,256]{2,1,0:T(8,128)S(1)} %add.29), channel_id=1, source_target_pairs={{0,2},{1,3},{2,0},{3,1},{4,6},{5,7},{6,4},{7,5},{8,10},{9,11},{10,... | collective-permute-start | bytes 393224 | tf_op jit(solution)/shard_map/ppermute | solution.py:443
  105.4 14.6 %collective-permute-start.16 = (f32[2,256,256]{2,1,0:T(8,128)S(1)}, f32[2,256,256]{2,1,0:T(8,128)S(1)}, u32[]{:S(2)}, u32[]{:S(2)}) collective-permute-start(f32[2,256,256]{2,1,0:T(8,128)S(1)} %get-tuple-element.70), channel_id=1, source_target_pairs={{0,16},{8,24},{16,0},{24,8},{1,17},{9,25},{17,1},{25,9},{2,18},{10... | collective-permute-start | bytes 1572872 | tf_op jit(solution)/shard_map/ppermute | solution.py:443
  106.0 4.7 %collective-permute-start.19 = (f32[256,256]{1,0:T(8,128)S(1)}, f32[256,256]{1,0:T(8,128)S(1)}, u32[]{:S(2)}, u32[]{:S(2)}) collective-permute-start(f32[256,256]{1,0:T(8,128)S(1)} %get-tuple-element.77), channel_id=1, source_target_pairs={{0,8},{8,0},{16,24},{24,16},{1,9},{9,1},{17,25},{25,17},{2,10},{10... | collective-permute-start | bytes 786440 | tf_op jit(solution)/shard_map/ppermute | solution.py:443
  110.6 10.9 %collective-permute-start.26 = (f32[2,64,256]{2,1,0:T(8,128)S(1)}, f32[2,64,256]{2,1,0:T(8,128)S(1)}, u32[]{:S(2)}, u32[]{:S(2)}) collective-permute-start(f32[2,64,256]{2,1,0:T(8,128)S(1)} %add.30.refs_1_), channel_id=1, source_target_pairs={{0,1},{1,0},{2,3},{3,2},{4,5},{5,4},{6,7},{7,6},{8,9},{9,8},{10,11... | collective-permute-start | bytes 393224 | tf_op jit(solution)/shard_map/ppermute | solution.py:443
  114.2 15.9 %collective-permute-start.33 = (f32[256,512]{1,0:T(8,128)S(1)}, f32[256,512]{1,0:T(8,128)S(1)}, u32[]{:S(2)}, u32[]{:S(2)}) collective-permute-start(f32[256,512]{1,0:T(8,128)S(1)} %get-tuple-element.92), channel_id=1, source_target_pairs={{0,1},{1,2},{2,3},{3,4},{4,5},{5,6},{6,7},{8,9},{9,10},{10,11},{11... | collective-permute-start | bytes 1572872 | tf_op jit(solution)/shard_map/ppermute | solution.py:461
  120.0 12.6 %collective-permute-start.32 = (f32[2,256,256]{2,1,0:T(8,128)S(1)}, f32[2,256,256]{2,1,0:T(8,128)S(1)}, u32[]{:S(2)}, u32[]{:S(2)}) collective-permute-start(f32[2,256,256]{2,1,0:T(8,128)S(1)} %get-tuple-element.91), channel_id=1, source_target_pairs={{0,16},{8,24},{16,0},{24,8},{1,17},{9,25},{17,1},{25,9},{2,18},{10... | collective-permute-start | bytes 1572872 | tf_op jit(solution)/shard_map/ppermute | solution.py:443
  122.2 2.4 %collective-permute-start.25 = (f32[256,256]{1,0:T(8,128)S(1)}, f32[256,256]{1,0:T(8,128)S(1)}, u32[]{:S(2)}, u32[]{:S(2)}) collective-permute-start(f32[256,256]{1,0:T(8,128)S(1)} %slice_bitcast_fusion.2), channel_id=1, source_target_pairs={{0,8},{8,0},{16,24},{24,16},{1,9},{9,1},{17,25},{25,17},{2,10},{10... | collective-permute-start | bytes 786440 | tf_op jit(solution)/shard_map/ppermute | solution.py:443
  126.7 16.6 %collective-permute-start.36 = (f32[256,512]{1,0:T(8,128)S(1)}, f32[256,512]{1,0:T(8,128)S(1)}, u32[]{:S(2)}, u32[]{:S(2)}) collective-permute-start(f32[256,512]{1,0:T(8,128)S(1)} %get-tuple-element.96), channel_id=1, source_target_pairs={{0,1},{1,2},{2,3},{3,4},{4,5},{5,6},{6,7},{8,9},{9,10},{10,11},{11... | collective-permute-start | bytes 1572872 | tf_op jit(solution)/shard_map/ppermute | solution.py:461
  129.2 14.3 %collective-permute-start.30 = (f32[2,256,256]{2,1,0:T(8,128)S(1)}, f32[2,256,256]{2,1,0:T(8,128)S(1)}, u32[]{:S(2)}, u32[]{:S(2)}) collective-permute-start(f32[2,256,256]{2,1,0:T(8,128)S(1)} %get-tuple-element.85), channel_id=1, source_target_pairs={{0,16},{8,24},{16,0},{24,8},{1,17},{9,25},{17,1},{25,9},{2,18},{10... | collective-permute-start | bytes 1572872 | tf_op jit(solution)/shard_map/ppermute | solution.py:443
  129.8 4.6 %collective-permute-start.31 = (f32[256,256]{1,0:T(8,128)S(1)}, f32[256,256]{1,0:T(8,128)S(1)}, u32[]{:S(2)}, u32[]{:S(2)}) collective-permute-start(f32[256,256]{1,0:T(8,128)S(1)} %get-tuple-element.90), channel_id=1, source_target_pairs={{0,8},{8,0},{16,24},{24,16},{1,9},{9,1},{17,25},{25,17},{2,10},{10... | collective-permute-start | bytes 786440 | tf_op jit(solution)/shard_map/ppermute | solution.py:443
  134.2 2.2 %collective-permute-start.41 = (f32[8,128]{1,0:T(8,128)S(1)}, f32[8,128]{1,0:T(8,128)S(1)}, u32[]{:S(2)}, u32[]{:S(2)}) collective-permute-start(f32[8,128]{1,0:T(8,128)S(1)} %collective-permute-done.40), channel_id=1, source_target_pairs={{0,8},{8,0},{16,24},{24,16},{1,9},{9,1},{17,25},{25,17},{2,10},{10... | collective-permute-start | bytes 12296 | tf_op jit(solution)/shard_map/ppermute | solution.py:443
  136.5 18.1 %collective-permute-start.42 = (f32[256,512]{1,0:T(8,128)S(1)}, f32[256,512]{1,0:T(8,128)S(1)}, u32[]{:S(2)}, u32[]{:S(2)}) collective-permute-start(f32[256,512]{1,0:T(8,128)S(1)} %gate.30), channel_id=1, source_target_pairs={{0,1},{1,2},{2,3},{3,4},{4,5},{5,6},{6,7},{8,9},{9,10},{10,11},{11... | collective-permute-start | bytes 1572872 | tf_op jit(solution)/shard_map/ppermute | solution.py:461
  138.7 6.0 %collective-permute-start.29 = (f32[256,256]{1,0:T(8,128)S(1)}, f32[256,256]{1,0:T(8,128)S(1)}, u32[]{:S(2)}, u32[]{:S(2)}) collective-permute-start(f32[256,256]{1,0:T(8,128)S(1)} %get-tuple-element.84), channel_id=1, source_target_pairs={{0,8},{8,0},{16,24},{24,16},{1,9},{9,1},{17,25},{25,17},{2,10},{10... | collective-permute-start | bytes 786440 | tf_op jit(solution)/shard_map/ppermute | solution.py:443
  144.5 2.7 %collective-permute-start.38 = (f32[8,128]{1,0:T(8,128)S(1)}, f32[8,128]{1,0:T(8,128)S(1)}, u32[]{:S(2)}, u32[]{:S(2)}) collective-permute-start(f32[8,128]{1,0:T(8,128)S(1)} %collective-permute-done.37), channel_id=1, source_target_pairs={{0,8},{8,0},{16,24},{24,16},{1,9},{9,1},{17,25},{25,17},{2,10},{10... | collective-permute-start | bytes 12296 | tf_op jit(solution)/shard_map/ppermute | solution.py:443
  147.2 17.9 %collective-permute-start.39 = (f32[256,512]{1,0:T(8,128)S(1)}, f32[256,512]{1,0:T(8,128)S(1)}, u32[]{:S(2)}, u32[]{:S(2)}) collective-permute-start(f32[256,512]{1,0:T(8,128)S(1)} %gate.28), channel_id=1, source_target_pairs={{0,1},{1,2},{2,3},{3,4},{4,5},{5,6},{6,7},{8,9},{9,10},{10,11},{11... | collective-permute-start | bytes 1572872 | tf_op jit(solution)/shard_map/ppermute | solution.py:461
  (21 other events, 109.0 us)

commit v5 on v4

--- a/solution.py
+++ b/solution.py
@@ -330,7 +330,7 @@
         history[layer + 1, 1] = im
         return carry
 
-    lax.fori_loop(0, layers - 1, forward, 0)
+    lax.fori_loop(0, layers - 1, forward, 0, unroll=True)
     re, im = mixed(layers - 1)
     for copy in settings[2:]:
         copy.wait()
@@ -369,7 +369,7 @@
         collect(layers - 2 - step, back_re, back_im)
         return carry
 
-    lax.fori_loop(0, layers - 1, backward, 0)
+    lax.fori_loop(0, layers - 1, backward, 0, unroll=True)
     grad[0], grad[1] = mirror_halves([grad[0], grad[1]], reversal(size // 2))
     shares = []
     for offset in range(peers):

time: 168 us -> 167 us (level)
  no operation moved by 1% of the time
where the time goes in v5:
time: 167 us; the launch traced here: 166 us
  waiting for transfers between devices  81.9 us (49%)
  Pallas kernels  41.5 us (25%)
  starting transfers between devices  39.2 us (23%)
  other arithmetic  2.13 us (1%)
    ppermute x8, waiting for transfers between devices, shift(): lax.ppermute(x, axis, [(i, i + by) for i in range(peers) if 0 <= i + by <...  41.3 us
    ppermute x36, waiting for transfers between devices, swap(): return lax.ppermute(x, axis, [(i, i ^ offset) for i in range(peers)])  40.6 us
    ppermute x8, starting transfers between devices, shift(): lax.ppermute(x, axis, [(i, i + by) for i in range(peers) if 0 <= i + by <...  20 us
    ppermute x36, starting transfers between devices, swap(): return lax.ppermute(x, axis, [(i, i ^ offset) for i in range(peers)])  19.1 us
    pallas_call x1, Pallas kernels, body(): run_kernel(functools.partial(optics_kernel, peers, per_device), 'optics',...  16.8 us
    pallas_call x4, Pallas kernels, body(): run_kernel(functools.partial(crop_kernel, peers, c, len(waits)), 'crop',...  10.9 us
    pallas_call x4, Pallas kernels, body(): run_kernel(functools.partial(place_kernel, peers, len(waits)), 'place', (...  8.2 us
    pallas_call x2, Pallas kernels, strips_of(): run_kernel(functools.partial(strip_kernel, planes, len(waits)), 'strip',...  4.21 us
  transfers between devices with their start and end apart: 44, of which 28 were waited for; matrix products, arithmetic and copies ran while one was open for 0% of the time, Pallas kernels for 14%

profile of v5, /device:TPU:4, one launch (start us, length us, event | category | flops | bytes accessed | tf_op | source)
XLA Modules:
  0.0 166.2 jit_solution(15934117821562156895)
XLA Ops:
  4.5 2.4 %strip.3 = (f32[256,512]{1,0:T(8,128)}, f32[256,512]{1,0:T(8,128)}, f32[256,512]{1,0:T(8,128)}) custom-call(f32[2,2,256,512]{3,2,1,0:T(8,128)} %strips.11, f32[256,512]{1,0:T(8,128)} %strip.2.rest_0_), custom_call_target="tpu_custom_call" | custom-call | flops 1000000 | bytes 1000 | tf_op jit(solution)/shard_map/strip/pallas_call | solution.py:486
  8.3 1.9 %collective-permute-start.4 = (f32[256,512]{1,0:T(8,128)}, f32[256,512]{1,0:T(8,128)}, u32[]{:S(2)}, u32[]{:S(2)}) collective-permute-start(f32[256,512]{1,0:T(8,128)} %gate.16), channel_id=1, source_target_pairs={{1,0},{2,1},{3,2},{4,3},{5,4},{6,5},{7,6},{9,8},{10,9},{11,10},{12... | collective-permute-start | bytes 1572872 | tf_op jit(solution)/shard_map/ppermute | solution.py:461
  10.3 10.0 %collective-permute-done.rim = f32[256,512]{1,0:T(8,128)S(1)} collective-permute-done((f32[256,512]{1,0:T(8,128)}, f32[256,512]{1,0:T(8,128)S(1)}, u32[]{:S(2)}, u32[]{:S(2)}) %collective-permute-start) | collective-permute-done | bytes 524320 | tf_op jit(solution)/shard_map/ppermute | solution.py:461
  20.3 2.5 %crop.4 = (f32[256,256]{1,0:T(8,128)S(1)}, f32[256,256]{1,0:T(8,128)S(1)}, f32[2,256,256]{2,1,0:T(8,128)S(1)}) custom-call(s32[2]{0:T(128)S(1)} %pad_add_fusion.ids, s32[4,2]{1,0:T(4,128)S(1)} %copy.37.positions, f32[2,2,256,512]{3,2,1,0:T(8,128)S(1)} %copy-done, f32[256,512]{1,0:T(8,128)S(1)} %collective-permute-done.rim, ...), custom_call_target="tpu_custom_call" | custom-call | flops 2000000 | bytes 2000 | tf_op jit(solution)/shard_map/crop/pallas_call | solution.py:506
  24.3 2.0 %collective-permute-start.8 = (f32[256,512]{1,0:T(8,128)S(1)}, f32[256,512]{1,0:T(8,128)S(1)}, u32[]{:S(2)}, u32[]{:S(2)}) collective-permute-start(f32[256,512]{1,0:T(8,128)S(1)} %gate.17), channel_id=1, source_target_pairs={{1,0},{2,1},{3,2},{4,3},{5,4},{6,5},{7,6},{9,8},{10,9},{11,10},{12... | collective-permute-start | bytes 1572872 | tf_op jit(solution)/shard_map/ppermute | solution.py:461
  26.4 5.2 %collective-permute-done.4.rim = f32[256,512]{1,0:T(8,128)} collective-permute-done((f32[256,512]{1,0:T(8,128)}, f32[256,512]{1,0:T(8,128)}, u32[]{:S(2)}, u32[]{:S(2)}) %collective-permute-start.4) | collective-permute-done | bytes 524320 | tf_op jit(solution)/shard_map/ppermute | solution.py:461
  31.6 3.4 %crop.5 = (f32[256,256]{1,0:T(8,128)S(1)}, f32[256,256]{1,0:T(8,128)S(1)}, f32[2,256,256]{2,1,0:T(8,128)S(1)}) custom-call(s32[2]{0:T(128)S(1)} %pad_add_fusion.ids, s32[4,2]{1,0:T(4,128)S(1)} %copy.37.positions, f32[2,2,256,512]{3,2,1,0:T(8,128)S(1)} %copy-done, f32[256,512]{1,0:T(8,128)} %collective-permute-done.4.rim, ...), custom_call_target="tpu_custom_call" | custom-call | flops 2000000 | bytes 2000 | tf_op jit(solution)/shard_map/crop/pallas_call | solution.py:506
  36.6 2.1 %collective-permute-start.12 = (f32[256,512]{1,0:T(8,128)S(1)}, f32[256,512]{1,0:T(8,128)S(1)}, u32[]{:S(2)}, u32[]{:S(2)}) collective-permute-start(f32[256,512]{1,0:T(8,128)S(1)} %gate.18), channel_id=1, source_target_pairs={{1,0},{2,1},{3,2},{4,3},{5,4},{6,5},{7,6},{9,8},{10,9},{11,10},{12... | collective-permute-start | bytes 1572872 | tf_op jit(solution)/shard_map/ppermute | solution.py:461
  38.7 4.0 %collective-permute-done.8.rim = f32[256,512]{1,0:T(8,128)S(1)} collective-permute-done((f32[256,512]{1,0:T(8,128)S(1)}, f32[256,512]{1,0:T(8,128)S(1)}, u32[]{:S(2)}, u32[]{:S(2)}) %collective-permute-start.8) | collective-permute-done | bytes 524320 | tf_op jit(solution)/shard_map/ppermute | solution.py:461
  42.8 2.5 %crop.6 = (f32[256,256]{1,0:T(8,128)S(1)}, f32[256,256]{1,0:T(8,128)S(1)}, f32[2,256,256]{2,1,0:T(8,128)S(1)}) custom-call(s32[2]{0:T(128)S(1)} %pad_add_fusion.ids, s32[4,2]{1,0:T(4,128)S(1)} %copy.37.positions, f32[2,2,256,512]{3,2,1,0:T(8,128)S(1)} %copy-done, f32[256,512]{1,0:T(8,128)S(1)} %collective-permute-done.8.rim, ...), custom_call_target="tpu_custom_call" | custom-call | flops 2000000 | bytes 2000 | tf_op jit(solution)/shard_map/crop/pallas_call | solution.py:506
  47.8 5.1 %collective-permute-done.12.rim = f32[256,512]{1,0:T(8,128)S(1)} collective-permute-done((f32[256,512]{1,0:T(8,128)S(1)}, f32[256,512]{1,0:T(8,128)S(1)}, u32[]{:S(2)}, u32[]{:S(2)}) %collective-permute-start.12) | collective-permute-done | bytes 524320 | tf_op jit(solution)/shard_map/ppermute | solution.py:461
  52.9 2.5 %crop.7 = (f32[256,256]{1,0:T(8,128)S(1)}, f32[256,256]{1,0:T(8,128)S(1)}, f32[2,256,256]{2,1,0:T(8,128)S(1)}) custom-call(s32[2]{0:T(128)S(1)} %pad_add_fusion.ids, s32[4,2]{1,0:T(4,128)S(1)} %copy.37.positions, f32[2,2,256,512]{3,2,1,0:T(8,128)S(1)} %copy-done, f32[256,512]{1,0:T(8,128)S(1)} %collective-permute-done.12.rim, ...), custom_call_target="tpu_custom_call" | custom-call | flops 2000000 | bytes 2000 | tf_op jit(solution)/shard_map/crop/pallas_call | solution.py:506
  57.1 2.2 %collective-permute-done.10.rest_10_ = f32[2,256,256]{2,1,0:T(8,128)S(1)} collective-permute-done((f32[2,256,256]{2,1,0:T(8,128)S(1)}, f32[2,256,256]{2,1,0:T(8,128)S(1)}, u32[]{:S(2)}, u32[]{:S(2)}) %collective-permute-start.10) | collective-permute-done | bytes 524320 | tf_op jit(solution)/shard_map/ppermute | solution.py:443
  60.8 8.5 %collective-permute-done.14.refs_0_ = f32[2,256,256]{2,1,0:T(8,128)S(1)} collective-permute-done((f32[2,256,256]{2,1,0:T(8,128)S(1)}, f32[2,256,256]{2,1,0:T(8,128)S(1)}, u32[]{:S(2)}, u32[]{:S(2)}) %collective-permute-start.14) | collective-permute-done | bytes 524320 | tf_op jit(solution)/shard_map/ppermute | solution.py:443
  70.9 16.8 %optics.1 = (f32[256,256]{1,0:T(8,128)S(1)}, f32[256,256]{1,0:T(8,128)S(1)}, f32[2,256,256]{2,1,0:T(8,128)S(1)}, f32[256,256]{1,0:T(8,128)S(1)}, f32[256,256]{1,...) custom-call(s32[2]{0:T(128)S(1)} %pad_add_fusion.ids, ...), custom_call_target="tpu_custom_call" | custom-call | flops 15000000 | bytes 15000 | tf_op jit(solution)/shard_map/optics/pallas_call | solution.py:524
  90.9 4.1 %collective-permute-done.18 = f32[1,2,64,256]{3,2,1,0:T(8,128)S(1)} collective-permute-done((f32[1,2,64,256]{3,2,1,0:T(8,128)S(1)}, f32[1,2,64,256]{3,2,1,0:T(8,128)S(1)}, u32[]{:S(2)}, u32[]{:S(2)}) %collective-permute-start.18) | collective-permute-done | bytes 131104 | tf_op jit(solution)/shard_map/ppermute | solution.py:443
  96.6 2.6 %collective-permute-start.21 = (f32[2,64,256]{2,1,0:T(8,128)S(1)}, f32[2,64,256]{2,1,0:T(8,128)S(1)}, u32[]{:S(2)}, u32[]{:S(2)}) collective-permute-start(f32[2,64,256]{2,1,0:T(8,128)S(1)} %fusion.refs_3_), channel_id=1, source_target_pairs={{0,4},{1,5},{2,6},{3,7},{4,0},{5,1},{6,2},{7,3},{8,12},{9,13},{10,... | collective-permute-start | bytes 393224 | tf_op jit(solution)/shard_map/ppermute | solution.py:443
  99.2 5.6 %collective-permute-done.21 = f32[2,64,256]{2,1,0:T(8,128)S(1)} collective-permute-done((f32[2,64,256]{2,1,0:T(8,128)S(1)}, f32[2,64,256]{2,1,0:T(8,128)S(1)}, u32[]{:S(2)}, u32[]{:S(2)}) %collective-permute-start.21) | collective-permute-done | bytes 131104 | tf_op jit(solution)/shard_map/ppermute | solution.py:443
  105.4 4.4 %collective-permute-done.22 = f32[2,64,256]{2,1,0:T(8,128)S(1)} collective-permute-done((f32[2,64,256]{2,1,0:T(8,128)S(1)}, f32[2,64,256]{2,1,0:T(8,128)S(1)}, u32[]{:S(2)}, u32[]{:S(2)}) %collective-permute-start.22) | collective-permute-done | bytes 131104 | tf_op jit(solution)/shard_map/ppermute | solution.py:443
  111.6 2.0 %place.4 = (f32[256,512]{1,0:T(8,128)S(1)}, f32[256,512]{1,0:T(8,128)S(1)}) custom-call(s32[2]{0:T(128)S(1)} %pad_add_fusion.ids, s32[4,2]{1,0:T(4,128)S(1)} %copy.37.positions, f32[256,256]{1,0:T(8,128)S(1)} %get-tuple-element.76.rest_0_, f32[256,256]{1,0:T(8,128)S(1)} %collective-permute-done.19.rest_1_, f32[2,256,256]{2,1,0:T(8,128)S(1)} %gate.21.rest_2_, ...), custom_call_target="tpu_custom_call" | custom-call | flops 2000000 | bytes 2000 | tf_op jit(solution)/shard_map/place/pallas_call | solution.py:573
  113.6 3.4 %collective-permute-start.33 = (f32[256,512]{1,0:T(8,128)S(1)}, f32[256,512]{1,0:T(8,128)S(1)}, u32[]{:S(2)}, u32[]{:S(2)}) collective-permute-start(f32[256,512]{1,0:T(8,128)S(1)} %get-tuple-element.92), channel_id=1, source_target_pairs={{0,1},{1,2},{2,3},{3,4},{4,5},{5,6},{6,7},{8,9},{9,10},{10,11},{11... | collective-permute-start | bytes 1572872 | tf_op jit(solution)/shard_map/ppermute | solution.py:461
  117.1 2.4 %collective-permute-done.16.refs_0_ = f32[2,256,256]{2,1,0:T(8,128)S(1)} collective-permute-done((f32[2,256,256]{2,1,0:T(8,128)S(1)}, f32[2,256,256]{2,1,0:T(8,128)S(1)}, u32[]{:S(2)}, u32[]{:S(2)}) %collective-permute-start.16) | collective-permute-done | bytes 524320 | tf_op jit(solution)/shard_map/ppermute | solution.py:443
  124.0 2.1 %place.5 = (f32[256,512]{1,0:T(8,128)S(1)}, f32[256,512]{1,0:T(8,128)S(1)}) custom-call(s32[2]{0:T(128)S(1)} %pad_add_fusion.ids, s32[4,2]{1,0:T(4,128)S(1)} %copy.37.positions, f32[256,256]{1,0:T(8,128)S(1)} %get-tuple-element.80.rest_0_, f32[256,256]{1,0:T(8,128)S(1)} %collective-permute-done.24.rest_1_, f32[2,256,256]{2,1,0:T(8,128)S(1)} %gate.22.rest_2_.refs_3_, ...), custom_call_target="tpu_custom_call" | custom-call | flops 2000000 | bytes 2000 | tf_op jit(solution)/shard_map/place/pallas_call | solution.py:573
  126.1 2.5 %collective-permute-start.36 = (f32[256,512]{1,0:T(8,128)S(1)}, f32[256,512]{1,0:T(8,128)S(1)}, u32[]{:S(2)}, u32[]{:S(2)}) collective-permute-start(f32[256,512]{1,0:T(8,128)S(1)} %get-tuple-element.96), channel_id=1, source_target_pairs={{0,1},{1,2},{2,3},{3,4},{4,5},{5,6},{6,7},{8,9},{9,10},{10,11},{11... | collective-permute-start | bytes 1572872 | tf_op jit(solution)/shard_map/ppermute | solution.py:461
  129.5 2.5 %collective-permute-done.32.refs_0_ = f32[2,256,256]{2,1,0:T(8,128)S(1)} collective-permute-done((f32[2,256,256]{2,1,0:T(8,128)S(1)}, f32[2,256,256]{2,1,0:T(8,128)S(1)}, u32[]{:S(2)}, u32[]{:S(2)}) %collective-permute-start.32) | collective-permute-done | bytes 524320 | tf_op jit(solution)/shard_map/ppermute | solution.py:443
  133.8 2.0 %place.6 = (f32[256,512]{1,0:T(8,128)S(1)}, f32[256,512]{1,0:T(8,128)S(1)}) custom-call(s32[2]{0:T(128)S(1)} %pad_add_fusion.ids, s32[4,2]{1,0:T(4,128)S(1)} %copy.37.positions, f32[256,256]{1,0:T(8,128)S(1)} %get-tuple-element.89.rest_0_, f32[256,256]{1,0:T(8,128)S(1)} %collective-permute-done.31.rest_1_, f32[2,256,256]{2,1,0:T(8,128)S(1)} %gate.25.rest_2_, ...), custom_call_target="tpu_custom_call" | custom-call | flops 2000000 | bytes 2000 | tf_op jit(solution)/shard_map/place/pallas_call | solution.py:573
  135.9 2.2 %collective-permute-start.42 = (f32[256,512]{1,0:T(8,128)S(1)}, f32[256,512]{1,0:T(8,128)S(1)}, u32[]{:S(2)}, u32[]{:S(2)}) collective-permute-start(f32[256,512]{1,0:T(8,128)S(1)} %gate.30), channel_id=1, source_target_pairs={{0,1},{1,2},{2,3},{3,4},{4,5},{5,6},{6,7},{8,9},{9,10},{10,11},{11... | collective-permute-start | bytes 1572872 | tf_op jit(solution)/shard_map/ppermute | solution.py:461
  138.3 4.5 %collective-permute-done.36.refs_0_ = f32[256,512]{1,0:T(8,128)S(1)} collective-permute-done((f32[256,512]{1,0:T(8,128)S(1)}, f32[256,512]{1,0:T(8,128)S(1)}, u32[]{:S(2)}, u32[]{:S(2)}) %collective-permute-start.36) | collective-permute-done | bytes 524320 | tf_op jit(solution)/shard_map/ppermute | solution.py:461
  144.5 2.0 %place.7 = (f32[256,512]{1,0:T(8,128)S(1)}, f32[256,512]{1,0:T(8,128)S(1)}) custom-call(s32[2]{0:T(128)S(1)} %pad_add_fusion.ids, s32[4,2]{1,0:T(4,128)S(1)} %copy.37.positions, f32[256,256]{1,0:T(8,128)S(1)} %get-tuple-element.83.rest_0_, f32[256,256]{1,0:T(8,128)S(1)} %collective-permute-done.29.rest_1_, f32[2,256,256]{2,1,0:T(8,128)S(1)} %gate.26.rest_2_, ...), custom_call_target="tpu_custom_call" | custom-call | flops 2000000 | bytes 2000 | tf_op jit(solution)/shard_map/place/pallas_call | solution.py:573
  146.6 3.9 %collective-permute-start.39 = (f32[256,512]{1,0:T(8,128)S(1)}, f32[256,512]{1,0:T(8,128)S(1)}, u32[]{:S(2)}, u32[]{:S(2)}) collective-permute-start(f32[256,512]{1,0:T(8,128)S(1)} %gate.28), channel_id=1, source_target_pairs={{0,1},{1,2},{2,3},{3,4},{4,5},{5,6},{6,7},{8,9},{9,10},{10,11},{11... | collective-permute-start | bytes 1572872 | tf_op jit(solution)/shard_map/ppermute | solution.py:461
  150.5 3.4 %collective-permute-done.42.refs_0_ = f32[256,512]{1,0:T(8,128)S(1)} collective-permute-done((f32[256,512]{1,0:T(8,128)S(1)}, f32[256,512]{1,0:T(8,128)S(1)}, u32[]{:S(2)}, u32[]{:S(2)}) %collective-permute-start.42) | collective-permute-done | bytes 524320 | tf_op jit(solution)/shard_map/ppermute | solution.py:461
  155.7 8.8 %collective-permute-done.39 = f32[256,512]{1,0:T(8,128)S(1)} collective-permute-done((f32[256,512]{1,0:T(8,128)S(1)}, f32[256,512]{1,0:T(8,128)S(1)}, u32[]{:S(2)}, u32[]{:S(2)}) %collective-permute-start.39) | collective-permute-done | bytes 524320 | tf_op jit(solution)/shard_map/ppermute | solution.py:461
  (128 shorter events, 35.4 us)
Async XLA Ops:
  2.5 17.8 %collective-permute-start = (f32[256,512]{1,0:T(8,128)}, f32[256,512]{1,0:T(8,128)S(1)}, u32[]{:S(2)}, u32[]{:S(2)}) collective-permute-start(f32[256,512]{1,0:T(8,128)} %strip.2.rest_0_), channel_id=1, source_target_pairs={{1,0},{2,1},{3,2},{4,3},{5,4},{6,5},{7,6},{9,8},{10,9},{11,10},{12... | collective-permute-start | bytes 1572872 | tf_op jit(solution)/shard_map/ppermute | solution.py:461
  8.3 23.4 %collective-permute-start.4 = (f32[256,512]{1,0:T(8,128)}, f32[256,512]{1,0:T(8,128)}, u32[]{:S(2)}, u32[]{:S(2)}) collective-permute-start(f32[256,512]{1,0:T(8,128)} %gate.16), channel_id=1, source_target_pairs={{1,0},{2,1},{3,2},{4,3},{5,4},{6,5},{7,6},{9,8},{10,9},{11,10},{12... | collective-permute-start | bytes 1572872 | tf_op jit(solution)/shard_map/ppermute | solution.py:461
  22.8 16.0 %collective-permute-start.2 = (f32[2,256,256]{2,1,0:T(8,128)S(1)}, f32[2,256,256]{2,1,0:T(8,128)S(1)}, u32[]{:S(2)}, u32[]{:S(2)}) collective-permute-start(f32[2,256,256]{2,1,0:T(8,128)S(1)} %get-tuple-element.54), channel_id=1, source_target_pairs={{0,16},{8,24},{16,0},{24,8},{1,17},{9,25},{17,1},{25,9},{2,18},{10... | collective-permute-start | bytes 1572872 | tf_op jit(solution)/shard_map/ppermute | solution.py:443
  24.3 18.4 %collective-permute-start.8 = (f32[256,512]{1,0:T(8,128)S(1)}, f32[256,512]{1,0:T(8,128)S(1)}, u32[]{:S(2)}, u32[]{:S(2)}) collective-permute-start(f32[256,512]{1,0:T(8,128)S(1)} %gate.17), channel_id=1, source_target_pairs={{1,0},{2,1},{3,2},{4,3},{5,4},{6,5},{7,6},{9,8},{10,9},{11,10},{12... | collective-permute-start | bytes 1572872 | tf_op jit(solution)/shard_map/ppermute | solution.py:461
  35.1 12.7 %collective-permute-start.6 = (f32[2,256,256]{2,1,0:T(8,128)S(1)}, f32[2,256,256]{2,1,0:T(8,128)S(1)}, u32[]{:S(2)}, u32[]{:S(2)}) collective-permute-start(f32[2,256,256]{2,1,0:T(8,128)S(1)} %get-tuple-element.58), channel_id=1, source_target_pairs={{0,16},{8,24},{16,0},{24,8},{1,17},{9,25},{17,1},{25,9},{2,18},{10... | collective-permute-start | bytes 1572872 | tf_op jit(solution)/shard_map/ppermute | solution.py:443
  36.6 16.2 %collective-permute-start.12 = (f32[256,512]{1,0:T(8,128)S(1)}, f32[256,512]{1,0:T(8,128)S(1)}, u32[]{:S(2)}, u32[]{:S(2)}) collective-permute-start(f32[256,512]{1,0:T(8,128)S(1)} %gate.18), channel_id=1, source_target_pairs={{1,0},{2,1},{3,2},{4,3},{5,4},{6,5},{7,6},{9,8},{10,9},{11,10},{12... | collective-permute-start | bytes 1572872 | tf_op jit(solution)/shard_map/ppermute | solution.py:461
  45.3 14.0 %collective-permute-start.10 = (f32[2,256,256]{2,1,0:T(8,128)S(1)}, f32[2,256,256]{2,1,0:T(8,128)S(1)}, u32[]{:S(2)}, u32[]{:S(2)}) collective-permute-start(f32[2,256,256]{2,1,0:T(8,128)S(1)} %get-tuple-element.62), channel_id=1, source_target_pairs={{0,16},{8,24},{16,0},{24,8},{1,17},{9,25},{17,1},{25,9},{2,18},{10... | collective-permute-start | bytes 1572872 | tf_op jit(solution)/shard_map/ppermute | solution.py:443
  46.8 12.5 %collective-permute-start.1 = (f32[256,256]{1,0:T(8,128)S(1)}, f32[256,256]{1,0:T(8,128)S(1)}, u32[]{:S(2)}, u32[]{:S(2)}) collective-permute-start(f32[256,256]{1,0:T(8,128)S(1)} %get-tuple-element.53), channel_id=1, source_target_pairs={{0,8},{8,0},{16,24},{24,16},{1,9},{9,1},{17,25},{25,17},{2,10},{10... | collective-permute-start | bytes 786440 | tf_op jit(solution)/shard_map/ppermute | solution.py:443
  46.8 13.0 %collective-permute-start.5 = (f32[256,256]{1,0:T(8,128)S(1)}, f32[256,256]{1,0:T(8,128)S(1)}, u32[]{:S(2)}, u32[]{:S(2)}) collective-permute-start(f32[256,256]{1,0:T(8,128)S(1)} %get-tuple-element.57), channel_id=1, source_target_pairs={{0,8},{8,0},{16,24},{24,16},{1,9},{9,1},{17,25},{25,17},{2,10},{10... | collective-permute-start | bytes 786440 | tf_op jit(solution)/shard_map/ppermute | solution.py:443
  55.4 13.9 %collective-permute-start.14 = (f32[2,256,256]{2,1,0:T(8,128)S(1)}, f32[2,256,256]{2,1,0:T(8,128)S(1)}, u32[]{:S(2)}, u32[]{:S(2)}) collective-permute-start(f32[2,256,256]{2,1,0:T(8,128)S(1)} %get-tuple-element.66), channel_id=1, source_target_pairs={{0,16},{8,24},{16,0},{24,8},{1,17},{9,25},{17,1},{25,9},{2,18},{10... | collective-permute-start | bytes 1572872 | tf_op jit(solution)/shard_map/ppermute | solution.py:443
  56.9 3.0 %collective-permute-start.3 = (f32[256,256]{1,0:T(8,128)S(1)}, f32[256,256]{1,0:T(8,128)S(1)}, u32[]{:S(2)}, u32[]{:S(2)}) collective-permute-start(f32[256,256]{1,0:T(8,128)S(1)} %slice_bitcast_fusion.7), channel_id=1, source_target_pairs={{0,8},{8,0},{16,24},{24,16},{1,9},{9,1},{17,25},{25,17},{2,10},{10... | collective-permute-start | bytes 786440 | tf_op jit(solution)/shard_map/ppermute | solution.py:443
  59.3 10.1 %collective-permute-start.9 = (f32[256,256]{1,0:T(8,128)S(1)}, f32[256,256]{1,0:T(8,128)S(1)}, u32[]{:S(2)}, u32[]{:S(2)}) collective-permute-start(f32[256,256]{1,0:T(8,128)S(1)} %get-tuple-element.61), channel_id=1, source_target_pairs={{0,8},{8,0},{16,24},{24,16},{1,9},{9,1},{17,25},{25,17},{2,10},{10... | collective-permute-start | bytes 786440 | tf_op jit(solution)/shard_map/ppermute | solution.py:443
  59.8 9.5 %collective-permute-start.13 = (f32[256,256]{1,0:T(8,128)S(1)}, f32[256,256]{1,0:T(8,128)S(1)}, u32[]{:S(2)}, u32[]{:S(2)}) collective-permute-start(f32[256,256]{1,0:T(8,128)S(1)} %get-tuple-element.65), channel_id=1, source_target_pairs={{0,8},{8,0},{16,24},{24,16},{1,9},{9,1},{17,25},{25,17},{2,10},{10... | collective-permute-start | bytes 786440 | tf_op jit(solution)/shard_map/ppermute | solution.py:443
  59.9 9.4 %collective-permute-start.11 = (f32[256,256]{1,0:T(8,128)S(1)}, f32[256,256]{1,0:T(8,128)S(1)}, u32[]{:S(2)}, u32[]{:S(2)}) collective-permute-start(f32[256,256]{1,0:T(8,128)S(1)} %slice_bitcast_fusion.5), channel_id=1, source_target_pairs={{0,8},{8,0},{16,24},{24,16},{1,9},{9,1},{17,25},{25,17},{2,10},{10... | collective-permute-start | bytes 786440 | tf_op jit(solution)/shard_map/ppermute | solution.py:443
  89.4 5.6 %collective-permute-start.18 = (f32[1,2,64,256]{3,2,1,0:T(8,128)S(1)}, f32[1,2,64,256]{3,2,1,0:T(8,128)S(1)}, u32[]{:S(2)}, u32[]{:S(2)}) collective-permute-start(f32[1,2,64,256]{3,2,1,0:T(8,128)S(1)} %slice.57), channel_id=1, source_target_pairs={{0,16},{8,24},{16,0},{24,8},{1,17},{9,25},{17,1},{25,9},{2,18},{10... | collective-permute-start | bytes 393224 | tf_op jit(solution)/shard_map/ppermute | solution.py:443
  95.0 14.9 %collective-permute-start.20 = (f32[2,256,256]{2,1,0:T(8,128)S(1)}, f32[2,256,256]{2,1,0:T(8,128)S(1)}, u32[]{:S(2)}, u32[]{:S(2)}) collective-permute-start(f32[2,256,256]{2,1,0:T(8,128)S(1)} %get-tuple-element.78), channel_id=1, source_target_pairs={{0,16},{8,24},{16,0},{24,8},{1,17},{9,25},{17,1},{25,9},{2,18},{10... | collective-permute-start | bytes 1572872 | tf_op jit(solution)/shard_map/ppermute | solution.py:443
  96.6 8.1 %collective-permute-start.21 = (f32[2,64,256]{2,1,0:T(8,128)S(1)}, f32[2,64,256]{2,1,0:T(8,128)S(1)}, u32[]{:S(2)}, u32[]{:S(2)}) collective-permute-start(f32[2,64,256]{2,1,0:T(8,128)S(1)} %fusion.refs_3_), channel_id=1, source_target_pairs={{0,4},{1,5},{2,6},{3,7},{4,0},{5,1},{6,2},{7,3},{8,12},{9,13},{10,... | collective-permute-start | bytes 393224 | tf_op jit(solution)/shard_map/ppermute | solution.py:443
  104.8 5.0 %collective-permute-start.22 = (f32[2,64,256]{2,1,0:T(8,128)S(1)}, f32[2,64,256]{2,1,0:T(8,128)S(1)}, u32[]{:S(2)}, u32[]{:S(2)}) collective-permute-start(f32[2,64,256]{2,1,0:T(8,128)S(1)} %add.29), channel_id=1, source_target_pairs={{0,2},{1,3},{2,0},{3,1},{4,6},{5,7},{6,4},{7,5},{8,10},{9,11},{10,... | collective-permute-start | bytes 393224 | tf_op jit(solution)/shard_map/ppermute | solution.py:443
  104.8 14.6 %collective-permute-start.16 = (f32[2,256,256]{2,1,0:T(8,128)S(1)}, f32[2,256,256]{2,1,0:T(8,128)S(1)}, u32[]{:S(2)}, u32[]{:S(2)}) collective-permute-start(f32[2,256,256]{2,1,0:T(8,128)S(1)} %get-tuple-element.70), channel_id=1, source_target_pairs={{0,16},{8,24},{16,0},{24,8},{1,17},{9,25},{17,1},{25,9},{2,18},{10... | collective-permute-start | bytes 1572872 | tf_op jit(solution)/shard_map/ppermute | solution.py:443
  105.4 4.7 %collective-permute-start.19 = (f32[256,256]{1,0:T(8,128)S(1)}, f32[256,256]{1,0:T(8,128)S(1)}, u32[]{:S(2)}, u32[]{:S(2)}) collective-permute-start(f32[256,256]{1,0:T(8,128)S(1)} %get-tuple-element.77), channel_id=1, source_target_pairs={{0,8},{8,0},{16,24},{24,16},{1,9},{9,1},{17,25},{25,17},{2,10},{10... | collective-permute-start | bytes 786440 | tf_op jit(solution)/shard_map/ppermute | solution.py:443
  110.1 10.9 %collective-permute-start.26 = (f32[2,64,256]{2,1,0:T(8,128)S(1)}, f32[2,64,256]{2,1,0:T(8,128)S(1)}, u32[]{:S(2)}, u32[]{:S(2)}) collective-permute-start(f32[2,64,256]{2,1,0:T(8,128)S(1)} %add.30.refs_1_), channel_id=1, source_target_pairs={{0,1},{1,0},{2,3},{3,2},{4,5},{5,4},{6,7},{7,6},{8,9},{9,8},{10,11... | collective-permute-start | bytes 393224 | tf_op jit(solution)/shard_map/ppermute | solution.py:443
  113.6 15.9 %collective-permute-start.33 = (f32[256,512]{1,0:T(8,128)S(1)}, f32[256,512]{1,0:T(8,128)S(1)}, u32[]{:S(2)}, u32[]{:S(2)}) collective-permute-start(f32[256,512]{1,0:T(8,128)S(1)} %get-tuple-element.92), channel_id=1, source_target_pairs={{0,1},{1,2},{2,3},{3,4},{4,5},{5,6},{6,7},{8,9},{9,10},{10,11},{11... | collective-permute-start | bytes 1572872 | tf_op jit(solution)/shard_map/ppermute | solution.py:461
  119.5 12.6 %collective-permute-start.32 = (f32[2,256,256]{2,1,0:T(8,128)S(1)}, f32[2,256,256]{2,1,0:T(8,128)S(1)}, u32[]{:S(2)}, u32[]{:S(2)}) collective-permute-start(f32[2,256,256]{2,1,0:T(8,128)S(1)} %get-tuple-element.91), channel_id=1, source_target_pairs={{0,16},{8,24},{16,0},{24,8},{1,17},{9,25},{17,1},{25,9},{2,18},{10... | collective-permute-start | bytes 1572872 | tf_op jit(solution)/shard_map/ppermute | solution.py:443
  121.6 2.4 %collective-permute-start.25 = (f32[256,256]{1,0:T(8,128)S(1)}, f32[256,256]{1,0:T(8,128)S(1)}, u32[]{:S(2)}, u32[]{:S(2)}) collective-permute-start(f32[256,256]{1,0:T(8,128)S(1)} %slice_bitcast_fusion.2), channel_id=1, source_target_pairs={{0,8},{8,0},{16,24},{24,16},{1,9},{9,1},{17,25},{25,17},{2,10},{10... | collective-permute-start | bytes 786440 | tf_op jit(solution)/shard_map/ppermute | solution.py:443
  126.1 16.6 %collective-permute-start.36 = (f32[256,512]{1,0:T(8,128)S(1)}, f32[256,512]{1,0:T(8,128)S(1)}, u32[]{:S(2)}, u32[]{:S(2)}) collective-permute-start(f32[256,512]{1,0:T(8,128)S(1)} %get-tuple-element.96), channel_id=1, source_target_pairs={{0,1},{1,2},{2,3},{3,4},{4,5},{5,6},{6,7},{8,9},{9,10},{10,11},{11... | collective-permute-start | bytes 1572872 | tf_op jit(solution)/shard_map/ppermute | solution.py:461
  128.7 14.3 %collective-permute-start.30 = (f32[2,256,256]{2,1,0:T(8,128)S(1)}, f32[2,256,256]{2,1,0:T(8,128)S(1)}, u32[]{:S(2)}, u32[]{:S(2)}) collective-permute-start(f32[2,256,256]{2,1,0:T(8,128)S(1)} %get-tuple-element.85), channel_id=1, source_target_pairs={{0,16},{8,24},{16,0},{24,8},{1,17},{9,25},{17,1},{25,9},{2,18},{10... | collective-permute-start | bytes 1572872 | tf_op jit(solution)/shard_map/ppermute | solution.py:443
  129.2 4.6 %collective-permute-start.31 = (f32[256,256]{1,0:T(8,128)S(1)}, f32[256,256]{1,0:T(8,128)S(1)}, u32[]{:S(2)}, u32[]{:S(2)}) collective-permute-start(f32[256,256]{1,0:T(8,128)S(1)} %get-tuple-element.90), channel_id=1, source_target_pairs={{0,8},{8,0},{16,24},{24,16},{1,9},{9,1},{17,25},{25,17},{2,10},{10... | collective-permute-start | bytes 786440 | tf_op jit(solution)/shard_map/ppermute | solution.py:443
  133.7 2.2 %collective-permute-start.41 = (f32[8,128]{1,0:T(8,128)S(1)}, f32[8,128]{1,0:T(8,128)S(1)}, u32[]{:S(2)}, u32[]{:S(2)}) collective-permute-start(f32[8,128]{1,0:T(8,128)S(1)} %collective-permute-done.40), channel_id=1, source_target_pairs={{0,8},{8,0},{16,24},{24,16},{1,9},{9,1},{17,25},{25,17},{2,10},{10... | collective-permute-start | bytes 12296 | tf_op jit(solution)/shard_map/ppermute | solution.py:443
  135.9 18.1 %collective-permute-start.42 = (f32[256,512]{1,0:T(8,128)S(1)}, f32[256,512]{1,0:T(8,128)S(1)}, u32[]{:S(2)}, u32[]{:S(2)}) collective-permute-start(f32[256,512]{1,0:T(8,128)S(1)} %gate.30), channel_id=1, source_target_pairs={{0,1},{1,2},{2,3},{3,4},{4,5},{5,6},{6,7},{8,9},{9,10},{10,11},{11... | collective-permute-start | bytes 1572872 | tf_op jit(solution)/shard_map/ppermute | solution.py:461
  138.1 6.1 %collective-permute-start.29 = (f32[256,256]{1,0:T(8,128)S(1)}, f32[256,256]{1,0:T(8,128)S(1)}, u32[]{:S(2)}, u32[]{:S(2)}) collective-permute-start(f32[256,256]{1,0:T(8,128)S(1)} %get-tuple-element.84), channel_id=1, source_target_pairs={{0,8},{8,0},{16,24},{24,16},{1,9},{9,1},{17,25},{25,17},{2,10},{10... | collective-permute-start | bytes 786440 | tf_op jit(solution)/shard_map/ppermute | solution.py:443
  143.9 2.7 %collective-permute-start.38 = (f32[8,128]{1,0:T(8,128)S(1)}, f32[8,128]{1,0:T(8,128)S(1)}, u32[]{:S(2)}, u32[]{:S(2)}) collective-permute-start(f32[8,128]{1,0:T(8,128)S(1)} %collective-permute-done.37), channel_id=1, source_target_pairs={{0,8},{8,0},{16,24},{24,16},{1,9},{9,1},{17,25},{25,17},{2,10},{10... | collective-permute-start | bytes 12296 | tf_op jit(solution)/shard_map/ppermute | solution.py:443
  146.6 17.9 %collective-permute-start.39 = (f32[256,512]{1,0:T(8,128)S(1)}, f32[256,512]{1,0:T(8,128)S(1)}, u32[]{:S(2)}, u32[]{:S(2)}) collective-permute-start(f32[256,512]{1,0:T(8,128)S(1)} %gate.28), channel_id=1, source_target_pairs={{0,1},{1,2},{2,3},{3,4},{4,5},{5,6},{6,7},{8,9},{9,10},{10,11},{11... | collective-permute-start | bytes 1572872 | tf_op jit(solution)/shard_map/ppermute | solution.py:461
  (21 other events, 109.0 us)

commit v6 on v5

--- a/solution.py
+++ b/solution.py
@@ -86,7 +86,7 @@
     probe_out[0], probe_out[1], amp_out[...] = mirror_halves([probe[0], probe[1], amplitudes[ids[0]]], flip)
 
 
-def crop_kernel(peers, plane, waits, ids, positions, strips, rim, *rest):
+def crop_kernel(peers, waits, ids, positions, strip, rim, *rest):
     rest = rest[waits:]
     own_out, near_out = rest[:2]
     far_outs, rest = rest[2 : peers // 2 + 1], rest[peers // 2 + 1 :]
@@ -100,7 +100,7 @@
         columns = pl.ds(block * LANES, LANES)
         loads.append(
             pltpu.make_async_copy(
-                strips.at[plane[0], plane[1], :, columns], ext.at[block, pl.ds(0, rows)], loaded.at[2 * block]
+                strip.at[:, columns], ext.at[block, pl.ds(0, rows)], loaded.at[2 * block]
             )
         )
         loads.append(
@@ -504,7 +504,7 @@
         rim = shift(strips[k], "tile", -1)
         waits = crops[k - ahead][2::2] if k >= ahead else [probe, amplitude]
         mine = run_kernel(
-            functools.partial(crop_kernel, peers, c, len(waits)),
+            functools.partial(crop_kernel, peers, len(waits)),
             "crop",
             group,
             [SMEM_SPEC, SMEM_SPEC] + [HBM_SPEC] * (2 + len(waits)),
@@ -516,7 +516,7 @@
                 pltpu.SemaphoreType.DMA((peers,)),
             ],
             2,
-        )(ids, scan_positions, transmission, rim, *waits)
+        )(ids, scan_positions, strips[k], rim, *waits)
         strips[k + ahead : k + ahead + 1] = gate(strips[k + ahead : k + ahead + 1], mine[:1])
         early = [x for got in crops[:-1] for x in got[1:2] + got[3::2]] if k == len(chunks) - 1 else []
         crops.append(exchanged(mine, early))

time: 167 us -> 167 us (level)
  no operation moved by 1% of the time
where the time goes in v6:
time: 167 us; the launch traced here: 166 us
  waiting for transfers between devices  81.8 us (49%)
  Pallas kernels  41.5 us (25%)
  starting transfers between devices  39.2 us (23%)
  other arithmetic  2.17 us (1%)
    ppermute x8, waiting for transfers between devices, shift(): lax.ppermute(x, axis, [(i, i + by) for i in range(peers) if 0 <= i + by <...  41.7 us
    ppermute x36, waiting for transfers between devices, swap(): return lax.ppermute(x, axis, [(i, i ^ offset) for i in range(peers)])  40.1 us
    ppermute x8, starting transfers between devices, shift(): lax.ppermute(x, axis, [(i, i + by) for i in range(peers) if 0 <= i + by <...  20 us
    ppermute x36, starting transfers between devices, swap(): return lax.ppermute(x, axis, [(i, i ^ offset) for i in range(peers)])  19.1 us
    pallas_call x1, Pallas kernels, body(): run_kernel(functools.partial(optics_kernel, peers, per_device), 'optics',...  16.8 us
    pallas_call x4, Pallas kernels, body(): run_kernel(functools.partial(crop_kernel, peers, len(waits)), 'crop', gro...  10.9 us
    pallas_call x4, Pallas kernels, body(): run_kernel(functools.partial(place_kernel, peers, len(waits)), 'place', (...  8.18 us
    pallas_call x2, Pallas kernels, strips_of(): run_kernel(functools.partial(strip_kernel, planes, len(waits)), 'strip',...  4.22 us
  transfers between devices with their start and end apart: 44, of which 28 were waited for; matrix products, arithmetic and copies ran while one was open for 0% of the time, Pallas kernels for 14%

profile of v6, /device:TPU:4, one launch (start us, length us, event | category | flops | bytes accessed | tf_op | source)
XLA Modules:
  0.0 166.1 jit_solution(12837451920933376012)
XLA Ops:
  0.6 1.9 %strip.2.rest_0_ = f32[256,512]{1,0:T(8,128)} custom-call(f32[2,2,256,512]{3,2,1,0:T(8,128)} %strips.3), custom_call_target="tpu_custom_call" | custom-call | flops 1000000 | bytes 1000 | tf_op jit(solution)/shard_map/strip/pallas_call | solution.py:486
  2.6 1.9 %collective-permute-start = (f32[256,512]{1,0:T(8,128)}, f32[256,512]{1,0:T(8,128)S(1)}, u32[]{:S(2)}, u32[]{:S(2)}) collective-permute-start(f32[256,512]{1,0:T(8,128)} %strip.2.rest_0_), channel_id=1, source_target_pairs={{1,0},{2,1},{3,2},{4,3},{5,4},{6,5},{7,6},{9,8},{10,9},{11,10},{12... | collective-permute-start | bytes 1572872 | tf_op jit(solution)/shard_map/ppermute | solution.py:461
  4.6 2.3 %strip.3 = (f32[256,512]{1,0:T(8,128)}, f32[256,512]{1,0:T(8,128)}, f32[256,512]{1,0:T(8,128)}) custom-call(f32[2,2,256,512]{3,2,1,0:T(8,128)} %strips.3, f32[256,512]{1,0:T(8,128)} %strip.2.rest_0_), custom_call_target="tpu_custom_call" | custom-call | flops 1000000 | bytes 1000 | tf_op jit(solution)/shard_map/strip/pallas_call | solution.py:486
  8.3 1.9 %collective-permute-start.4 = (f32[256,512]{1,0:T(8,128)}, f32[256,512]{1,0:T(8,128)S(1)}, u32[]{:S(2)}, u32[]{:S(2)}) collective-permute-start(f32[256,512]{1,0:T(8,128)} %gate.16.strip), channel_id=1, source_target_pairs={{1,0},{2,1},{3,2},{4,3},{5,4},{6,5},{7,6},{9,8},{10,9},{11,10},{12... | collective-permute-start | bytes 1572872 | tf_op jit(solution)/shard_map/ppermute | solution.py:461
  10.3 10.1 %collective-permute-done.rim = f32[256,512]{1,0:T(8,128)S(1)} collective-permute-done((f32[256,512]{1,0:T(8,128)}, f32[256,512]{1,0:T(8,128)S(1)}, u32[]{:S(2)}, u32[]{:S(2)}) %collective-permute-start) | collective-permute-done | bytes 524320 | tf_op jit(solution)/shard_map/ppermute | solution.py:461
  20.4 2.5 %crop.4 = (f32[256,256]{1,0:T(8,128)S(1)}, f32[256,256]{1,0:T(8,128)S(1)}, f32[2,256,256]{2,1,0:T(8,128)S(1)}) custom-call(s32[2]{0:T(128)S(1)} %pad_add_fusion.ids, s32[4,2]{1,0:T(4,128)S(1)} %copy.37.positions, f32[256,512]{1,0:T(8,128)S(1)} %copy-done, f32[256,512]{1,0:T(8,128)S(1)} %collective-permute-done.rim, ...), custom_call_target="tpu_custom_call" | custom-call | flops 2000000 | bytes 2000 | tf_op jit(solution)/shard_map/crop/pallas_call | solution.py:506
  26.4 5.3 %collective-permute-done.4.rim = f32[256,512]{1,0:T(8,128)S(1)} collective-permute-done((f32[256,512]{1,0:T(8,128)}, f32[256,512]{1,0:T(8,128)S(1)}, u32[]{:S(2)}, u32[]{:S(2)}) %collective-permute-start.4) | collective-permute-done | bytes 524320 | tf_op jit(solution)/shard_map/ppermute | solution.py:461
  31.6 3.4 %crop.5 = (f32[256,256]{1,0:T(8,128)S(1)}, f32[256,256]{1,0:T(8,128)S(1)}, f32[2,256,256]{2,1,0:T(8,128)S(1)}) custom-call(s32[2]{0:T(128)S(1)} %pad_add_fusion.ids, s32[4,2]{1,0:T(4,128)S(1)} %copy.37.positions, f32[256,512]{1,0:T(8,128)} %gate.16.strip, f32[256,512]{1,0:T(8,128)S(1)} %collective-permute-done.4.rim, ...), custom_call_target="tpu_custom_call" | custom-call | flops 2000000 | bytes 2000 | tf_op jit(solution)/shard_map/crop/pallas_call | solution.py:506
  36.6 2.1 %collective-permute-start.12 = (f32[256,512]{1,0:T(8,128)S(1)}, f32[256,512]{1,0:T(8,128)S(1)}, u32[]{:S(2)}, u32[]{:S(2)}) collective-permute-start(f32[256,512]{1,0:T(8,128)S(1)} %gate.18.strip), channel_id=1, source_target_pairs={{1,0},{2,1},{3,2},{4,3},{5,4},{6,5},{7,6},{9,8},{10,9},{11,10},{12... | collective-permute-start | bytes 1572872 | tf_op jit(solution)/shard_map/ppermute | solution.py:461
  38.7 4.1 %collective-permute-done.8.rim = f32[256,512]{1,0:T(8,128)S(1)} collective-permute-done((f32[256,512]{1,0:T(8,128)S(1)}, f32[256,512]{1,0:T(8,128)S(1)}, u32[]{:S(2)}, u32[]{:S(2)}) %collective-permute-start.8) | collective-permute-done | bytes 524320 | tf_op jit(solution)/shard_map/ppermute | solution.py:461
  42.9 2.5 %crop.6 = (f32[256,256]{1,0:T(8,128)S(1)}, f32[256,256]{1,0:T(8,128)S(1)}, f32[2,256,256]{2,1,0:T(8,128)S(1)}) custom-call(s32[2]{0:T(128)S(1)} %pad_add_fusion.ids, s32[4,2]{1,0:T(4,128)S(1)} %copy.37.positions, f32[256,512]{1,0:T(8,128)S(1)} %gate.17.strip, f32[256,512]{1,0:T(8,128)S(1)} %collective-permute-done.8.rim, ...), custom_call_target="tpu_custom_call" | custom-call | flops 2000000 | bytes 2000 | tf_op jit(solution)/shard_map/crop/pallas_call | solution.py:506
  47.6 5.3 %collective-permute-done.12.rim = f32[256,512]{1,0:T(8,128)S(1)} collective-permute-done((f32[256,512]{1,0:T(8,128)S(1)}, f32[256,512]{1,0:T(8,128)S(1)}, u32[]{:S(2)}, u32[]{:S(2)}) %collective-permute-start.12) | collective-permute-done | bytes 524320 | tf_op jit(solution)/shard_map/ppermute | solution.py:461
  53.0 2.5 %crop.7 = (f32[256,256]{1,0:T(8,128)S(1)}, f32[256,256]{1,0:T(8,128)S(1)}, f32[2,256,256]{2,1,0:T(8,128)S(1)}) custom-call(s32[2]{0:T(128)S(1)} %pad_add_fusion.ids, s32[4,2]{1,0:T(4,128)S(1)} %copy.37.positions, f32[256,512]{1,0:T(8,128)S(1)} %gate.18.strip, f32[256,512]{1,0:T(8,128)S(1)} %collective-permute-done.12.rim, ...), custom_call_target="tpu_custom_call" | custom-call | flops 2000000 | bytes 2000 | tf_op jit(solution)/shard_map/crop/pallas_call | solution.py:506
  60.5 8.7 %collective-permute-done.14.refs_0_ = f32[2,256,256]{2,1,0:T(8,128)S(1)} collective-permute-done((f32[2,256,256]{2,1,0:T(8,128)S(1)}, f32[2,256,256]{2,1,0:T(8,128)S(1)}, u32[]{:S(2)}, u32[]{:S(2)}) %collective-permute-start.14) | collective-permute-done | bytes 524320 | tf_op jit(solution)/shard_map/ppermute | solution.py:443
  70.9 16.8 %optics.1 = (f32[256,256]{1,0:T(8,128)S(1)}, f32[256,256]{1,0:T(8,128)S(1)}, f32[2,256,256]{2,1,0:T(8,128)S(1)}, f32[256,256]{1,0:T(8,128)S(1)}, f32[256,256]{1,...) custom-call(s32[2]{0:T(128)S(1)} %pad_add_fusion.ids, ...), custom_call_target="tpu_custom_call" | custom-call | flops 15000000 | bytes 15000 | tf_op jit(solution)/shard_map/optics/pallas_call | solution.py:524
  90.9 4.1 %collective-permute-done.18 = f32[1,2,64,256]{3,2,1,0:T(8,128)S(1)} collective-permute-done((f32[1,2,64,256]{3,2,1,0:T(8,128)S(1)}, f32[1,2,64,256]{3,2,1,0:T(8,128)S(1)}, u32[]{:S(2)}, u32[]{:S(2)}) %collective-permute-start.18) | collective-permute-done | bytes 131104 | tf_op jit(solution)/shard_map/ppermute | solution.py:443
  96.5 2.6 %collective-permute-start.21 = (f32[2,64,256]{2,1,0:T(8,128)S(1)}, f32[2,64,256]{2,1,0:T(8,128)S(1)}, u32[]{:S(2)}, u32[]{:S(2)}) collective-permute-start(f32[2,64,256]{2,1,0:T(8,128)S(1)} %fusion.refs_3_), channel_id=1, source_target_pairs={{0,4},{1,5},{2,6},{3,7},{4,0},{5,1},{6,2},{7,3},{8,12},{9,13},{10,... | collective-permute-start | bytes 393224 | tf_op jit(solution)/shard_map/ppermute | solution.py:443
  99.1 5.5 %collective-permute-done.21 = f32[2,64,256]{2,1,0:T(8,128)S(1)} collective-permute-done((f32[2,64,256]{2,1,0:T(8,128)S(1)}, f32[2,64,256]{2,1,0:T(8,128)S(1)}, u32[]{:S(2)}, u32[]{:S(2)}) %collective-permute-start.21) | collective-permute-done | bytes 131104 | tf_op jit(solution)/shard_map/ppermute | solution.py:443
  105.4 4.3 %collective-permute-done.22 = f32[2,64,256]{2,1,0:T(8,128)S(1)} collective-permute-done((f32[2,64,256]{2,1,0:T(8,128)S(1)}, f32[2,64,256]{2,1,0:T(8,128)S(1)}, u32[]{:S(2)}, u32[]{:S(2)}) %collective-permute-start.22) | collective-permute-done | bytes 131104 | tf_op jit(solution)/shard_map/ppermute | solution.py:443
  111.6 2.0 %place.4 = (f32[256,512]{1,0:T(8,128)S(1)}, f32[256,512]{1,0:T(8,128)S(1)}) custom-call(s32[2]{0:T(128)S(1)} %pad_add_fusion.ids, s32[4,2]{1,0:T(4,128)S(1)} %copy.37.positions, f32[256,256]{1,0:T(8,128)S(1)} %get-tuple-element.76.rest_0_, f32[256,256]{1,0:T(8,128)S(1)} %collective-permute-done.19.rest_1_, f32[2,256,256]{2,1,0:T(8,128)S(1)} %gate.21.rest_2_, ...), custom_call_target="tpu_custom_call" | custom-call | flops 2000000 | bytes 2000 | tf_op jit(solution)/shard_map/place/pallas_call | solution.py:573
  113.6 3.5 %collective-permute-start.33 = (f32[256,512]{1,0:T(8,128)S(1)}, f32[256,512]{1,0:T(8,128)S(1)}, u32[]{:S(2)}, u32[]{:S(2)}) collective-permute-start(f32[256,512]{1,0:T(8,128)S(1)} %get-tuple-element.92), channel_id=1, source_target_pairs={{0,1},{1,2},{2,3},{3,4},{4,5},{5,6},{6,7},{8,9},{9,10},{10,11},{11... | collective-permute-start | bytes 1572872 | tf_op jit(solution)/shard_map/ppermute | solution.py:461
  117.1 2.3 %collective-permute-done.16.refs_0_ = f32[2,256,256]{2,1,0:T(8,128)S(1)} collective-permute-done((f32[2,256,256]{2,1,0:T(8,128)S(1)}, f32[2,256,256]{2,1,0:T(8,128)S(1)}, u32[]{:S(2)}, u32[]{:S(2)}) %collective-permute-start.16) | collective-permute-done | bytes 524320 | tf_op jit(solution)/shard_map/ppermute | solution.py:443
  124.0 2.0 %place.5 = (f32[256,512]{1,0:T(8,128)S(1)}, f32[256,512]{1,0:T(8,128)S(1)}) custom-call(s32[2]{0:T(128)S(1)} %pad_add_fusion.ids, s32[4,2]{1,0:T(4,128)S(1)} %copy.37.positions, f32[256,256]{1,0:T(8,128)S(1)} %get-tuple-element.80.rest_0_, f32[256,256]{1,0:T(8,128)S(1)} %collective-permute-done.24.rest_1_, f32[2,256,256]{2,1,0:T(8,128)S(1)} %gate.22.rest_2_.refs_3_, ...), custom_call_target="tpu_custom_call" | custom-call | flops 2000000 | bytes 2000 | tf_op jit(solution)/shard_map/place/pallas_call | solution.py:573
  126.1 2.5 %collective-permute-start.36 = (f32[256,512]{1,0:T(8,128)S(1)}, f32[256,512]{1,0:T(8,128)S(1)}, u32[]{:S(2)}, u32[]{:S(2)}) collective-permute-start(f32[256,512]{1,0:T(8,128)S(1)} %get-tuple-element.96), channel_id=1, source_target_pairs={{0,1},{1,2},{2,3},{3,4},{4,5},{5,6},{6,7},{8,9},{9,10},{10,11},{11... | collective-permute-start | bytes 1572872 | tf_op jit(solution)/shard_map/ppermute | solution.py:461
  129.5 2.6 %collective-permute-done.32.refs_0_ = f32[2,256,256]{2,1,0:T(8,128)S(1)} collective-permute-done((f32[2,256,256]{2,1,0:T(8,128)S(1)}, f32[2,256,256]{2,1,0:T(8,128)S(1)}, u32[]{:S(2)}, u32[]{:S(2)}) %collective-permute-start.32) | collective-permute-done | bytes 524320 | tf_op jit(solution)/shard_map/ppermute | solution.py:443
  133.8 2.0 %place.6 = (f32[256,512]{1,0:T(8,128)S(1)}, f32[256,512]{1,0:T(8,128)S(1)}) custom-call(s32[2]{0:T(128)S(1)} %pad_add_fusion.ids, s32[4,2]{1,0:T(4,128)S(1)} %copy.37.positions, f32[256,256]{1,0:T(8,128)S(1)} %get-tuple-element.89.rest_0_, f32[256,256]{1,0:T(8,128)S(1)} %collective-permute-done.31.rest_1_, f32[2,256,256]{2,1,0:T(8,128)S(1)} %gate.25.rest_2_, ...), custom_call_target="tpu_custom_call" | custom-call | flops 2000000 | bytes 2000 | tf_op jit(solution)/shard_map/place/pallas_call | solution.py:573
  135.9 2.3 %collective-permute-start.42 = (f32[256,512]{1,0:T(8,128)S(1)}, f32[256,512]{1,0:T(8,128)S(1)}, u32[]{:S(2)}, u32[]{:S(2)}) collective-permute-start(f32[256,512]{1,0:T(8,128)S(1)} %gate.30), channel_id=1, source_target_pairs={{0,1},{1,2},{2,3},{3,4},{4,5},{5,6},{6,7},{8,9},{9,10},{10,11},{11... | collective-permute-start | bytes 1572872 | tf_op jit(solution)/shard_map/ppermute | solution.py:461
  138.3 4.4 %collective-permute-done.36.refs_0_ = f32[256,512]{1,0:T(8,128)S(1)} collective-permute-done((f32[256,512]{1,0:T(8,128)S(1)}, f32[256,512]{1,0:T(8,128)S(1)}, u32[]{:S(2)}, u32[]{:S(2)}) %collective-permute-start.36) | collective-permute-done | bytes 524320 | tf_op jit(solution)/shard_map/ppermute | solution.py:461
  144.5 2.0 %place.7 = (f32[256,512]{1,0:T(8,128)S(1)}, f32[256,512]{1,0:T(8,128)S(1)}) custom-call(s32[2]{0:T(128)S(1)} %pad_add_fusion.ids, s32[4,2]{1,0:T(4,128)S(1)} %copy.37.positions, f32[256,256]{1,0:T(8,128)S(1)} %get-tuple-element.83.rest_0_, f32[256,256]{1,0:T(8,128)S(1)} %collective-permute-done.29.rest_1_, f32[2,256,256]{2,1,0:T(8,128)S(1)} %gate.26.rest_2_, ...), custom_call_target="tpu_custom_call" | custom-call | flops 2000000 | bytes 2000 | tf_op jit(solution)/shard_map/place/pallas_call | solution.py:573
  146.6 3.9 %collective-permute-start.39 = (f32[256,512]{1,0:T(8,128)S(1)}, f32[256,512]{1,0:T(8,128)S(1)}, u32[]{:S(2)}, u32[]{:S(2)}) collective-permute-start(f32[256,512]{1,0:T(8,128)S(1)} %gate.28), channel_id=1, source_target_pairs={{0,1},{1,2},{2,3},{3,4},{4,5},{5,6},{6,7},{8,9},{9,10},{10,11},{11... | collective-permute-start | bytes 1572872 | tf_op jit(solution)/shard_map/ppermute | solution.py:461
  150.5 3.4 %collective-permute-done.42.refs_0_ = f32[256,512]{1,0:T(8,128)S(1)} collective-permute-done((f32[256,512]{1,0:T(8,128)S(1)}, f32[256,512]{1,0:T(8,128)S(1)}, u32[]{:S(2)}, u32[]{:S(2)}) %collective-permute-start.42) | collective-permute-done | bytes 524320 | tf_op jit(solution)/shard_map/ppermute | solution.py:461
  155.7 8.8 %collective-permute-done.39 = f32[256,512]{1,0:T(8,128)S(1)} collective-permute-done((f32[256,512]{1,0:T(8,128)S(1)}, f32[256,512]{1,0:T(8,128)S(1)}, u32[]{:S(2)}, u32[]{:S(2)}) %collective-permute-start.39) | collective-permute-done | bytes 524320 | tf_op jit(solution)/shard_map/ppermute | solution.py:461
  (128 shorter events, 35.1 us)
Async XLA Ops:
  2.6 17.8 %collective-permute-start = (f32[256,512]{1,0:T(8,128)}, f32[256,512]{1,0:T(8,128)S(1)}, u32[]{:S(2)}, u32[]{:S(2)}) collective-permute-start(f32[256,512]{1,0:T(8,128)} %strip.2.rest_0_), channel_id=1, source_target_pairs={{1,0},{2,1},{3,2},{4,3},{5,4},{6,5},{7,6},{9,8},{10,9},{11,10},{12... | collective-permute-start | bytes 1572872 | tf_op jit(solution)/shard_map/ppermute | solution.py:461
  8.3 23.3 %collective-permute-start.4 = (f32[256,512]{1,0:T(8,128)}, f32[256,512]{1,0:T(8,128)S(1)}, u32[]{:S(2)}, u32[]{:S(2)}) collective-permute-start(f32[256,512]{1,0:T(8,128)} %gate.16.strip), channel_id=1, source_target_pairs={{1,0},{2,1},{3,2},{4,3},{5,4},{6,5},{7,6},{9,8},{10,9},{11,10},{12... | collective-permute-start | bytes 1572872 | tf_op jit(solution)/shard_map/ppermute | solution.py:461
  22.9 15.8 %collective-permute-start.2 = (f32[2,256,256]{2,1,0:T(8,128)S(1)}, f32[2,256,256]{2,1,0:T(8,128)S(1)}, u32[]{:S(2)}, u32[]{:S(2)}) collective-permute-start(f32[2,256,256]{2,1,0:T(8,128)S(1)} %get-tuple-element.54), channel_id=1, source_target_pairs={{0,16},{8,24},{16,0},{24,8},{1,17},{9,25},{17,1},{25,9},{2,18},{10... | collective-permute-start | bytes 1572872 | tf_op jit(solution)/shard_map/ppermute | solution.py:443
  24.4 18.4 %collective-permute-start.8 = (f32[256,512]{1,0:T(8,128)S(1)}, f32[256,512]{1,0:T(8,128)S(1)}, u32[]{:S(2)}, u32[]{:S(2)}) collective-permute-start(f32[256,512]{1,0:T(8,128)S(1)} %gate.17.strip), channel_id=1, source_target_pairs={{1,0},{2,1},{3,2},{4,3},{5,4},{6,5},{7,6},{9,8},{10,9},{11,10},{12... | collective-permute-start | bytes 1572872 | tf_op jit(solution)/shard_map/ppermute | solution.py:461
  35.1 12.6 %collective-permute-start.6 = (f32[2,256,256]{2,1,0:T(8,128)S(1)}, f32[2,256,256]{2,1,0:T(8,128)S(1)}, u32[]{:S(2)}, u32[]{:S(2)}) collective-permute-start(f32[2,256,256]{2,1,0:T(8,128)S(1)} %get-tuple-element.58), channel_id=1, source_target_pairs={{0,16},{8,24},{16,0},{24,8},{1,17},{9,25},{17,1},{25,9},{2,18},{10... | collective-permute-start | bytes 1572872 | tf_op jit(solution)/shard_map/ppermute | solution.py:443
  36.6 16.3 %collective-permute-start.12 = (f32[256,512]{1,0:T(8,128)S(1)}, f32[256,512]{1,0:T(8,128)S(1)}, u32[]{:S(2)}, u32[]{:S(2)}) collective-permute-start(f32[256,512]{1,0:T(8,128)S(1)} %gate.18.strip), channel_id=1, source_target_pairs={{1,0},{2,1},{3,2},{4,3},{5,4},{6,5},{7,6},{9,8},{10,9},{11,10},{12... | collective-permute-start | bytes 1572872 | tf_op jit(solution)/shard_map/ppermute | solution.py:461
  45.4 13.7 %collective-permute-start.10 = (f32[2,256,256]{2,1,0:T(8,128)S(1)}, f32[2,256,256]{2,1,0:T(8,128)S(1)}, u32[]{:S(2)}, u32[]{:S(2)}) collective-permute-start(f32[2,256,256]{2,1,0:T(8,128)S(1)} %get-tuple-element.62), channel_id=1, source_target_pairs={{0,16},{8,24},{16,0},{24,8},{1,17},{9,25},{17,1},{25,9},{2,18},{10... | collective-permute-start | bytes 1572872 | tf_op jit(solution)/shard_map/ppermute | solution.py:443
  46.9 12.1 %collective-permute-start.1 = (f32[256,256]{1,0:T(8,128)S(1)}, f32[256,256]{1,0:T(8,128)S(1)}, u32[]{:S(2)}, u32[]{:S(2)}) collective-permute-start(f32[256,256]{1,0:T(8,128)S(1)} %get-tuple-element.53), channel_id=1, source_target_pairs={{0,8},{8,0},{16,24},{24,16},{1,9},{9,1},{17,25},{25,17},{2,10},{10... | collective-permute-start | bytes 786440 | tf_op jit(solution)/shard_map/ppermute | solution.py:443
  46.9 12.7 %collective-permute-start.5 = (f32[256,256]{1,0:T(8,128)S(1)}, f32[256,256]{1,0:T(8,128)S(1)}, u32[]{:S(2)}, u32[]{:S(2)}) collective-permute-start(f32[256,256]{1,0:T(8,128)S(1)} %get-tuple-element.57), channel_id=1, source_target_pairs={{0,8},{8,0},{16,24},{24,16},{1,9},{9,1},{17,25},{25,17},{2,10},{10... | collective-permute-start | bytes 786440 | tf_op jit(solution)/shard_map/ppermute | solution.py:443
  55.5 13.8 %collective-permute-start.14 = (f32[2,256,256]{2,1,0:T(8,128)S(1)}, f32[2,256,256]{2,1,0:T(8,128)S(1)}, u32[]{:S(2)}, u32[]{:S(2)}) collective-permute-start(f32[2,256,256]{2,1,0:T(8,128)S(1)} %get-tuple-element.66), channel_id=1, source_target_pairs={{0,16},{8,24},{16,0},{24,8},{1,17},{9,25},{17,1},{25,9},{2,18},{10... | collective-permute-start | bytes 1572872 | tf_op jit(solution)/shard_map/ppermute | solution.py:443
  57.0 2.7 %collective-permute-start.3 = (f32[256,256]{1,0:T(8,128)S(1)}, f32[256,256]{1,0:T(8,128)S(1)}, u32[]{:S(2)}, u32[]{:S(2)}) collective-permute-start(f32[256,256]{1,0:T(8,128)S(1)} %slice_bitcast_fusion.7), channel_id=1, source_target_pairs={{0,8},{8,0},{16,24},{24,16},{1,9},{9,1},{17,25},{25,17},{2,10},{10... | collective-permute-start | bytes 786440 | tf_op jit(solution)/shard_map/ppermute | solution.py:443
  59.0 10.3 %collective-permute-start.9 = (f32[256,256]{1,0:T(8,128)S(1)}, f32[256,256]{1,0:T(8,128)S(1)}, u32[]{:S(2)}, u32[]{:S(2)}) collective-permute-start(f32[256,256]{1,0:T(8,128)S(1)} %get-tuple-element.61), channel_id=1, source_target_pairs={{0,8},{8,0},{16,24},{24,16},{1,9},{9,1},{17,25},{25,17},{2,10},{10... | collective-permute-start | bytes 786440 | tf_op jit(solution)/shard_map/ppermute | solution.py:443
  59.6 9.7 %collective-permute-start.13 = (f32[256,256]{1,0:T(8,128)S(1)}, f32[256,256]{1,0:T(8,128)S(1)}, u32[]{:S(2)}, u32[]{:S(2)}) collective-permute-start(f32[256,256]{1,0:T(8,128)S(1)} %get-tuple-element.65), channel_id=1, source_target_pairs={{0,8},{8,0},{16,24},{24,16},{1,9},{9,1},{17,25},{25,17},{2,10},{10... | collective-permute-start | bytes 786440 | tf_op jit(solution)/shard_map/ppermute | solution.py:443
  59.7 9.7 %collective-permute-start.11 = (f32[256,256]{1,0:T(8,128)S(1)}, f32[256,256]{1,0:T(8,128)S(1)}, u32[]{:S(2)}, u32[]{:S(2)}) collective-permute-start(f32[256,256]{1,0:T(8,128)S(1)} %slice_bitcast_fusion.5), channel_id=1, source_target_pairs={{0,8},{8,0},{16,24},{24,16},{1,9},{9,1},{17,25},{25,17},{2,10},{10... | collective-permute-start | bytes 786440 | tf_op jit(solution)/shard_map/ppermute | solution.py:443
  89.4 5.6 %collective-permute-start.18 = (f32[1,2,64,256]{3,2,1,0:T(8,128)S(1)}, f32[1,2,64,256]{3,2,1,0:T(8,128)S(1)}, u32[]{:S(2)}, u32[]{:S(2)}) collective-permute-start(f32[1,2,64,256]{3,2,1,0:T(8,128)S(1)} %slice.57), channel_id=1, source_target_pairs={{0,16},{8,24},{16,0},{24,8},{1,17},{9,25},{17,1},{25,9},{2,18},{10... | collective-permute-start | bytes 393224 | tf_op jit(solution)/shard_map/ppermute | solution.py:443
  95.0 14.9 %collective-permute-start.20 = (f32[2,256,256]{2,1,0:T(8,128)S(1)}, f32[2,256,256]{2,1,0:T(8,128)S(1)}, u32[]{:S(2)}, u32[]{:S(2)}) collective-permute-start(f32[2,256,256]{2,1,0:T(8,128)S(1)} %get-tuple-element.78), channel_id=1, source_target_pairs={{0,16},{8,24},{16,0},{24,8},{1,17},{9,25},{17,1},{25,9},{2,18},{10... | collective-permute-start | bytes 1572872 | tf_op jit(solution)/shard_map/ppermute | solution.py:443
  96.5 8.1 %collective-permute-start.21 = (f32[2,64,256]{2,1,0:T(8,128)S(1)}, f32[2,64,256]{2,1,0:T(8,128)S(1)}, u32[]{:S(2)}, u32[]{:S(2)}) collective-permute-start(f32[2,64,256]{2,1,0:T(8,128)S(1)} %fusion.refs_3_), channel_id=1, source_target_pairs={{0,4},{1,5},{2,6},{3,7},{4,0},{5,1},{6,2},{7,3},{8,12},{9,13},{10,... | collective-permute-start | bytes 393224 | tf_op jit(solution)/shard_map/ppermute | solution.py:443
  104.7 5.0 %collective-permute-start.22 = (f32[2,64,256]{2,1,0:T(8,128)S(1)}, f32[2,64,256]{2,1,0:T(8,128)S(1)}, u32[]{:S(2)}, u32[]{:S(2)}) collective-permute-start(f32[2,64,256]{2,1,0:T(8,128)S(1)} %add.29), channel_id=1, source_target_pairs={{0,2},{1,3},{2,0},{3,1},{4,6},{5,7},{6,4},{7,5},{8,10},{9,11},{10,... | collective-permute-start | bytes 393224 | tf_op jit(solution)/shard_map/ppermute | solution.py:443
  104.8 14.7 %collective-permute-start.16 = (f32[2,256,256]{2,1,0:T(8,128)S(1)}, f32[2,256,256]{2,1,0:T(8,128)S(1)}, u32[]{:S(2)}, u32[]{:S(2)}) collective-permute-start(f32[2,256,256]{2,1,0:T(8,128)S(1)} %get-tuple-element.70), channel_id=1, source_target_pairs={{0,16},{8,24},{16,0},{24,8},{1,17},{9,25},{17,1},{25,9},{2,18},{10... | collective-permute-start | bytes 1572872 | tf_op jit(solution)/shard_map/ppermute | solution.py:443
  105.4 4.7 %collective-permute-start.19 = (f32[256,256]{1,0:T(8,128)S(1)}, f32[256,256]{1,0:T(8,128)S(1)}, u32[]{:S(2)}, u32[]{:S(2)}) collective-permute-start(f32[256,256]{1,0:T(8,128)S(1)} %get-tuple-element.77), channel_id=1, source_target_pairs={{0,8},{8,0},{16,24},{24,16},{1,9},{9,1},{17,25},{25,17},{2,10},{10... | collective-permute-start | bytes 786440 | tf_op jit(solution)/shard_map/ppermute | solution.py:443
  110.0 10.9 %collective-permute-start.26 = (f32[2,64,256]{2,1,0:T(8,128)S(1)}, f32[2,64,256]{2,1,0:T(8,128)S(1)}, u32[]{:S(2)}, u32[]{:S(2)}) collective-permute-start(f32[2,64,256]{2,1,0:T(8,128)S(1)} %add.30.refs_1_), channel_id=1, source_target_pairs={{0,1},{1,0},{2,3},{3,2},{4,5},{5,4},{6,7},{7,6},{8,9},{9,8},{10,11... | collective-permute-start | bytes 393224 | tf_op jit(solution)/shard_map/ppermute | solution.py:443
  113.6 15.9 %collective-permute-start.33 = (f32[256,512]{1,0:T(8,128)S(1)}, f32[256,512]{1,0:T(8,128)S(1)}, u32[]{:S(2)}, u32[]{:S(2)}) collective-permute-start(f32[256,512]{1,0:T(8,128)S(1)} %get-tuple-element.92), channel_id=1, source_target_pairs={{0,1},{1,2},{2,3},{3,4},{4,5},{5,6},{6,7},{8,9},{9,10},{10,11},{11... | collective-permute-start | bytes 1572872 | tf_op jit(solution)/shard_map/ppermute | solution.py:461
  119.4 12.6 %collective-permute-start.32 = (f32[2,256,256]{2,1,0:T(8,128)S(1)}, f32[2,256,256]{2,1,0:T(8,128)S(1)}, u32[]{:S(2)}, u32[]{:S(2)}) collective-permute-start(f32[2,256,256]{2,1,0:T(8,128)S(1)} %get-tuple-element.91), channel_id=1, source_target_pairs={{0,16},{8,24},{16,0},{24,8},{1,17},{9,25},{17,1},{25,9},{2,18},{10... | collective-permute-start | bytes 1572872 | tf_op jit(solution)/shard_map/ppermute | solution.py:443
  121.6 2.4 %collective-permute-start.25 = (f32[256,256]{1,0:T(8,128)S(1)}, f32[256,256]{1,0:T(8,128)S(1)}, u32[]{:S(2)}, u32[]{:S(2)}) collective-permute-start(f32[256,256]{1,0:T(8,128)S(1)} %slice_bitcast_fusion.2), channel_id=1, source_target_pairs={{0,8},{8,0},{16,24},{24,16},{1,9},{9,1},{17,25},{25,17},{2,10},{10... | collective-permute-start | bytes 786440 | tf_op jit(solution)/shard_map/ppermute | solution.py:443
  126.1 16.7 %collective-permute-start.36 = (f32[256,512]{1,0:T(8,128)S(1)}, f32[256,512]{1,0:T(8,128)S(1)}, u32[]{:S(2)}, u32[]{:S(2)}) collective-permute-start(f32[256,512]{1,0:T(8,128)S(1)} %get-tuple-element.96), channel_id=1, source_target_pairs={{0,1},{1,2},{2,3},{3,4},{4,5},{5,6},{6,7},{8,9},{9,10},{10,11},{11... | collective-permute-start | bytes 1572872 | tf_op jit(solution)/shard_map/ppermute | solution.py:461
  128.6 14.3 %collective-permute-start.30 = (f32[2,256,256]{2,1,0:T(8,128)S(1)}, f32[2,256,256]{2,1,0:T(8,128)S(1)}, u32[]{:S(2)}, u32[]{:S(2)}) collective-permute-start(f32[2,256,256]{2,1,0:T(8,128)S(1)} %get-tuple-element.85), channel_id=1, source_target_pairs={{0,16},{8,24},{16,0},{24,8},{1,17},{9,25},{17,1},{25,9},{2,18},{10... | collective-permute-start | bytes 1572872 | tf_op jit(solution)/shard_map/ppermute | solution.py:443
  129.2 4.6 %collective-permute-start.31 = (f32[256,256]{1,0:T(8,128)S(1)}, f32[256,256]{1,0:T(8,128)S(1)}, u32[]{:S(2)}, u32[]{:S(2)}) collective-permute-start(f32[256,256]{1,0:T(8,128)S(1)} %get-tuple-element.90), channel_id=1, source_target_pairs={{0,8},{8,0},{16,24},{24,16},{1,9},{9,1},{17,25},{25,17},{2,10},{10... | collective-permute-start | bytes 786440 | tf_op jit(solution)/shard_map/ppermute | solution.py:443
  133.7 2.2 %collective-permute-start.41 = (f32[8,128]{1,0:T(8,128)S(1)}, f32[8,128]{1,0:T(8,128)S(1)}, u32[]{:S(2)}, u32[]{:S(2)}) collective-permute-start(f32[8,128]{1,0:T(8,128)S(1)} %collective-permute-done.40), channel_id=1, source_target_pairs={{0,8},{8,0},{16,24},{24,16},{1,9},{9,1},{17,25},{25,17},{2,10},{10... | collective-permute-start | bytes 12296 | tf_op jit(solution)/shard_map/ppermute | solution.py:443
  135.9 18.1 %collective-permute-start.42 = (f32[256,512]{1,0:T(8,128)S(1)}, f32[256,512]{1,0:T(8,128)S(1)}, u32[]{:S(2)}, u32[]{:S(2)}) collective-permute-start(f32[256,512]{1,0:T(8,128)S(1)} %gate.30), channel_id=1, source_target_pairs={{0,1},{1,2},{2,3},{3,4},{4,5},{5,6},{6,7},{8,9},{9,10},{10,11},{11... | collective-permute-start | bytes 1572872 | tf_op jit(solution)/shard_map/ppermute | solution.py:461
  138.1 6.0 %collective-permute-start.29 = (f32[256,256]{1,0:T(8,128)S(1)}, f32[256,256]{1,0:T(8,128)S(1)}, u32[]{:S(2)}, u32[]{:S(2)}) collective-permute-start(f32[256,256]{1,0:T(8,128)S(1)} %get-tuple-element.84), channel_id=1, source_target_pairs={{0,8},{8,0},{16,24},{24,16},{1,9},{9,1},{17,25},{25,17},{2,10},{10... | collective-permute-start | bytes 786440 | tf_op jit(solution)/shard_map/ppermute | solution.py:443
  143.9 2.7 %collective-permute-start.38 = (f32[8,128]{1,0:T(8,128)S(1)}, f32[8,128]{1,0:T(8,128)S(1)}, u32[]{:S(2)}, u32[]{:S(2)}) collective-permute-start(f32[8,128]{1,0:T(8,128)S(1)} %collective-permute-done.37), channel_id=1, source_target_pairs={{0,8},{8,0},{16,24},{24,16},{1,9},{9,1},{17,25},{25,17},{2,10},{10... | collective-permute-start | bytes 12296 | tf_op jit(solution)/shard_map/ppermute | solution.py:443
  146.6 17.9 %collective-permute-start.39 = (f32[256,512]{1,0:T(8,128)S(1)}, f32[256,512]{1,0:T(8,128)S(1)}, u32[]{:S(2)}, u32[]{:S(2)}) collective-permute-start(f32[256,512]{1,0:T(8,128)S(1)} %gate.28), channel_id=1, source_target_pairs={{0,1},{1,2},{2,3},{3,4},{4,5},{5,6},{6,7},{8,9},{9,10},{10,11},{11... | collective-permute-start | bytes 1572872 | tf_op jit(solution)/shard_map/ppermute | solution.py:461
  (21 other events, 120.0 us)
